TPU v7x, 256 devices: a whole 4x4x8 slice. The times are simulated.
256 devices in a mesh: dp: 32 (over x, z), tensor: 8 (over y, core).
Axes of the slice: x: 4, y: 4, z: 8, core: 2. Of those that a mesh axis runs over, the one named last changes fastest.
Arguments:
- token_rows: bfloat16 [16384, 8192], P(('dp', 'tensor')), may hold values from -24 to 24
- advantage: int32 [16384], P(('dp', 'tensor')), may hold values from 1 to 81920
- cotangent: bfloat16 [16384, 2048], P('dp', 'tensor'), may hold values from -1 to 1
- master: float32 [8192, 2048], P('dp', 'tensor'), may hold values from -3 to 3
- moment_one: float32 [8192, 2048], P('dp', 'tensor'), may hold values from -3 to 3
- moment_two: float32 [8192, 2048], P('dp', 'tensor'), may hold values from 0.1 to 3
Outputs:
- weights: bfloat16 [8192, 2048], P(None, 'tensor')
- new_master: float32 [8192, 2048], P('dp', 'tensor')
- new_moment_one: float32 [8192, 2048], P('dp', 'tensor')
- new_moment_two: float32 [8192, 2048], P('dp', 'tensor')
Inputs may be any that keep to these rules, and one draw needn't show every extreme that they name: advantage weight in units of 2**-12.
All inputs are finite; a program needn't handle non-finite values.
Results may differ from a plain program's by a relative error of at most 0.00042.
Values may be sent and summed in bfloat16 or wider, within the bound.
No kernel may reach another device: no remote copies, remote signals or barrier semaphores. Data moves between devices by JAX's collectives and lax.ppermute only.
A program may use at most 64 MiB of HBM per device.

v0:
```python
import functools
import jax
import jax.numpy as jnp
from jax import lax
from jax.experimental import pallas as pl
from jax.experimental.pallas import tpu as pltpu
from jax.sharding import Mesh, PartitionSpec as P

STEP = 10
SCALE_FIXED = 2.0 ** (-12)
EPS_ADA = 1e-06

NX, NZ, NY, NC = 4, 8, 4, 2
REP = NX * NZ
TOK = 512
BLK = 256
ROWS_A = 288
F32 = jnp.float32
BF16 = jnp.bfloat16
HIGH = lax.Precision.HIGHEST


def shift(array, axis, size, by):
    return lax.ppermute(array, axis, [(i, (i + by) % size) for i in range(size)])


def side(at, core):
    return 1 - 2 * ((at + core) % 2)


def near(array, axis, size, which):
    pairs = [(a * NC + c, (a + which * side(a, c)) % size * NC + c) for a in range(size) for c in range(NC)]
    return lax.ppermute(array, (axis, "c"), pairs)


def swapped_ring(block, axis, size):
    pair = jnp.stack([block, near(block, axis, size, 1)])
    found, held, which = [pair], pair, -1
    for _ in range(size // 2 - 1):
        held = near(held, axis, size, which)
        found.append(held)
        which = -which
    return found


def gather_plane(block, cut):
    line = jnp.concatenate(swapped_ring(block[:cut], "z", NZ))
    other = jnp.concatenate(swapped_ring(block[cut:], "x", NX))
    ahead = near(line, "x", NX, 1)
    behind = near(line, "x", NX, -1)
    far = near(ahead, "x", NX, -1)
    out = [(piece, 0, [((), kx, 1, 0, NZ)]) for kx, piece in enumerate((line, ahead, behind, far))]
    for no, piece in enumerate(swapped_ring(other, "z", NZ)):
        out.append((piece, cut, [((i,), 0, NX, 2 * no + i, 1) for i in range(2)]))
    return out


STEPS = (0, 1, -1, -2, 2, 3, -3, -4)


def replica_of(place, kx, kz):
    x = lax.rem(place[0] + place[2] * STEPS[kx] + NX, NX)
    z = lax.rem(place[1] + place[3] * STEPS[kz] + NZ, NZ)
    return x * NZ + z


def mirrored(k, size):
    return jnp.where((k == 0) | (k == size - 1), k, k + 1 - 2 * ((k + 1) % 2))


def replicas_of(place, slots):
    def step(k):
        return sum(jnp.where(k == i, STEPS[i], 0) for i in range(NZ))

    x = lax.rem(place[0] + place[2] * step(slots // NZ) + NX, NX)
    z = lax.rem(place[1] + place[3] * step(slots % NZ) + NZ, NZ)
    return x * NZ + z


def grads_kernel(layout, place, *refs):
    tokens = NY * NC
    x_pieces, refs = refs[:tokens], refs[tokens:]
    count = len(layout)
    pieces, (mean_ref, g_hbm, sums_ref) = refs[:count], refs[count:count + 3]
    xv, wv, gv, xsem, wsem, gsem = refs[count + 3:]
    y, core, turn = place[4], place[5], place[6]
    parts, across, along = [], [], [[] for _ in range(NX)]
    for no in range(tokens):
        c = core if no < NY else 1 - core
        row = lax.rem(y + (turn if no < NY else -turn) * STEPS[no % NY] + NY, NY)
        parts.append(pltpu.make_async_copy(x_pieces[no], xv.at[row, c], xsem.at[no]))
    for no, (offset, rows, chunks) in enumerate(layout):
        for chunk, (index, kx, nx, kz, nz) in enumerate(chunks):
            source = pieces[no].at[index] if index else pieces[no]
            copy = pltpu.make_async_copy(
                source.reshape(nx, nz, rows, BLK),
                wv.at[pl.ds(kx, nx), pl.ds(kz, nz), pl.ds(offset, rows)], wsem.at[no, chunk])
            (across if offset else along[kx]).append(copy)
    for copy in parts + across + sum(along, []):
        copy.start()
    for copy in parts + across:
        copy.wait()

    def multiply(slot, _):
        kx, kz = slot // NZ, lax.rem(slot, NZ)
        other = mirrored(kx, NX) * NZ + mirrored(kz, NZ)
        rows = jnp.stack([xv[:, 0, jnp.where(core == 0, slot, other)],
                          xv[:, 1, jnp.where(core == 0, other, slot)]], axis=1).reshape(TOK, BLK)
        gv[slot] = lax.dot_general(rows, wv[kx, kz], (((0,), (0,)), ((), ())), preferred_element_type=F32)
        return 0

    outs = []
    for part in range(NX):
        for copy in along[part]:
            copy.wait()
        lax.fori_loop(part * NZ, (part + 1) * NZ, multiply, 0, unroll=2)
        at = pl.ds(part * NZ, NZ)
        outs.append(pltpu.make_async_copy(gv.at[at], g_hbm.at[at], gsem.at[part]))
        outs[-1].start()

    def add(j, total):
        y = jnp.concatenate(
            [gv[:, pl.ds(pl.multiple_of(j * 32 + 8 * h, 8), 8), :].reshape(BLK, BLK) for h in range(4)], axis=1)
        high = y.astype(BF16)
        low = (y - high.astype(F32)).astype(BF16)
        both = jnp.concatenate([high, low], axis=0)
        return total + lax.dot_general(high, both, (((1,), (1,)), ((), ())), preferred_element_type=F32)

    total = lax.fori_loop(0, BLK // 32, add, jnp.zeros((BLK, 2 * BLK), F32))
    cross = total[:, BLK:]
    total = total[:, :BLK] + cross + cross.T
    i = lax.broadcasted_iota(jnp.int32, (BLK, BLK), 0)
    j = lax.broadcasted_iota(jnp.int32, (BLK, BLK), 1)
    total = jnp.where(i % 8 == j % 8, total, 0.0)

    pick_rows = (lax.broadcasted_iota(jnp.int32, (REP, BLK), 0)
                 == replicas_of(place, lax.broadcasted_iota(jnp.int32, (REP, BLK), 1) // 8)).astype(F32)
    pick_cols = (lax.broadcasted_iota(jnp.int32, (BLK, 128), 1) % REP
                 == replicas_of(place, lax.broadcasted_iota(jnp.int32, (BLK, 128), 0) // 8)).astype(F32)
    gram = jnp.dot(jnp.dot(pick_rows, total, preferred_element_type=F32, precision=HIGH), pick_cols,
                   preferred_element_type=F32, precision=HIGH)
    lane = lax.broadcasted_iota(jnp.int32, (8, 128), 1)
    packed = jnp.zeros((8, 128), F32)
    for q in range(REP // 8):
        packed = packed + jnp.where(lane // REP == q, gram[8 * q:8 * q + 8], 0.0)
    sums_ref[0:8] = packed
    sums_ref[8:16] = jnp.where(lane % REP == replica_of(place, 0, 0), mean_ref[...], 0.0)
    for out in outs:
        out.wait()


def grads_and_sums(place, x_pieces, pieces, mean):
    layout = [(offset, piece.shape[-2], chunks) for piece, offset, chunks in pieces]
    any_spec = pl.BlockSpec(memory_space=pl.ANY)
    return pl.pallas_call(
        functools.partial(grads_kernel, layout),
        out_shape=(jax.ShapeDtypeStruct((REP, BLK, BLK), F32), jax.ShapeDtypeStruct((16, 128), F32)),
        in_specs=[pl.BlockSpec(memory_space=pltpu.SMEM)] + [any_spec] * (len(x_pieces) + len(layout))
        + [pl.BlockSpec(memory_space=pltpu.VMEM)],
        out_specs=(any_spec, pl.BlockSpec(memory_space=pltpu.VMEM)),
        scratch_shapes=[
            pltpu.VMEM((NY, NC, REP, TOK // (NY * NC), BLK), BF16),
            pltpu.VMEM((NX, NZ, TOK, BLK), BF16),
            pltpu.VMEM((REP, BLK, BLK), F32),
            pltpu.SemaphoreType.DMA((NY * NC,)),
            pltpu.SemaphoreType.DMA((len(layout), 2)),
            pltpu.SemaphoreType.DMA((NX,)),
        ],
        compiler_params=pltpu.CompilerParams(vmem_limit_bytes=58 * 2**20),
        cost_estimate=pl.CostEstimate(flops=6 * 10**9, bytes_accessed=24 * 2**20, transcendentals=0),
    )(place, *x_pieces, *[piece for piece, _, _ in pieces], mean)


def tree_weights(sums):
    lane = lax.broadcasted_iota(jnp.int32, (REP, 128), 1) % REP
    row = lax.broadcasted_iota(jnp.int32, (REP, 128), 0)
    inverse_lanes = float(NY * NC) / sums[8:9]
    inverse_rows = jnp.sum(jnp.where((lax.broadcasted_iota(jnp.int32, (REP, 128), 1) == row),
                                     jnp.broadcast_to(inverse_lanes, (REP, 128)), 0.0), axis=1, keepdims=True)
    wide = lax.broadcasted_iota(jnp.int32, (8, 128), 1)
    table = jnp.concatenate(
        [jnp.where(wide < REP, sums[0:8] if q == 0 else pltpu.roll(sums[0:8], 128 - REP * q, 1), 0.0)
         for q in range(REP // 8)], axis=0)
    table = table + pltpu.roll(table, REP, 1)
    table = table + pltpu.roll(table, 2 * REP, 1)
    table = table * inverse_rows * inverse_lanes
    factor = inverse_rows
    first = lax.broadcasted_iota(jnp.int32, (REP, 128), 1) < REP
    size = REP
    while size > 1:
        half = size // 2
        own = lane == row
        other_rows = lane == (row + half) % REP
        other_lanes = row == (lane + half) % REP
        own_r = jnp.sum(jnp.where(own & first, table, 0.0), axis=1, keepdims=True)
        cross_r = jnp.sum(jnp.where(other_rows & first, table, 0.0), axis=1, keepdims=True)
        own_l = jnp.sum(jnp.where(own, table, 0.0), axis=0, keepdims=True)
        cross_l = jnp.sum(jnp.where(other_lanes, table, 0.0), axis=0, keepdims=True)
        coef_r = 1.0 - cross_r / (2.0 * own_r + EPS_ADA)
        coef_l = 1.0 - cross_l / (2.0 * own_l + EPS_ADA)
        factor = factor * coef_r
        table = table * coef_r * coef_l
        table = table + pltpu.roll(table, half, 0)
        table = table + pltpu.roll(table, half, 1)
        size = half
    return jnp.broadcast_to(factor, (REP, 128))


def update_kernel(place, sums_ref, g_hbm, master_ref, one_ref, two_ref, weights_ref, master_out, one_out, two_out,
                  gv, factors, sem):
    copies = [pltpu.make_async_copy(g_hbm.at[r], gv.at[r], sem.at[r]) for r in range(REP)]
    for copy in copies:
        copy.start()
    factors[...] = tree_weights(sums_ref[...])
    for copy in copies:
        copy.wait()

    scales = [factors[pl.ds(replica_of(place, r // NZ, r % NZ), 1), :] for r in range(REP)]

    def strip(s, _):
        at = pl.ds(pl.multiple_of(s * 16, 16), 16)
        combined = jnp.zeros((16, BLK), F32)
        for r in range(REP):
            scale = scales[r]
            combined = combined + jnp.concatenate([scale, scale], axis=1) * gv[r, at, :]
        new_one = 0.9 * one_ref[at, :] + 0.1 * combined
        new_two = 0.95 * two_ref[at, :] + 0.05 * combined * combined
        first_hat = new_one / (1.0 - 0.9**STEP)
        second_hat = new_two / (1.0 - 0.95**STEP)
        master = master_ref[at, :]
        updated = master - 0.001 * (first_hat / (jnp.sqrt(second_hat) + 1e-08) + 0.1 * master)
        weights_ref[at, :] = updated.astype(BF16)
        master_out[at, :] = updated
        one_out[at, :] = new_one
        two_out[at, :] = new_two
        return 0

    lax.fori_loop(0, BLK // 16, strip, 0)


def update(place, sums, grads, master, one, two):
    vmem = pl.BlockSpec(memory_space=pltpu.VMEM)
    state = jax.ShapeDtypeStruct((BLK, BLK), F32)
    return pl.pallas_call(
        update_kernel,
        out_shape=(jax.ShapeDtypeStruct((BLK, BLK), BF16), state, state, state),
        in_specs=[pl.BlockSpec(memory_space=pltpu.SMEM), vmem, pl.BlockSpec(memory_space=pl.ANY), vmem, vmem, vmem],
        out_specs=(vmem,) * 4,
        scratch_shapes=[
            pltpu.VMEM((REP, BLK, BLK), F32),
            pltpu.VMEM((REP, 128), F32),
            pltpu.SemaphoreType.DMA((REP,)),
        ],
        compiler_params=pltpu.CompilerParams(vmem_limit_bytes=58 * 2**20),
        cost_estimate=pl.CostEstimate(flops=5 * 10**6, bytes_accessed=10 * 2**20, transcendentals=0),
    )(place, sums, grads, master, one, two)


def place_kernel(layout, place, *refs):
    count = len(layout)
    pieces, out_hbm, held, sem, out_sem = refs[:count], *refs[count:]
    copies = []
    for no, (offset, rows, chunks) in enumerate(layout):
        for index, kx, nx, kz, nz in chunks:
            source = pieces[no].at[index] if index else pieces[no]
            for i in range(nx * nz):
                r = replica_of(place, kx + i // nz, kz + i % nz)
                copies.append(pltpu.make_async_copy(
                    source.at[i], held.at[r, pl.ds(offset, rows)], sem.at[len(copies)]))
    for copy in copies:
        copy.start()
    for copy in copies:
        copy.wait()
    outs = []
    for part in range(8):
        at = pl.ds(part * REP // 8, REP // 8)
        outs.append(pltpu.make_async_copy(held.at[at], out_hbm.at[at], out_sem.at[part]))
        outs[-1].start()
    for out in outs:
        out.wait()


def place_rows(place, pieces):
    layout = [(offset, piece.shape[-2], chunks) for piece, offset, chunks in pieces]
    any_spec = pl.BlockSpec(memory_space=pl.ANY)
    total = 2 * REP
    return pl.pallas_call(
        functools.partial(place_kernel, layout),
        out_shape=jax.ShapeDtypeStruct((REP, BLK, BLK), BF16),
        in_specs=[pl.BlockSpec(memory_space=pltpu.SMEM)] + [any_spec] * len(layout),
        out_specs=any_spec,
        scratch_shapes=[
            pltpu.VMEM((REP, BLK, BLK), BF16),
            pltpu.SemaphoreType.DMA((total,)),
            pltpu.SemaphoreType.DMA((8,)),
        ],
        compiler_params=pltpu.CompilerParams(vmem_limit_bytes=56 * 2**20),
        cost_estimate=pl.CostEstimate(flops=0, bytes_accessed=8 * 2**20, transcendentals=0),
    )(place, *[piece for piece, _, _ in pieces])


def total_over_slice(sums):
    for axes, size in ((("x", "y"), NX * NY), (("z", "c"), NZ * NC)):
        sums = jnp.sum(lax.all_to_all(jnp.broadcast_to(sums[None], (size,) + sums.shape), axes, 0, 0), axis=0)
    return sums


def send_blocks(blocks, axis, size, at, core):
    turn = side(at, core)
    found = []
    for step in STEPS[:size]:
        sign = 1 if step % 2 else -1
        block = lax.dynamic_index_in_dim(blocks, lax.rem(at + sign * step * turn + size, size), 0, keepdims=False)
        if step:
            pairs = [(a * NC + c, (a + sign * step * side(a, c)) % size * NC + c)
                     for a in range(size) for c in range(NC)]
            block = lax.ppermute(block, (axis, "c"), pairs)
        found.append(block)
    return found


def exchange(token_rows, x, z, core):
    count = token_rows.shape[0]
    blocks = token_rows.reshape(count, NX, NZ, BLK).transpose(2, 1, 0, 3)
    line = jnp.stack(send_blocks(blocks, "z", NZ, z, core), axis=1)
    return jnp.concatenate(send_blocks(line, "x", NX, x, core))


def gather_tokens(own):
    ahead, behind = near(own, "y", NY, 1), near(own, "y", NY, -1)
    mine = [own, ahead, behind, near(ahead, "y", NY, -1)]
    return mine + [shift(piece, "c", NC, 1) for piece in mine]


def local(token_rows, advantage, cotangent, master, moment_one, moment_two):
    x, z, y, core = (lax.axis_index(name) for name in ("x", "z", "y", "c"))
    place = jnp.stack([x, z, side(x, core), side(z, core), y, core, side(y, core)]).astype(jnp.int32)
    x_pieces = gather_tokens(exchange(token_rows, x, z, core))
    weights = lax.all_gather(advantage, ("y", "c"), axis=0, tiled=True).astype(F32) * SCALE_FIXED
    weighted = (weights[:, None] * cotangent.astype(F32)).astype(BF16)
    mean = jnp.full((8, 128), jnp.sum(weights) / TOK)
    grads, sums = grads_and_sums(place, x_pieces, gather_plane(weighted, ROWS_A), mean)
    sums = total_over_slice(sums)
    new_weights, new_master, new_one, new_two = update(place, sums, grads, master, moment_one, moment_two)
    out = place_rows(place, gather_plane(new_weights, 128))
    return (out.reshape(REP * BLK, BLK), new_master, new_one, new_two)


def solution(mesh):
    fine = Mesh(mesh.devices.reshape(NX, NZ, NY, NC), ("x", "z", "y", "c"))
    dp, tensor = ("x", "z"), ("y", "c")
    state = P(dp, tensor)
    return jax.shard_map(
        local,
        mesh=fine,
        in_specs=(P(dp + tensor, None), P(dp + tensor), state, state, state, state),
        out_specs=(P(None, tensor), state, state, state),
        check_vma=False,
    )
```

profile of v0, /device:TPU:4, one launch (start us, length us, event | category | flops | bytes accessed | tf_op | source)
XLA Modules:
  0.0 239.5 jit_solution(15034616028049094618)
XLA Ops:
  0.6 1.4 dynamic-slice.32
  2.7 0.9 dynamic-update-slice
  3.5 9.5 %all-reduce = s32[512]{0:T(512)S(1)} all-reduce(s32[512]{0:T(512)S(1)} %dynamic-update-slice), channel_id=1, replica_groups=mesh['x'=4,'z'=8,'y'=4,'c'=2] {'y','c'}, use_global_device_ids=true, to_apply=%add | all-reduce | flops 512 | bytes 4096
  13.0 0.6 fusion.1
  13.6 1.1 multiply_convert_fusion
  14.7 0.7 slice_bitcast_fusion.1
  15.4 1.2 collective-permute-start.24
  16.6 2.0 collective-permute-start.17
  18.9 2.3 constant_dynamic-slice_fusion
  21.5 5.9 %collective-permute-start.1 = (bf16[4,64,256]{2,1,0:T(8,128)(2,1)S(1)}, bf16[4,64,256]{2,1,0:T(8,128)(2,1)}, u32[]{:S(2)}, u32[]{:S(2)}) collective-permute-start(bf16[4,64,256]{2,1,0:T(8,128)(2,1)S(1)} %bitcast.109), channel_id=1, source_target_pairs={{0,56},{1,9},{8,16},{9,1},{16,8},{17,25},{24,32},{25,17},{32,24},{... | collective-permute-start | bytes 393224 | tf_op jit(solution)/shard_map/ppermute | solution.py:317
  27.9 4.2 %collective-permute-start.3 = (bf16[4,64,256]{2,1,0:T(8,128)(2,1)S(1)}, bf16[4,64,256]{2,1,0:T(8,128)(2,1)S(1)}, u32[]{:S(2)}, u32[]{:S(2)}) collective-permute-start(bf16[4,64,256]{2,1,0:T(8,128)(2,1)S(1)} %bitcast.114), channel_id=1, source_target_pairs={{0,48},{1,17},{8,24},{9,57},{16,0},{17,33},{24,40},{25,9},{32,16},... | collective-permute-start | bytes 393224 | tf_op jit(solution)/shard_map/ppermute | solution.py:317
  32.1 2.0 collective-permute-start.4
  34.1 0.9 bitcast_dynamic-update-slice_fusion.6
  35.0 0.8 collective-permute-start.5
  35.8 0.9 bitcast_dynamic-update-slice_fusion.5
  36.7 5.6 %collective-permute-start.6 = (bf16[4,64,256]{2,1,0:T(8,128)(2,1)S(1)}, bf16[4,64,256]{2,1,0:T(8,128)(2,1)S(1)}, u32[]{:S(2)}, u32[]{:S(2)}) collective-permute-start(bf16[4,64,256]{2,1,0:T(8,128)(2,1)S(1)} %bitcast.111), channel_id=1, source_target_pairs={{0,32},{1,33},{8,40},{9,41},{16,48},{17,49},{24,56},{25,57},{32,0}... | collective-permute-start | bytes 393224 | tf_op jit(solution)/shard_map/ppermute | solution.py:317
  42.3 0.9 bitcast_dynamic-update-slice_fusion.4
  43.4 2.5 %collective-permute-done.4 = bf16[4,64,256]{2,1,0:T(8,128)(2,1)S(1)} collective-permute-done((bf16[4,64,256]{2,1,0:T(8,128)(2,1)S(1)}, bf16[4,64,256]{2,1,0:T(8,128)(2,1)S(1)}, u32[]{:S(2)}, u32[]{:S(2)}) %collective-permute-start.4) | collective-permute-done | bytes 131104 | tf_op jit(solution)/shard_map/ppermute | solution.py:317
  45.9 5.6 %collective-permute-done.6 = bf16[4,64,256]{2,1,0:T(8,128)(2,1)S(1)} collective-permute-done((bf16[4,64,256]{2,1,0:T(8,128)(2,1)S(1)}, bf16[4,64,256]{2,1,0:T(8,128)(2,1)S(1)}, u32[]{:S(2)}, u32[]{:S(2)}) %collective-permute-start.6) | collective-permute-done | bytes 131104 | tf_op jit(solution)/shard_map/ppermute | solution.py:317
  51.6 3.6 %collective-permute-start.18 = (bf16[2,288,256]{2,1,0:T(8,128)(2,1)S(1)}, bf16[2,288,256]{2,1,0:T(8,128)(2,1)S(1)}, u32[]{:S(2)}, u32[]{:S(2)}) collective-permute-start(bf16[2,288,256]{2,1,0:T(8,128)(2,1)S(1)} %pad_maximum_fusion.4), channel_id=1, source_target_pairs={{0,56},{1,9},{8,16},{9,1},{16,8},{17,25},{24,32},{25,17},{32,24},{... | collective-permute-start | bytes 884744 | tf_op jit(solution)/shard_map/ppermute | solution.py:33
  55.3 1.0 collective-permute-start.9
  56.5 3.6 %collective-permute-start.7 = (bf16[8,64,256]{2,1,0:T(8,128)(2,1)S(1)}, bf16[8,64,256]{2,1,0:T(8,128)(2,1)S(1)}, u32[]{:S(2)}, u32[]{:S(2)}) collective-permute-start(bf16[8,64,256]{2,1,0:T(8,128)(2,1)S(1)} %get-tuple-element.19), channel_id=1, source_target_pairs={{0,64},{1,193},{64,0},{65,129},{128,192},{129,65},{192,128},{193,1... | collective-permute-start | bytes 786440 | tf_op jit(solution)/shard_map/ppermute | solution.py:317
  60.2 1.3 collective-permute-done.18
  61.5 0.8 collective-permute-start.19
  62.3 2.1 collective-permute-done.9
  64.4 2.7 %collective-permute-done.8 = bf16[8,64,256]{2,1,0:T(8,128)(2,1)S(1)} collective-permute-done((bf16[8,64,256]{2,1,0:T(8,128)(2,1)S(1)}, bf16[8,64,256]{2,1,0:T(8,128)(2,1)S(1)}, u32[]{:S(2)}, u32[]{:S(2)}) %collective-permute-start.8) | collective-permute-done | bytes 262176 | tf_op jit(solution)/shard_map/ppermute | solution.py:317
  67.8 5.0 %collective-permute-done.19 = bf16[2,288,256]{2,1,0:T(8,128)(2,1)S(1)} collective-permute-done((bf16[2,288,256]{2,1,0:T(8,128)(2,1)S(1)}, bf16[2,288,256]{2,1,0:T(8,128)(2,1)S(1)}, u32[]{:S(2)}, u32[]{:S(2)}) %collective-permute-start.19) | collective-permute-done | bytes 294944 | tf_op jit(solution)/shard_map/ppermute | solution.py:33
  72.9 3.3 %collective-permute-start.27 = (bf16[2,4,224,256]{3,2,1,0:T(8,128)(2,1)S(1)}, bf16[2,4,224,256]{3,2,1,0:T(8,128)(2,1)S(1)}, u32[]{:S(2)}, u32[]{:S(2)}) collective-permute-start(bf16[2,4,224,256]{3,2,1,0:T(8,128)(2,1)S(1)} %pad_maximum_fusion.1.refs_12_), channel_id=1, source_target_pairs={{0,56},{1,9},{8,16},{9,1},{16,8},{17,25},{24,32},{25,17},{32,24},{... | collective-permute-start | bytes 2752520 | tf_op jit(solution)/shard_map/ppermute | solution.py:33
  76.3 4.4 %collective-permute-done.20 = bf16[2,288,256]{2,1,0:T(8,128)(2,1)S(1)} collective-permute-done((bf16[2,288,256]{2,1,0:T(8,128)(2,1)S(1)}, bf16[2,288,256]{2,1,0:T(8,128)(2,1)S(1)}, u32[]{:S(2)}, u32[]{:S(2)}) %collective-permute-start.20) | collective-permute-done | bytes 294944 | tf_op jit(solution)/shard_map/ppermute | solution.py:33
  81.1 3.4 %collective-permute-done.10.refs_1_ = bf16[32,64,256]{2,1,0:T(8,128)(2,1)} collective-permute-done((bf16[32,64,256]{2,1,0:T(8,128)(2,1)S(1)}, bf16[32,64,256]{2,1,0:T(8,128)(2,1)}, u32[]{:S(2)}, u32[]{:S(2)}) %collective-permute-start.10) | collective-permute-done | bytes 1048608 | tf_op jit(solution)/shard_map/ppermute | solution.py:33
  84.5 7.8 %collective-permute-done.27.refs_13_ = bf16[2,4,224,256]{3,2,1,0:T(8,128)(2,1)S(1)} collective-permute-done((bf16[2,4,224,256]{3,2,1,0:T(8,128)(2,1)S(1)}, bf16[2,4,224,256]{3,2,1,0:T(8,128)(2,1)S(1)}, u32[]{:S(2)}, u32[]{:S(2)}) %collective-permute-start.27) | collective-permute-done | bytes 917536 | tf_op jit(solution)/shard_map/ppermute | solution.py:33
  92.3 16.9 %collective-permute-done.21.refs_9_ = bf16[8,288,256]{2,1,0:T(8,128)(2,1)S(1)} collective-permute-done((bf16[8,288,256]{2,1,0:T(8,128)(2,1)S(1)}, bf16[8,288,256]{2,1,0:T(8,128)(2,1)S(1)}, u32[]{:S(2)}, u32[]{:S(2)}) %collective-permute-start.21) | collective-permute-done | bytes 1179680 | tf_op jit(solution)/shard_map/ppermute | solution.py:33
  109.3 1.1 copy-done.14
  110.4 0.4 collective-permute-start.14
  111.8 0.6 stack.112.place
  112.4 1.4 collective-permute-done.14.refs_5_
  113.8 11.7 %collective-permute-done.23.refs_11_ = bf16[8,288,256]{2,1,0:T(8,128)(2,1)} collective-permute-done((bf16[8,288,256]{2,1,0:T(8,128)(2,1)S(1)}, bf16[8,288,256]{2,1,0:T(8,128)(2,1)}, u32[]{:S(2)}, u32[]{:S(2)}) %collective-permute-start.23) | collective-permute-done | bytes 1179680 | tf_op jit(solution)/shard_map/ppermute | solution.py:33
  125.5 0.5 collective-permute-done.29.refs_15_
  126.0 0.6 broadcast_in_dim.6.refs_16_
  126.6 18.3 %shard_map.93 = (f32[32,256,256]{2,1,0:T(8,128)}, f32[16,128]{1,0:T(8,128)}) custom-call(s32[7]{0:T(128)} %stack.112.place, bf16[32,64,256]{2,1,0:T(8,128)(2,1)} %copy-done.2, bf16[32,64,256]{2,1,0:T(8,128)(2,1)} %collective-permute-done.10.refs_1_, bf16[32,64,256]{2,1,0:T(8,128)(2,1)} %collective-permute-done.11.refs_2_, ...), custom_call_target="tpu_custom_call" | custom-call | flops 6000000000 | bytes 25165824 | tf_op jit(solution)/shard_map/pallas_call | solution.py:155
  144.8 0.7 broadcast_in_dim.7
  145.6 10.7 %all_to_all.10 = f32[16,16,128]{2,1,0:T(8,128)S(1)} all-to-all(f32[16,16,128]{2,1,0:T(8,128)S(1)} %broadcast_in_dim.7), channel_id=1, replica_groups=mesh['x'=4,'z'=8,'y'=4,'c'=2] {'x','y'}, dimensions={0} | all-to-all | bytes 262144 | tf_op jit(solution)/shard_map/all_to_all | solution.py:304
  156.3 11.9 %all_to_all.11 = f32[16,16,128]{2,1,0:T(8,128)S(1)} all-to-all(f32[16,16,128]{2,1,0:T(8,128)S(1)} %broadcast_in_dim.8), channel_id=1, replica_groups=mesh['x'=4,'z'=8,'y'=4,'c'=2] {'z','c'}, dimensions={0} | all-to-all | bytes 262144 | tf_op jit(solution)/shard_map/all_to_all | solution.py:304
  168.2 0.6 reduce_sum.29.sums_ref
  168.8 7.6 %shard_map.94 = (bf16[256,256]{1,0:T(8,128)(2,1)}, f32[256,256]{1,0:T(8,128)}, f32[256,256]{1,0:T(8,128)}, f32[256,256]{1,0:T(8,128)}) custom-call(s32[7]{0:T(128)} %stack.112.place, f32[16,128]{1,0:T(8,128)} %reduce_sum.29.sums_ref, f32[32,256,256]{2,1,0:T(8,128)} %get-tuple-element.11.g_hbm, f32[256,256]{1,0:T(8,128)} %master_ref.1, f32[256,256]{1,0:T(8,128)} %one_ref.1, ...), custom_call_target="tpu_custom_call" | custom-call | flops 5000000 | bytes 10485760 | tf_op jit(solution)/shard_map/pallas_call | solution.py:244
  176.5 0.9 slice_bitcast_fusion
  177.4 1.4 collective-permute-start.37
  178.8 3.0 %collective-permute-done.37 = bf16[128,256]{1,0:T(8,128)(2,1)S(1)} collective-permute-done((bf16[128,256]{1,0:T(8,128)(2,1)S(1)}, bf16[128,256]{1,0:T(8,128)(2,1)S(1)}, u32[]{:S(2)}, u32[]{:S(2)}) %collective-permute-start.37) | collective-permute-done | bytes 65568 | tf_op jit(solution)/shard_map/ppermute | solution.py:33
  181.8 1.4 collective-permute-start.38
  183.2 0.5 collective-permute-start.30
  183.7 3.1 %collective-permute-done.38 = bf16[2,128,256]{2,1,0:T(8,128)(2,1)S(1)} collective-permute-done((bf16[2,128,256]{2,1,0:T(8,128)(2,1)S(1)}, bf16[2,128,256]{2,1,0:T(8,128)(2,1)S(1)}, u32[]{:S(2)}, u32[]{:S(2)}) %collective-permute-start.38) | collective-permute-done | bytes 131104 | tf_op jit(solution)/shard_map/ppermute | solution.py:33
  186.9 0.6 collective-permute-start.39
  187.5 1.3 collective-permute-start.31
  188.9 5.7 %collective-permute-done.31 = bf16[2,128,256]{2,1,0:T(8,128)(2,1)S(1)} collective-permute-done((bf16[2,128,256]{2,1,0:T(8,128)(2,1)S(1)}, bf16[2,128,256]{2,1,0:T(8,128)(2,1)S(1)}, u32[]{:S(2)}, u32[]{:S(2)}) %collective-permute-start.31) | collective-permute-done | bytes 131104 | tf_op jit(solution)/shard_map/ppermute | solution.py:33
  195.2 5.7 %collective-permute-done.32 = bf16[2,128,256]{2,1,0:T(8,128)(2,1)S(1)} collective-permute-done((bf16[2,128,256]{2,1,0:T(8,128)(2,1)S(1)}, bf16[2,128,256]{2,1,0:T(8,128)(2,1)S(1)}, u32[]{:S(2)}, u32[]{:S(2)}) %collective-permute-start.32) | collective-permute-done | bytes 131104 | tf_op jit(solution)/shard_map/ppermute | solution.py:33
  200.9 6.1 %collective-permute-done.33 = bf16[2,128,256]{2,1,0:T(8,128)(2,1)S(1)} collective-permute-done((bf16[2,128,256]{2,1,0:T(8,128)(2,1)S(1)}, bf16[2,128,256]{2,1,0:T(8,128)(2,1)S(1)}, u32[]{:S(2)}, u32[]{:S(2)}) %collective-permute-start.33) | collective-permute-done | bytes 131104 | tf_op jit(solution)/shard_map/ppermute | solution.py:33
  207.1 2.6 %collective-permute-start.34 = (bf16[8,128,256]{2,1,0:T(8,128)(2,1)S(1)}, bf16[8,128,256]{2,1,0:T(8,128)(2,1)S(1)}, u32[]{:S(2)}, u32[]{:S(2)}) collective-permute-start(bf16[8,128,256]{2,1,0:T(8,128)(2,1)S(1)} %constant_dynamic-update-slice_fusion.5.refs_0_), channel_id=1, source_target_pairs={{0,64},{1,193},{64,0},{65,129},{128,192},{129,65},{192,128},{193,1... | collective-permute-start | bytes 1572872 | tf_op jit(solution)/shard_map/ppermute | solution.py:33
  209.7 1.7 collective-permute-start.35
  211.4 11.0 %collective-permute-done.34.refs_1_ = bf16[8,128,256]{2,1,0:T(8,128)(2,1)S(1)} collective-permute-done((bf16[8,128,256]{2,1,0:T(8,128)(2,1)S(1)}, bf16[8,128,256]{2,1,0:T(8,128)(2,1)S(1)}, u32[]{:S(2)}, u32[]{:S(2)}) %collective-permute-start.34) | collective-permute-done | bytes 524320 | tf_op jit(solution)/shard_map/ppermute | solution.py:33
  222.5 1.2 collective-permute-start.42
  223.8 7.8 %collective-permute-done.36.refs_3_ = bf16[8,128,256]{2,1,0:T(8,128)(2,1)S(1)} collective-permute-done((bf16[8,128,256]{2,1,0:T(8,128)(2,1)S(1)}, bf16[8,128,256]{2,1,0:T(8,128)(2,1)S(1)}, u32[]{:S(2)}, u32[]{:S(2)}) %collective-permute-start.36) | collective-permute-done | bytes 524320 | tf_op jit(solution)/shard_map/ppermute | solution.py:33
  231.6 1.4 collective-permute-done.42.refs_7_
  233.0 0.8 copy-done.10
  233.8 5.5 %shard_map.95 = bf16[32,256,256]{2,1,0:T(8,128)(2,1)} custom-call(s32[7]{0:T(128)} %stack.112.place, bf16[8,128,256]{2,1,0:T(8,128)(2,1)} %copy-done.4, bf16[8,128,256]{2,1,0:T(8,128)(2,1)} %copy-done.6, bf16[8,128,256]{2,1,0:T(8,128)(2,1)} %copy-done.8, bf16[8,128,256]{2,1,0:T(8,128)(2,1)} %copy-done.9, bf16[2,4,128,256]{3,2,1,0:T(8,128)(2,1)} %copy-done, ...), custom_call_target="tpu_custom_call" | custom-call | bytes 8388608 | tf_op jit(solution)/shard_map/pallas_call | solution.py:287
  (115 shorter events, 4.1 us)
Async XLA Ops:
  0.6 18.0 %copy-start.1 = (bf16[64,8192]{1,0:T(8,128)(2,1)S(1)}, bf16[64,8192]{1,0:T(8,128)(2,1)}, u32[]{:S(2)}) copy-start(bf16[64,8192]{1,0:T(8,128)(2,1)} %param.6) | copy-start | bytes 3145732
  15.4 12.5 %collective-permute-start.24 = (bf16[224,256]{1,0:T(8,128)(2,1)}, bf16[224,256]{1,0:T(8,128)(2,1)S(1)}, u32[]{:S(2)}, u32[]{:S(2)}) collective-permute-start(bf16[224,256]{1,0:T(8,128)(2,1)} %get-tuple-element.33), channel_id=1, source_target_pairs={{0,64},{1,193},{64,0},{65,129},{128,192},{129,65},{192,128},{193,1... | collective-permute-start | bytes 344072 | tf_op jit(solution)/shard_map/ppermute | solution.py:33
  16.6 34.9 %collective-permute-start.17 = (bf16[288,256]{1,0:T(8,128)(2,1)S(1)}, bf16[288,256]{1,0:T(8,128)(2,1)S(1)}, u32[]{:S(2)}, u32[]{:S(2)}) collective-permute-start(bf16[288,256]{1,0:T(8,128)(2,1)S(1)} %get-tuple-element.35), channel_id=1, source_target_pairs={{0,8},{1,57},{8,0},{9,17},{16,24},{17,9},{24,16},{25,33},{32,40},{... | collective-permute-start | bytes 442376 | tf_op jit(solution)/shard_map/ppermute | solution.py:33
  21.2 10.9 %collective-permute-start = (bf16[4,64,256]{2,1,0:T(8,128)(2,1)S(1)}, bf16[4,64,256]{2,1,0:T(8,128)(2,1)}, u32[]{:S(2)}, u32[]{:S(2)}) collective-permute-start(bf16[4,64,256]{2,1,0:T(8,128)(2,1)S(1)} %bitcast.110), channel_id=1, source_target_pairs={{0,8},{1,57},{8,0},{9,17},{16,24},{17,9},{24,16},{25,33},{32,40},{... | collective-permute-start | bytes 393224 | tf_op jit(solution)/shard_map/ppermute | solution.py:317
  21.5 13.6 %collective-permute-start.1 = (bf16[4,64,256]{2,1,0:T(8,128)(2,1)S(1)}, bf16[4,64,256]{2,1,0:T(8,128)(2,1)}, u32[]{:S(2)}, u32[]{:S(2)}) collective-permute-start(bf16[4,64,256]{2,1,0:T(8,128)(2,1)S(1)} %bitcast.109), channel_id=1, source_target_pairs={{0,56},{1,9},{8,16},{9,1},{16,8},{17,25},{24,32},{25,17},{32,24},{... | collective-permute-start | bytes 393224 | tf_op jit(solution)/shard_map/ppermute | solution.py:317
  27.5 9.2 %collective-permute-start.2 = (bf16[4,64,256]{2,1,0:T(8,128)(2,1)S(1)}, bf16[4,64,256]{2,1,0:T(8,128)(2,1)}, u32[]{:S(2)}, u32[]{:S(2)}) collective-permute-start(bf16[4,64,256]{2,1,0:T(8,128)(2,1)S(1)} %bitcast.108), channel_id=1, source_target_pairs={{0,16},{1,49},{8,56},{9,25},{16,32},{17,1},{24,8},{25,41},{32,48},... | collective-permute-start | bytes 393224 | tf_op jit(solution)/shard_map/ppermute | solution.py:317
  27.9 15.3 %collective-permute-start.3 = (bf16[4,64,256]{2,1,0:T(8,128)(2,1)S(1)}, bf16[4,64,256]{2,1,0:T(8,128)(2,1)S(1)}, u32[]{:S(2)}, u32[]{:S(2)}) collective-permute-start(bf16[4,64,256]{2,1,0:T(8,128)(2,1)S(1)} %bitcast.114), channel_id=1, source_target_pairs={{0,48},{1,17},{8,24},{9,57},{16,0},{17,33},{24,40},{25,9},{32,16},... | collective-permute-start | bytes 393224 | tf_op jit(solution)/shard_map/ppermute | solution.py:317
  32.1 13.7 %collective-permute-start.4 = (bf16[4,64,256]{2,1,0:T(8,128)(2,1)S(1)}, bf16[4,64,256]{2,1,0:T(8,128)(2,1)S(1)}, u32[]{:S(2)}, u32[]{:S(2)}) collective-permute-start(bf16[4,64,256]{2,1,0:T(8,128)(2,1)S(1)} %bitcast.113), channel_id=1, source_target_pairs={{0,24},{1,41},{8,48},{9,33},{16,40},{17,57},{24,0},{25,49},{32,56}... | collective-permute-start | bytes 393224 | tf_op jit(solution)/shard_map/ppermute | solution.py:317
  35.0 10.8 %collective-permute-start.5 = (bf16[4,64,256]{2,1,0:T(8,128)(2,1)S(1)}, bf16[4,64,256]{2,1,0:T(8,128)(2,1)S(1)}, u32[]{:S(2)}, u32[]{:S(2)}) collective-permute-start(bf16[4,64,256]{2,1,0:T(8,128)(2,1)S(1)} %bitcast.112), channel_id=1, source_target_pairs={{0,40},{1,25},{8,32},{9,49},{16,56},{17,41},{24,48},{25,1},{32,8},... | collective-permute-start | bytes 393224 | tf_op jit(solution)/shard_map/ppermute | solution.py:317
  36.7 14.8 %collective-permute-start.6 = (bf16[4,64,256]{2,1,0:T(8,128)(2,1)S(1)}, bf16[4,64,256]{2,1,0:T(8,128)(2,1)S(1)}, u32[]{:S(2)}, u32[]{:S(2)}) collective-permute-start(bf16[4,64,256]{2,1,0:T(8,128)(2,1)S(1)} %bitcast.111), channel_id=1, source_target_pairs={{0,32},{1,33},{8,40},{9,41},{16,48},{17,49},{24,56},{25,57},{32,0}... | collective-permute-start | bytes 393224 | tf_op jit(solution)/shard_map/ppermute | solution.py:317
  43.2 16.8 %collective-permute-start.25 = (bf16[2,224,256]{2,1,0:T(8,128)(2,1)S(1)}, bf16[2,224,256]{2,1,0:T(8,128)(2,1)S(1)}, u32[]{:S(2)}, u32[]{:S(2)}) collective-permute-start(bf16[2,224,256]{2,1,0:T(8,128)(2,1)S(1)} %pad_maximum_fusion.6), channel_id=1, source_target_pairs={{0,192},{1,65},{64,128},{65,1},{128,64},{129,193},{192,0},{193,129... | collective-permute-start | bytes 688136 | tf_op jit(solution)/shard_map/ppermute | solution.py:33
  51.6 9.9 %collective-permute-start.18 = (bf16[2,288,256]{2,1,0:T(8,128)(2,1)S(1)}, bf16[2,288,256]{2,1,0:T(8,128)(2,1)S(1)}, u32[]{:S(2)}, u32[]{:S(2)}) collective-permute-start(bf16[2,288,256]{2,1,0:T(8,128)(2,1)S(1)} %pad_maximum_fusion.4), channel_id=1, source_target_pairs={{0,56},{1,9},{8,16},{9,1},{16,8},{17,25},{24,32},{25,17},{32,24},{... | collective-permute-start | bytes 884744 | tf_op jit(solution)/shard_map/ppermute | solution.py:33
  55.3 9.1 %collective-permute-start.9 = (bf16[8,64,256]{2,1,0:T(8,128)(2,1)S(1)}, bf16[8,64,256]{2,1,0:T(8,128)(2,1)S(1)}, u32[]{:S(2)}, u32[]{:S(2)}) collective-permute-start(bf16[8,64,256]{2,1,0:T(8,128)(2,1)S(1)} %get-tuple-element.17), channel_id=1, source_target_pairs={{0,128},{1,129},{64,192},{65,193},{128,0},{129,1},{192,64},{193,65... | collective-permute-start | bytes 786440 | tf_op jit(solution)/shard_map/ppermute | solution.py:317
  56.3 10.8 %collective-permute-start.8 = (bf16[8,64,256]{2,1,0:T(8,128)(2,1)S(1)}, bf16[8,64,256]{2,1,0:T(8,128)(2,1)S(1)}, u32[]{:S(2)}, u32[]{:S(2)}) collective-permute-start(bf16[8,64,256]{2,1,0:T(8,128)(2,1)S(1)} %get-tuple-element.18), channel_id=1, source_target_pairs={{0,192},{1,65},{64,128},{65,1},{128,64},{129,193},{192,0},{193,129... | collective-permute-start | bytes 786440 | tf_op jit(solution)/shard_map/ppermute | solution.py:317
  56.5 10.9 %collective-permute-start.7 = (bf16[8,64,256]{2,1,0:T(8,128)(2,1)S(1)}, bf16[8,64,256]{2,1,0:T(8,128)(2,1)S(1)}, u32[]{:S(2)}, u32[]{:S(2)}) collective-permute-start(bf16[8,64,256]{2,1,0:T(8,128)(2,1)S(1)} %get-tuple-element.19), channel_id=1, source_target_pairs={{0,64},{1,193},{64,0},{65,129},{128,192},{129,65},{192,128},{193,1... | collective-permute-start | bytes 786440 | tf_op jit(solution)/shard_map/ppermute | solution.py:317
  60.1 12.7 %collective-permute-start.26 = (bf16[4,224,256]{2,1,0:T(8,128)(2,1)S(1)}, bf16[4,224,256]{2,1,0:T(8,128)(2,1)S(1)}, u32[]{:S(2)}, u32[]{:S(2)}) collective-permute-start(bf16[4,224,256]{2,1,0:T(8,128)(2,1)S(1)} %get-tuple-element.29), channel_id=1, source_target_pairs={{0,8},{1,57},{8,0},{9,17},{16,24},{17,9},{24,16},{25,33},{32,40},{... | collective-permute-start | bytes 1376264 | tf_op jit(solution)/shard_map/ppermute | solution.py:33
  61.5 11.3 %collective-permute-start.19 = (bf16[2,288,256]{2,1,0:T(8,128)(2,1)S(1)}, bf16[2,288,256]{2,1,0:T(8,128)(2,1)S(1)}, u32[]{:S(2)}, u32[]{:S(2)}) collective-permute-start(bf16[2,288,256]{2,1,0:T(8,128)(2,1)S(1)} %collective-permute-done.18), channel_id=1, source_target_pairs={{0,8},{1,57},{8,0},{9,17},{16,24},{17,9},{24,16},{25,33},{32,40},{... | collective-permute-start | bytes 884744 | tf_op jit(solution)/shard_map/ppermute | solution.py:33
  67.5 13.5 %copy-start.2 = (bf16[32,64,256]{2,1,0:T(8,128)(2,1)}, bf16[32,64,256]{2,1,0:T(8,128)(2,1)S(1)}, u32[]{:S(2)}) copy-start(bf16[32,64,256]{2,1,0:T(8,128)(2,1)S(1)} %pad_maximum_fusion.refs_0_) | copy-start | bytes 3145732
  67.5 13.4 %collective-permute-start.13 = (bf16[32,64,256]{2,1,0:T(8,128)(2,1)S(1)}, bf16[32,64,256]{2,1,0:T(8,128)(2,1)S(1)}, u32[]{:S(2)}, u32[]{:S(2)}) collective-permute-start(bf16[32,64,256]{2,1,0:T(8,128)(2,1)S(1)} %pad_maximum_fusion.refs_0_), channel_id=1, source_target_pairs={{0,1},{1,0},{2,3},{3,2},{4,5},{5,4},{6,7},{7,6},{8,9},{9,8},{10,11... | collective-permute-start | bytes 3145736 | tf_op jit(solution)/shard_map/ppermute | solution.py:24
  67.6 16.9 %collective-permute-start.10 = (bf16[32,64,256]{2,1,0:T(8,128)(2,1)S(1)}, bf16[32,64,256]{2,1,0:T(8,128)(2,1)}, u32[]{:S(2)}, u32[]{:S(2)}) collective-permute-start(bf16[32,64,256]{2,1,0:T(8,128)(2,1)S(1)} %pad_maximum_fusion.refs_0_), channel_id=1, source_target_pairs={{0,2},{1,7},{2,0},{3,5},{4,6},{5,3},{6,4},{7,1},{8,10},{9,15},{10,... | collective-permute-start | bytes 3145736 | tf_op jit(solution)/shard_map/ppermute | solution.py:33
  72.8 7.9 %collective-permute-start.20 = (bf16[2,288,256]{2,1,0:T(8,128)(2,1)S(1)}, bf16[2,288,256]{2,1,0:T(8,128)(2,1)S(1)}, u32[]{:S(2)}, u32[]{:S(2)}) collective-permute-start(bf16[2,288,256]{2,1,0:T(8,128)(2,1)S(1)} %collective-permute-done.19), channel_id=1, source_target_pairs={{0,56},{1,9},{8,16},{9,1},{16,8},{17,25},{24,32},{25,17},{32,24},{... | collective-permute-start | bytes 884744 | tf_op jit(solution)/shard_map/ppermute | solution.py:33
  72.9 53.7 %copy-start.3 = (bf16[2,4,224,256]{3,2,1,0:T(8,128)(2,1)}, bf16[2,4,224,256]{3,2,1,0:T(8,128)(2,1)S(1)}, u32[]{:S(2)}) copy-start(bf16[2,4,224,256]{3,2,1,0:T(8,128)(2,1)S(1)} %pad_maximum_fusion.1.refs_12_) | copy-start | bytes 2752516
  72.9 19.4 %collective-permute-start.27 = (bf16[2,4,224,256]{3,2,1,0:T(8,128)(2,1)S(1)}, bf16[2,4,224,256]{3,2,1,0:T(8,128)(2,1)S(1)}, u32[]{:S(2)}, u32[]{:S(2)}) collective-permute-start(bf16[2,4,224,256]{3,2,1,0:T(8,128)(2,1)S(1)} %pad_maximum_fusion.1.refs_12_), channel_id=1, source_target_pairs={{0,56},{1,9},{8,16},{9,1},{16,8},{17,25},{24,32},{25,17},{32,24},{... | collective-permute-start | bytes 2752520 | tf_op jit(solution)/shard_map/ppermute | solution.py:33
  80.8 28.4 %copy-start.12 = (bf16[8,288,256]{2,1,0:T(8,128)(2,1)}, bf16[8,288,256]{2,1,0:T(8,128)(2,1)S(1)}, u32[]{:S(2)}) copy-start(bf16[8,288,256]{2,1,0:T(8,128)(2,1)S(1)} %constant_dynamic-update-slice_fusion.refs_8_) | copy-start | bytes 3538948
  80.8 28.4 %collective-permute-start.21 = (bf16[8,288,256]{2,1,0:T(8,128)(2,1)S(1)}, bf16[8,288,256]{2,1,0:T(8,128)(2,1)S(1)}, u32[]{:S(2)}, u32[]{:S(2)}) collective-permute-start(bf16[8,288,256]{2,1,0:T(8,128)(2,1)S(1)} %constant_dynamic-update-slice_fusion.refs_8_), channel_id=1, source_target_pairs={{0,64},{1,193},{64,0},{65,129},{128,192},{129,65},{192,128},{193,1... | collective-permute-start | bytes 3538952 | tf_op jit(solution)/shard_map/ppermute | solution.py:33
  80.9 28.4 %collective-permute-start.22 = (bf16[8,288,256]{2,1,0:T(8,128)(2,1)S(1)}, bf16[8,288,256]{2,1,0:T(8,128)(2,1)S(1)}, u32[]{:S(2)}, u32[]{:S(2)}) collective-permute-start(bf16[8,288,256]{2,1,0:T(8,128)(2,1)S(1)} %constant_dynamic-update-slice_fusion.refs_8_), channel_id=1, source_target_pairs={{0,192},{1,65},{64,128},{65,1},{128,64},{129,193},{192,0},{193,129... | collective-permute-start | bytes 3538952 | tf_op jit(solution)/shard_map/ppermute | solution.py:33
  81.0 29.8 %copy-start.15 = (bf16[32,64,256]{2,1,0:T(8,128)(2,1)}, bf16[32,64,256]{2,1,0:T(8,128)(2,1)S(1)}, u32[]{:S(2)}) copy-start(bf16[32,64,256]{2,1,0:T(8,128)(2,1)S(1)} %collective-permute-done.13.refs_4_) | copy-start | bytes 3145732
  81.0 28.2 %collective-permute-start.11 = (bf16[32,64,256]{2,1,0:T(8,128)(2,1)S(1)}, bf16[32,64,256]{2,1,0:T(8,128)(2,1)}, u32[]{:S(2)}, u32[]{:S(2)}) collective-permute-start(bf16[32,64,256]{2,1,0:T(8,128)(2,1)S(1)} %pad_maximum_fusion.refs_0_), channel_id=1, source_target_pairs={{0,6},{1,3},{2,4},{3,1},{4,2},{5,7},{6,0},{7,5},{8,14},{9,11},{10,... | collective-permute-start | bytes 3145736 | tf_op jit(solution)/shard_map/ppermute | solution.py:33
  84.5 26.3 %collective-permute-start.12 = (bf16[32,64,256]{2,1,0:T(8,128)(2,1)}, bf16[32,64,256]{2,1,0:T(8,128)(2,1)}, u32[]{:S(2)}, u32[]{:S(2)}) collective-permute-start(bf16[32,64,256]{2,1,0:T(8,128)(2,1)} %collective-permute-done.10.refs_1_), channel_id=1, source_target_pairs={{0,6},{1,3},{2,4},{3,1},{4,2},{5,7},{6,0},{7,5},{8,14},{9,11},{10,... | collective-permute-start | bytes 3145736 | tf_op jit(solution)/shard_map/ppermute | solution.py:33
  92.3 18.5 %copy-start.17 = (bf16[2,4,224,256]{3,2,1,0:T(8,128)(2,1)}, bf16[2,4,224,256]{3,2,1,0:T(8,128)(2,1)S(1)}, u32[]{:S(2)}) copy-start(bf16[2,4,224,256]{3,2,1,0:T(8,128)(2,1)S(1)} %collective-permute-done.27.refs_13_) | copy-start | bytes 2752516
  92.3 18.7 %collective-permute-start.28 = (bf16[2,4,224,256]{3,2,1,0:T(8,128)(2,1)S(1)}, bf16[2,4,224,256]{3,2,1,0:T(8,128)(2,1)}, u32[]{:S(2)}, u32[]{:S(2)}) collective-permute-start(bf16[2,4,224,256]{3,2,1,0:T(8,128)(2,1)S(1)} %collective-permute-done.27.refs_13_), channel_id=1, source_target_pairs={{0,8},{1,57},{8,0},{9,17},{16,24},{17,9},{24,16},{25,33},{32,40},{... | collective-permute-start | bytes 2752520 | tf_op jit(solution)/shard_map/ppermute | solution.py:33
  109.2 17.4 %copy-start.13 = (bf16[8,288,256]{2,1,0:T(8,128)(2,1)}, bf16[8,288,256]{2,1,0:T(8,128)(2,1)S(1)}, u32[]{:S(2)}) copy-start(bf16[8,288,256]{2,1,0:T(8,128)(2,1)S(1)} %collective-permute-done.21.refs_9_) | copy-start | bytes 3538948
  109.2 16.3 %collective-permute-start.23 = (bf16[8,288,256]{2,1,0:T(8,128)(2,1)S(1)}, bf16[8,288,256]{2,1,0:T(8,128)(2,1)}, u32[]{:S(2)}, u32[]{:S(2)}) collective-permute-start(bf16[8,288,256]{2,1,0:T(8,128)(2,1)S(1)} %collective-permute-done.21.refs_9_), channel_id=1, source_target_pairs={{0,192},{1,65},{64,128},{65,1},{128,64},{129,193},{192,0},{193,129... | collective-permute-start | bytes 3538952 | tf_op jit(solution)/shard_map/ppermute | solution.py:33
  109.2 3.2 %collective-permute-start.15 = (bf16[32,64,256]{2,1,0:T(8,128)(2,1)}, bf16[32,64,256]{2,1,0:T(8,128)(2,1)S(1)}, u32[]{:S(2)}, u32[]{:S(2)}) collective-permute-start(bf16[32,64,256]{2,1,0:T(8,128)(2,1)} %collective-permute-done.11.refs_2_), channel_id=1, source_target_pairs={{0,1},{1,0},{2,3},{3,2},{4,5},{5,4},{6,7},{7,6},{8,9},{9,8},{10,11... | collective-permute-start | bytes 3145736 | tf_op jit(solution)/shard_map/ppermute | solution.py:24
  109.3 1.1 copy-start.14
  110.4 3.4 %collective-permute-start.14 = (bf16[32,64,256]{2,1,0:T(8,128)(2,1)}, bf16[32,64,256]{2,1,0:T(8,128)(2,1)}, u32[]{:S(2)}, u32[]{:S(2)}) collective-permute-start(bf16[32,64,256]{2,1,0:T(8,128)(2,1)} %collective-permute-done.10.refs_1_), channel_id=1, source_target_pairs={{0,1},{1,0},{2,3},{3,2},{4,5},{5,4},{6,7},{7,6},{8,9},{9,8},{10,11... | collective-permute-start | bytes 3145736 | tf_op jit(solution)/shard_map/ppermute | solution.py:24
  110.8 14.7 %collective-permute-start.16 = (bf16[32,64,256]{2,1,0:T(8,128)(2,1)}, bf16[32,64,256]{2,1,0:T(8,128)(2,1)}, u32[]{:S(2)}, u32[]{:S(2)}) collective-permute-start(bf16[32,64,256]{2,1,0:T(8,128)(2,1)} %collective-permute-done.12.refs_3_), channel_id=1, source_target_pairs={{0,1},{1,0},{2,3},{3,2},{4,5},{5,4},{6,7},{7,6},{8,9},{9,8},{10,11... | collective-permute-start | bytes 3145736 | tf_op jit(solution)/shard_map/ppermute | solution.py:24
  111.0 14.9 %collective-permute-start.29 = (bf16[2,4,224,256]{3,2,1,0:T(8,128)(2,1)}, bf16[2,4,224,256]{3,2,1,0:T(8,128)(2,1)}, u32[]{:S(2)}, u32[]{:S(2)}) collective-permute-start(bf16[2,4,224,256]{3,2,1,0:T(8,128)(2,1)} %collective-permute-done.28.refs_14_), channel_id=1, source_target_pairs={{0,56},{1,9},{8,16},{9,1},{16,8},{17,25},{24,32},{25,17},{32,24},{... | collective-permute-start | bytes 2752520 | tf_op jit(solution)/shard_map/ppermute | solution.py:33
  112.4 14.2 %copy-start.16 = (bf16[32,64,256]{2,1,0:T(8,128)(2,1)}, bf16[32,64,256]{2,1,0:T(8,128)(2,1)S(1)}, u32[]{:S(2)}) copy-start(bf16[32,64,256]{2,1,0:T(8,128)(2,1)S(1)} %collective-permute-done.15.refs_6_) | copy-start | bytes 3145732
  176.5 12.4 %copy-start.11 = (bf16[256,256]{1,0:T(8,128)(2,1)S(1)}, bf16[256,256]{1,0:T(8,128)(2,1)}, u32[]{:S(2)}) copy-start(bf16[256,256]{1,0:T(8,128)(2,1)} %get-tuple-element.12) | copy-start | bytes 393220
  177.4 4.4 %collective-permute-start.37 = (bf16[128,256]{1,0:T(8,128)(2,1)S(1)}, bf16[128,256]{1,0:T(8,128)(2,1)S(1)}, u32[]{:S(2)}, u32[]{:S(2)}) collective-permute-start(bf16[128,256]{1,0:T(8,128)(2,1)S(1)} %get-tuple-element.38), channel_id=1, source_target_pairs={{0,64},{1,193},{64,0},{65,129},{128,192},{129,65},{192,128},{193,1... | collective-permute-start | bytes 196616 | tf_op jit(solution)/shard_map/ppermute | solution.py:33
  181.8 5.1 %collective-permute-start.38 = (bf16[2,128,256]{2,1,0:T(8,128)(2,1)S(1)}, bf16[2,128,256]{2,1,0:T(8,128)(2,1)S(1)}, u32[]{:S(2)}, u32[]{:S(2)}) collective-permute-start(bf16[2,128,256]{2,1,0:T(8,128)(2,1)S(1)} %pad_maximum_fusion.8), channel_id=1, source_target_pairs={{0,192},{1,65},{64,128},{65,1},{128,64},{129,193},{192,0},{193,129... | collective-permute-start | bytes 393224 | tf_op jit(solution)/shard_map/ppermute | solution.py:33
  183.2 4.3 %collective-permute-start.30 = (bf16[128,256]{1,0:T(8,128)(2,1)S(1)}, bf16[128,256]{1,0:T(8,128)(2,1)S(1)}, u32[]{:S(2)}, u32[]{:S(2)}) collective-permute-start(bf16[128,256]{1,0:T(8,128)(2,1)S(1)} %get-tuple-element.39), channel_id=1, source_target_pairs={{0,8},{1,57},{8,0},{9,17},{16,24},{17,9},{24,16},{25,33},{32,40},{... | collective-permute-start | bytes 196616 | tf_op jit(solution)/shard_map/ppermute | solution.py:33
  186.9 7.9 %collective-permute-start.39 = (bf16[4,128,256]{2,1,0:T(8,128)(2,1)S(1)}, bf16[4,128,256]{2,1,0:T(8,128)(2,1)S(1)}, u32[]{:S(2)}, u32[]{:S(2)}) collective-permute-start(bf16[4,128,256]{2,1,0:T(8,128)(2,1)S(1)} %get-tuple-element.31), channel_id=1, source_target_pairs={{0,8},{1,57},{8,0},{9,17},{16,24},{17,9},{24,16},{25,33},{32,40},{... | collective-permute-start | bytes 786440 | tf_op jit(solution)/shard_map/ppermute | solution.py:33
  187.5 7.1 %collective-permute-start.31 = (bf16[2,128,256]{2,1,0:T(8,128)(2,1)S(1)}, bf16[2,128,256]{2,1,0:T(8,128)(2,1)S(1)}, u32[]{:S(2)}, u32[]{:S(2)}) collective-permute-start(bf16[2,128,256]{2,1,0:T(8,128)(2,1)S(1)} %pad_maximum_fusion.7), channel_id=1, source_target_pairs={{0,56},{1,9},{8,16},{9,1},{16,8},{17,25},{24,32},{25,17},{32,24},{... | collective-permute-start | bytes 393224 | tf_op jit(solution)/shard_map/ppermute | solution.py:33
  194.6 6.3 %collective-permute-start.32 = (bf16[2,128,256]{2,1,0:T(8,128)(2,1)S(1)}, bf16[2,128,256]{2,1,0:T(8,128)(2,1)S(1)}, u32[]{:S(2)}, u32[]{:S(2)}) collective-permute-start(bf16[2,128,256]{2,1,0:T(8,128)(2,1)S(1)} %collective-permute-done.31), channel_id=1, source_target_pairs={{0,8},{1,57},{8,0},{9,17},{16,24},{17,9},{24,16},{25,33},{32,40},{... | collective-permute-start | bytes 393224 | tf_op jit(solution)/shard_map/ppermute | solution.py:33
  194.8 38.1 %copy-start = (bf16[2,4,128,256]{3,2,1,0:T(8,128)(2,1)}, bf16[2,4,128,256]{3,2,1,0:T(8,128)(2,1)S(1)}, u32[]{:S(2)}) copy-start(bf16[2,4,128,256]{3,2,1,0:T(8,128)(2,1)S(1)} %pad_maximum_fusion.2.refs_4_) | copy-start | bytes 1572868
  194.8 14.9 %collective-permute-start.40 = (bf16[2,4,128,256]{3,2,1,0:T(8,128)(2,1)S(1)}, bf16[2,4,128,256]{3,2,1,0:T(8,128)(2,1)S(1)}, u32[]{:S(2)}, u32[]{:S(2)}) collective-permute-start(bf16[2,4,128,256]{3,2,1,0:T(8,128)(2,1)S(1)} %pad_maximum_fusion.2.refs_4_), channel_id=1, source_target_pairs={{0,56},{1,9},{8,16},{9,1},{16,8},{17,25},{24,32},{25,17},{32,24},{... | collective-permute-start | bytes 1572872 | tf_op jit(solution)/shard_map/ppermute | solution.py:33
  200.9 6.2 %collective-permute-start.33 = (bf16[2,128,256]{2,1,0:T(8,128)(2,1)S(1)}, bf16[2,128,256]{2,1,0:T(8,128)(2,1)S(1)}, u32[]{:S(2)}, u32[]{:S(2)}) collective-permute-start(bf16[2,128,256]{2,1,0:T(8,128)(2,1)S(1)} %collective-permute-done.32), channel_id=1, source_target_pairs={{0,56},{1,9},{8,16},{9,1},{16,8},{17,25},{24,32},{25,17},{32,24},{... | collective-permute-start | bytes 393224 | tf_op jit(solution)/shard_map/ppermute | solution.py:33
  207.1 25.8 %copy-start.4 = (bf16[8,128,256]{2,1,0:T(8,128)(2,1)}, bf16[8,128,256]{2,1,0:T(8,128)(2,1)S(1)}, u32[]{:S(2)}) copy-start(bf16[8,128,256]{2,1,0:T(8,128)(2,1)S(1)} %constant_dynamic-update-slice_fusion.5.refs_0_) | copy-start | bytes 1572868
  207.1 15.3 %collective-permute-start.34 = (bf16[8,128,256]{2,1,0:T(8,128)(2,1)S(1)}, bf16[8,128,256]{2,1,0:T(8,128)(2,1)S(1)}, u32[]{:S(2)}, u32[]{:S(2)}) collective-permute-start(bf16[8,128,256]{2,1,0:T(8,128)(2,1)S(1)} %constant_dynamic-update-slice_fusion.5.refs_0_), channel_id=1, source_target_pairs={{0,64},{1,193},{64,0},{65,129},{128,192},{129,65},{192,128},{193,1... | collective-permute-start | bytes 1572872 | tf_op jit(solution)/shard_map/ppermute | solution.py:33
  209.7 23.3 %copy-start.5 = (bf16[2,4,128,256]{3,2,1,0:T(8,128)(2,1)}, bf16[2,4,128,256]{3,2,1,0:T(8,128)(2,1)S(1)}, u32[]{:S(2)}) copy-start(bf16[2,4,128,256]{3,2,1,0:T(8,128)(2,1)S(1)} %collective-permute-done.40.refs_5_) | copy-start | bytes 1572868
  209.7 12.9 %collective-permute-start.41 = (bf16[2,4,128,256]{3,2,1,0:T(8,128)(2,1)S(1)}, bf16[2,4,128,256]{3,2,1,0:T(8,128)(2,1)S(1)}, u32[]{:S(2)}, u32[]{:S(2)}) collective-permute-start(bf16[2,4,128,256]{3,2,1,0:T(8,128)(2,1)S(1)} %collective-permute-done.40.refs_5_), channel_id=1, source_target_pairs={{0,8},{1,57},{8,0},{9,17},{16,24},{17,9},{24,16},{25,33},{32,40},{... | collective-permute-start | bytes 1572872 | tf_op jit(solution)/shard_map/ppermute | solution.py:33
  209.7 14.1 %collective-permute-start.35 = (bf16[8,128,256]{2,1,0:T(8,128)(2,1)S(1)}, bf16[8,128,256]{2,1,0:T(8,128)(2,1)S(1)}, u32[]{:S(2)}, u32[]{:S(2)}) collective-permute-start(bf16[8,128,256]{2,1,0:T(8,128)(2,1)S(1)} %constant_dynamic-update-slice_fusion.5.refs_0_), channel_id=1, source_target_pairs={{0,192},{1,65},{64,128},{65,1},{128,64},{129,193},{192,0},{193,129... | collective-permute-start | bytes 1572872 | tf_op jit(solution)/shard_map/ppermute | solution.py:33
  222.4 10.6 %copy-start.6 = (bf16[8,128,256]{2,1,0:T(8,128)(2,1)}, bf16[8,128,256]{2,1,0:T(8,128)(2,1)S(1)}, u32[]{:S(2)}) copy-start(bf16[8,128,256]{2,1,0:T(8,128)(2,1)S(1)} %collective-permute-done.34.refs_1_) | copy-start | bytes 1572868
  222.4 9.2 %collective-permute-start.36 = (bf16[8,128,256]{2,1,0:T(8,128)(2,1)S(1)}, bf16[8,128,256]{2,1,0:T(8,128)(2,1)S(1)}, u32[]{:S(2)}, u32[]{:S(2)}) collective-permute-start(bf16[8,128,256]{2,1,0:T(8,128)(2,1)S(1)} %collective-permute-done.34.refs_1_), channel_id=1, source_target_pairs={{0,192},{1,65},{64,128},{65,1},{128,64},{129,193},{192,0},{193,129... | collective-permute-start | bytes 1572872 | tf_op jit(solution)/shard_map/ppermute | solution.py:33
  222.5 10.4 %copy-start.7 = (bf16[2,4,128,256]{3,2,1,0:T(8,128)(2,1)}, bf16[2,4,128,256]{3,2,1,0:T(8,128)(2,1)S(1)}, u32[]{:S(2)}) copy-start(bf16[2,4,128,256]{3,2,1,0:T(8,128)(2,1)S(1)} %collective-permute-done.41.refs_6_) | copy-start | bytes 1572868
  222.5 10.4 %collective-permute-start.42 = (bf16[2,4,128,256]{3,2,1,0:T(8,128)(2,1)S(1)}, bf16[2,4,128,256]{3,2,1,0:T(8,128)(2,1)S(1)}, u32[]{:S(2)}, u32[]{:S(2)}) collective-permute-start(bf16[2,4,128,256]{3,2,1,0:T(8,128)(2,1)S(1)} %collective-permute-done.41.refs_6_), channel_id=1, source_target_pairs={{0,56},{1,9},{8,16},{9,1},{16,8},{17,25},{24,32},{25,17},{32,24},{... | collective-permute-start | bytes 1572872 | tf_op jit(solution)/shard_map/ppermute | solution.py:33
  223.8 9.2 %copy-start.8 = (bf16[8,128,256]{2,1,0:T(8,128)(2,1)}, bf16[8,128,256]{2,1,0:T(8,128)(2,1)S(1)}, u32[]{:S(2)}) copy-start(bf16[8,128,256]{2,1,0:T(8,128)(2,1)S(1)} %collective-permute-done.35.refs_2_) | copy-start | bytes 1572868
  231.6 1.4 copy-start.9
  233.0 0.8 copy-start.10
where the time goes:
time: 242 us; the launch traced here: 239 us
  waiting for transfers between devices  110 us (45%)
  starting transfers between devices  47.2 us (20%)
  blocking collectives  32.1 us (13%)
  Pallas kernels  31.4 us (13%)
  local copies, waits for them, and re-layouts  13.5 us (6%)
  between operations  2.8 us (1%)
  other arithmetic  2.79 us (1%)
    ppermute x29, waiting for transfers between devices, near(): return lax.ppermute(array, (axis, 'c'), pairs)  94.9 us
    ppermute x10, starting transfers between devices, send_blocks(): block = lax.ppermute(block, (axis, 'c'), pairs)  23.5 us
    ppermute x29, starting transfers between devices, near(): return lax.ppermute(array, (axis, 'c'), pairs)  22.9 us
    all_to_all x2, blocking collectives, total_over_slice(): lax.all_to_all(jnp.broadcast_to(sums[None], (size,) + sums.shape), axes,...  22.6 us
    pallas_call x1, Pallas kernels, grads_and_sums(): pl.pallas_call(functools.partial(grads_kernel, layout), out_shape=(jax.Sh...  18.3 us
    ppermute x10, waiting for transfers between devices, send_blocks(): block = lax.ppermute(block, (axis, 'c'), pairs)  13.3 us
    unnamed x1, blocking collectives  9.48 us
    unnamed x62, local copies, waits for them, and re-layouts  7.65 us
  transfers between devices with their start and end apart: 43, of which 23 were waited for; matrix products, arithmetic and copies ran while one was open for 3% of the time, Pallas kernels for 0%

commit v1 on v0

v1 whole, which is shorter than its diff:
```python
import functools
import jax
import jax.numpy as jnp
from jax import lax
from jax.experimental import pallas as pl
from jax.experimental.pallas import tpu as pltpu
from jax.sharding import Mesh, PartitionSpec as P

STEP = 10
SCALE_FIXED = 2.0 ** (-12)
EPS_ADA = 1e-06

NX, NZ, NY, NC = 4, 8, 4, 2
REP = NX * NZ
TOK = 512
BLK = 256
F32 = jnp.float32
BF16 = jnp.bfloat16
HIGH = lax.Precision.HIGHEST


def shift(array, axis, size, by):
    return lax.ppermute(array, axis, [(i, (i + by) % size) for i in range(size)])


def side(at, core):
    return 1 - 2 * ((at + core) % 2)


def near(array, axis, size, which):
    pairs = [(a * NC + c, (a + which * side(a, c)) % size * NC + c) for a in range(size) for c in range(NC)]
    return lax.ppermute(array, (axis, "c"), pairs)


def swapped_ring(block, axis, size):
    pair = jnp.stack([block, near(block, axis, size, 1)])
    found, held, which = [pair], pair, -1
    for _ in range(size // 2 - 1):
        held = near(held, axis, size, which)
        found.append(held)
        which = -which
    return found


def gather_plane(block):
    out = []
    for line in swapped_ring(block, "z", NZ):
        ahead, behind = near(line, "x", NX, 1), near(line, "x", NX, -1)
        out += [line, ahead, behind, near(ahead, "x", NX, -1)]
    return out


STEPS = (0, 1, -1, -2, 2, 3, -3, -4)


def step_of(k):
    return sum(jnp.where(k == i, step, 0) for i, step in enumerate(STEPS))


def replicas_of(place, slots):
    x = lax.rem(place[0] + place[2] * step_of(slots % NX) + NX, NX)
    z = lax.rem(place[1] + place[3] * step_of(slots // NX) + NZ, NZ)
    return x * NZ + z


def replica_of(place, slot):
    x = lax.rem(place[0] + place[2] * STEPS[slot % NX] + NX, NX)
    z = lax.rem(place[1] + place[3] * STEPS[slot // NX] + NZ, NZ)
    return x * NZ + z


def grads_kernel(count, place, *refs):
    tokens = NY * NC
    x_pieces, refs = refs[:tokens], refs[tokens:]
    pieces, (weights_ref, g_hbm, sums_ref) = refs[:count], refs[count:count + 3]
    xv, wv, gv, xsem, wsem, gsem = refs[count + 3:]
    y, core, turn = place[4], place[5], place[6]
    parts = []
    for no in range(tokens):
        c = core if no < NY else 1 - core
        row = lax.rem(y + (turn if no < NY else -turn) * STEPS[no % NY] + NY, NY)
        parts.append(pltpu.make_async_copy(x_pieces[no], xv.at[row, c], xsem.at[no]))
    loads = [pltpu.make_async_copy(pieces[no], wv.at[pl.ds(no // NX * 2, 2), no % NX], wsem.at[no])
             for no in range(count)]
    for copy in parts + loads:
        copy.start()
    for copy in parts:
        copy.wait()

    def multiply(slot, _):
        rows = xv[:, :, replicas_of(place, slot)].reshape(TOK, BLK)
        gv[slot] = lax.dot_general(rows, wv[slot // NX, lax.rem(slot, NX)], (((0,), (0,)), ((), ())),
                                   preferred_element_type=F32)
        return 0

    outs = []
    for part in range(count // NX):
        for copy in loads[part * NX:(part + 1) * NX]:
            copy.wait()
        lax.fori_loop(part * 2 * NX, (part + 1) * 2 * NX, multiply, 0, unroll=2)
        at = pl.ds(part * 2 * NX, 2 * NX)
        outs.append(pltpu.make_async_copy(gv.at[at], g_hbm.at[at], gsem.at[part]))
        outs[-1].start()

    def add(j, total):
        y = jnp.concatenate(
            [gv[:, pl.ds(pl.multiple_of(j * 32 + 8 * h, 8), 8), :].reshape(BLK, BLK) for h in range(4)], axis=1)
        high = y.astype(BF16)
        low = (y - high.astype(F32)).astype(BF16)
        both = jnp.concatenate([high, low], axis=0)
        return total + lax.dot_general(high, both, (((1,), (1,)), ((), ())), preferred_element_type=F32)

    total = lax.fori_loop(0, BLK // 32, add, jnp.zeros((BLK, 2 * BLK), F32))
    cross = total[:, BLK:]
    total = total[:, :BLK] + cross + cross.T
    i = lax.broadcasted_iota(jnp.int32, (BLK, BLK), 0)
    j = lax.broadcasted_iota(jnp.int32, (BLK, BLK), 1)
    total = jnp.where(i % 8 == j % 8, total, 0.0)

    pick_rows = (lax.broadcasted_iota(jnp.int32, (REP, BLK), 0)
                 == replicas_of(place, lax.broadcasted_iota(jnp.int32, (REP, BLK), 1) // 8)).astype(F32)
    pick_cols = (lax.broadcasted_iota(jnp.int32, (BLK, 128), 1) % REP
                 == replicas_of(place, lax.broadcasted_iota(jnp.int32, (BLK, 128), 0) // 8)).astype(F32)
    gram = jnp.dot(jnp.dot(pick_rows, total, preferred_element_type=F32, precision=HIGH), pick_cols,
                   preferred_element_type=F32, precision=HIGH)
    lane = lax.broadcasted_iota(jnp.int32, (8, 128), 1)
    packed = jnp.zeros((8, 128), F32)
    for q in range(REP // 8):
        packed = packed + jnp.where(lane // REP == q, gram[8 * q:8 * q + 8], 0.0)
    mean = jnp.sum(weights_ref[...], axis=(0, 1), keepdims=True) / TOK
    means = jnp.where(lane % REP == place[0] * NZ + place[1], mean, 0.0)
    for copy in range(sums_ref.shape[0]):
        sums_ref[copy, 0:8] = packed
        sums_ref[copy, 8:16] = means
    for out in outs:
        out.wait()


def grads_and_sums(place, x_pieces, pieces, weights):
    any_spec = pl.BlockSpec(memory_space=pl.ANY)
    return pl.pallas_call(
        functools.partial(grads_kernel, len(pieces)),
        out_shape=(jax.ShapeDtypeStruct((REP, BLK, BLK), F32), jax.ShapeDtypeStruct((NX * NY, 16, 128), F32)),
        in_specs=[pl.BlockSpec(memory_space=pltpu.SMEM)] + [any_spec] * (len(x_pieces) + len(pieces))
        + [pl.BlockSpec(memory_space=pltpu.VMEM)],
        out_specs=(any_spec, pl.BlockSpec(memory_space=pltpu.VMEM)),
        scratch_shapes=[
            pltpu.VMEM((NY, NC, REP, TOK // (NY * NC), BLK), BF16),
            pltpu.VMEM((NZ, NX, TOK, BLK), BF16),
            pltpu.VMEM((REP, BLK, BLK), F32),
            pltpu.SemaphoreType.DMA((NY * NC,)),
            pltpu.SemaphoreType.DMA((len(pieces),)),
            pltpu.SemaphoreType.DMA((NX,)),
        ],
        compiler_params=pltpu.CompilerParams(vmem_limit_bytes=58 * 2**20),
        cost_estimate=pl.CostEstimate(flops=6 * 10**9, bytes_accessed=24 * 2**20, transcendentals=0),
    )(place, *x_pieces, *pieces, weights)


def tree_weights(sums):
    lane = lax.broadcasted_iota(jnp.int32, (REP, 128), 1) % REP
    row = lax.broadcasted_iota(jnp.int32, (REP, 128), 0)
    inverse_lanes = float(NY * NC) / sums[8:9]
    inverse_rows = jnp.sum(jnp.where((lax.broadcasted_iota(jnp.int32, (REP, 128), 1) == row),
                                     jnp.broadcast_to(inverse_lanes, (REP, 128)), 0.0), axis=1, keepdims=True)
    wide = lax.broadcasted_iota(jnp.int32, (8, 128), 1)
    table = jnp.concatenate(
        [jnp.where(wide < REP, sums[0:8] if q == 0 else pltpu.roll(sums[0:8], 128 - REP * q, 1), 0.0)
         for q in range(REP // 8)], axis=0)
    table = table + pltpu.roll(table, REP, 1)
    table = table + pltpu.roll(table, 2 * REP, 1)
    table = table * inverse_rows * inverse_lanes
    factor = inverse_rows
    first = lax.broadcasted_iota(jnp.int32, (REP, 128), 1) < REP
    size = REP
    while size > 1:
        half = size // 2
        own = lane == row
        other_rows = lane == (row + half) % REP
        other_lanes = row == (lane + half) % REP
        own_r = jnp.sum(jnp.where(own & first, table, 0.0), axis=1, keepdims=True)
        cross_r = jnp.sum(jnp.where(other_rows & first, table, 0.0), axis=1, keepdims=True)
        own_l = jnp.sum(jnp.where(own, table, 0.0), axis=0, keepdims=True)
        cross_l = jnp.sum(jnp.where(other_lanes, table, 0.0), axis=0, keepdims=True)
        coef_r = 1.0 - cross_r / (2.0 * own_r + EPS_ADA)
        coef_l = 1.0 - cross_l / (2.0 * own_l + EPS_ADA)
        factor = factor * coef_r
        table = table * coef_r * coef_l
        table = table + pltpu.roll(table, half, 0)
        table = table + pltpu.roll(table, half, 1)
        size = half
    return jnp.broadcast_to(factor, (REP, 128))


def update_kernel(place, sums_ref, g_hbm, master_ref, one_ref, two_ref, weights_ref, master_out, one_out, two_out,
                  gv, total, factors, sem):
    group = 4
    copies = [pltpu.make_async_copy(g_hbm.at[pl.ds(r, group)], gv.at[pl.ds(r, group)], sem.at[r])
              for r in range(0, REP, group)]
    for copy in copies:
        copy.start()
    factors[...] = tree_weights(jnp.sum(sums_ref[...], axis=0))

    for no, copy in enumerate(copies):
        scales = []
        for r in range(no * group, (no + 1) * group):
            scale = factors[pl.ds(replica_of(place, r), 1), :]
            scales.append(jnp.concatenate([scale, scale], axis=1))
        copy.wait()

        def strip(s, _):
            at = pl.ds(pl.multiple_of(s * 32, 32), 32)
            part = scales[0] * gv[no * group, at, :]
            for r in range(1, group):
                part = part + scales[r] * gv[no * group + r, at, :]
            total[at, :] = total[at, :] + part if no else part
            return 0

        lax.fori_loop(0, BLK // 32, strip, 0, unroll=2)

    combined = total[...]
    new_one = 0.9 * one_ref[...] + 0.1 * combined
    new_two = 0.95 * two_ref[...] + 0.05 * combined * combined
    first_hat = new_one / (1.0 - 0.9**STEP)
    second_hat = new_two / (1.0 - 0.95**STEP)
    master = master_ref[...]
    updated = master - 0.001 * (first_hat / (jnp.sqrt(second_hat) + 1e-08) + 0.1 * master)
    weights_ref[...] = updated.astype(BF16)
    master_out[...] = updated
    one_out[...] = new_one
    two_out[...] = new_two


def update(place, sums, grads, master, one, two):
    vmem = pl.BlockSpec(memory_space=pltpu.VMEM)
    state = jax.ShapeDtypeStruct((BLK, BLK), F32)
    return pl.pallas_call(
        update_kernel,
        out_shape=(jax.ShapeDtypeStruct((BLK, BLK), BF16), state, state, state),
        in_specs=[pl.BlockSpec(memory_space=pltpu.SMEM), vmem, pl.BlockSpec(memory_space=pl.ANY), vmem, vmem, vmem],
        out_specs=(vmem,) * 4,
        scratch_shapes=[
            pltpu.VMEM((REP, BLK, BLK), F32),
            pltpu.VMEM((BLK, BLK), F32),
            pltpu.VMEM((REP, 128), F32),
            pltpu.SemaphoreType.DMA((REP,)),
        ],
        compiler_params=pltpu.CompilerParams(vmem_limit_bytes=58 * 2**20),
        cost_estimate=pl.CostEstimate(flops=5 * 10**6, bytes_accessed=10 * 2**20, transcendentals=0),
    )(place, sums, grads, master, one, two)


def place_kernel(first, count, place, *refs):
    pieces, out_hbm, held, sem, out_sem = refs[:count], *refs[-4:]
    copies, outs = [], []
    for no in range(count):
        for i in range(2):
            slot = ((first + no) // NX * 2 + i) * NX + no % NX
            at = no * 2 + i
            copies.append(pltpu.make_async_copy(pieces[no].at[i], held.at[at], sem.at[at]))
            outs.append(pltpu.make_async_copy(held.at[at], out_hbm.at[replica_of(place, slot)], out_sem.at[at]))
    for copy in copies:
        copy.start()
    for copy, out in zip(copies, outs):
        copy.wait()
        out.start()
    for out in outs:
        out.wait()


def place_rows(place, pieces, first, out):
    any_spec = pl.BlockSpec(memory_space=pl.ANY)
    count = len(pieces)
    return pl.pallas_call(
        functools.partial(place_kernel, first, count),
        out_shape=jax.ShapeDtypeStruct((REP, BLK, BLK), BF16),
        in_specs=[pl.BlockSpec(memory_space=pltpu.SMEM)] + [any_spec] * (count + len(out)),
        out_specs=any_spec,
        scratch_shapes=[
            pltpu.VMEM((2 * count, BLK, BLK), BF16),
            pltpu.SemaphoreType.DMA((2 * count,)),
            pltpu.SemaphoreType.DMA((2 * count,)),
        ],
        input_output_aliases={1 + count: 0} if out else {},
        compiler_params=pltpu.CompilerParams(vmem_limit_bytes=56 * 2**20),
        cost_estimate=pl.CostEstimate(flops=0, bytes_accessed=2**18 * count, transcendentals=0),
    )(place, *pieces, *out)


def totals_of_groups(sums):
    sums = jnp.sum(lax.all_to_all(sums, ("x", "y"), 0, 0), axis=0)
    return lax.all_to_all(jnp.broadcast_to(sums[None], (NZ * NC,) + sums.shape), ("z", "c"), 0, 0)


def gather_tokens(own):
    ahead, behind = near(own, "y", NY, 1), near(own, "y", NY, -1)
    mine = [own, ahead, behind, near(ahead, "y", NY, -1)]
    return mine + [shift(piece, "c", NC, 1) for piece in mine]


def local(token_rows, advantage, cotangent, master, moment_one, moment_two):
    x, z, y, core = (lax.axis_index(name) for name in ("x", "z", "y", "c"))
    place = jnp.stack([x, z, side(x, core), side(z, core), y, core, side(y, core)]).astype(jnp.int32)
    weights = lax.all_gather(advantage, ("y", "c"), axis=0, tiled=True).astype(F32) * SCALE_FIXED
    weighted = (weights[:, None] * cotangent.astype(F32)).astype(BF16)
    own = lax.all_to_all(token_rows, ("x", "z"), 1, 0, tiled=True).reshape(REP, -1, BLK)
    x_pieces = gather_tokens(own)
    grads, sums = grads_and_sums(place, x_pieces, gather_plane(weighted), weights.reshape(-1, 128))
    sums = totals_of_groups(sums)
    new_weights, new_master, new_one, new_two = update(place, sums, grads, master, moment_one, moment_two)
    pieces = gather_plane(new_weights)
    early = len(pieces) - NX
    out = place_rows(place, pieces[:early], 0, ())
    out = place_rows(place, pieces[early:], early, (out,))
    return (out.reshape(REP * BLK, BLK), new_master, new_one, new_two)


def solution(mesh):
    fine = Mesh(mesh.devices.reshape(NX, NZ, NY, NC), ("x", "z", "y", "c"))
    dp, tensor = ("x", "z"), ("y", "c")
    state = P(dp, tensor)
    return jax.shard_map(
        local,
        mesh=fine,
        in_specs=(P(dp + tensor, None), P(dp + tensor), state, state, state, state),
        out_specs=(P(None, tensor), state, state, state),
        check_vma=False,
    )
```

time: 242 us -> 229 us (0.946)
  waiting for transfers between devices: 110 us -> 100 us
  local copies, waits for them, and re-layouts: 13.5 us -> 7.35 us
  blocking collectives: 32.1 us -> 38 us
    ppermute x10 -> x0, starting transfers between devices: 23.5 us -> none  [send_blocks(): block = lax.ppermute(block, (axis, 'c'), pairs)]
    ppermute x10 -> x0, waiting for transfers between devices: 13.3 us -> none  [send_blocks(): block = lax.ppermute(block, (axis, 'c'), pairs)]
    ppermute x29 -> x35, starting transfers between devices: 22.9 us -> 34.8 us  [near(): return lax.ppermute(array, (axis, 'c'), pairs)]
    all_to_all x0 -> x1, starting transfers between devices: none -> 11.6 us  [local(): lax.all_to_all(token_rows, ('x', 'z'), 1, 0, tiled=True)]
    all_to_all x2, blocking collectives: 22.6 us -> 28.5 us  [the longest x1 14.7 us: totals_of_groups(): sums = jnp.sum(lax.all_to_all(sums, ('x', 'y'), 0, 0), axis=0)]
    ppermute x29 -> x35, waiting for transfers between devices: 94.9 us -> 100 us  [near(): return lax.ppermute(array, (axis, 'c'), pairs)]
    another operation x5 -> x0, local copies, waits for them, and re-layouts: 3.9 us -> none
    unnamed x62 -> x69, local copies, waits for them, and re-layouts: 7.65 us -> 4.32 us
  transfers between devices with their start and end apart: 43 -> 40, of which waited for: 23 -> 24; matrix products, arithmetic and copies ran while one was open for 3% -> 1% of each run, Pallas kernels for 0% -> 2%
where the time goes in v1:
time: 229 us; the launch traced here: 227 us
  waiting for transfers between devices  100 us (44%)
  starting transfers between devices  46.9 us (20%)
  blocking collectives  38 us (17%)
  Pallas kernels  31.3 us (14%)
  local copies, waits for them, and re-layouts  7.35 us (3%)
    ppermute x35, waiting for transfers between devices, near(): return lax.ppermute(array, (axis, 'c'), pairs)  100 us
    ppermute x35, starting transfers between devices, near(): return lax.ppermute(array, (axis, 'c'), pairs)  34.8 us
    pallas_call x1, Pallas kernels, grads_and_sums(): pl.pallas_call(functools.partial(grads_kernel, len(pieces)), out_shape=(j...  18.3 us
    all_to_all x1, blocking collectives, totals_of_groups(): sums = jnp.sum(lax.all_to_all(sums, ('x', 'y'), 0, 0), axis=0)  14.7 us
    all_to_all x1, blocking collectives, totals_of_groups(): lax.all_to_all(jnp.broadcast_to(sums[None], (NZ * NC,) + sums.shape), ('z...  13.8 us
    all_to_all x1, starting transfers between devices, local(): lax.all_to_all(token_rows, ('x', 'z'), 1, 0, tiled=True)  11.6 us
    unnamed x1, blocking collectives  9.48 us
    pallas_call x2, Pallas kernels, place_rows(): pl.pallas_call(functools.partial(place_kernel, first, count), out_shape=j...  6.69 us
  transfers between devices with their start and end apart: 40, of which 24 were waited for; matrix products, arithmetic and copies ran while one was open for 1% of the time, Pallas kernels for 2%

profile of v1, /device:TPU:4, one launch (start us, length us, event | category | flops | bytes accessed | tf_op | source)
XLA Modules:
  0.0 227.2 jit_solution(1583066695991315401)
XLA Ops:
  0.7 2.4 %copy.14 = bf16[8,32,8,256]{3,2,0,1:T(8,128)(2,1)} copy(bf16[8,32,8,256]{3,2,1,0:T(8,128)(2,1)} %bitcast.22) | data formatting | bytes 2097152 | tf_op jit(solution)/shard_map/all_to_all | solution.py:306
  3.0 11.6 %all-to-all-start = ((bf16[64,32,256]{2,0,1:T(8,128)(2,1)}), bf16[64,32,256]{2,0,1:T(8,128)(2,1)S(1)}, u32[]{:S(2)}, u32[]{:S(2)}) async-start(bf16[64,32,256]{2,0,1:T(8,128)(2,1)} %bitcast.20), calls=%async_computation | async-start | bytes 2097152 | tf_op jit(solution)/shard_map/all_to_all | solution.py:306
  14.6 0.6 dynamic-slice
  16.2 9.5 %all-reduce = s32[512]{0:T(512)S(1)} all-reduce(s32[512]{0:T(512)S(1)} %dynamic-update-slice), channel_id=1, replica_groups=mesh['x'=4,'z'=8,'y'=4,'c'=2] {'y','c'}, use_global_device_ids=true, to_apply=%add | all-reduce | flops 512 | bytes 4096
  25.6 0.6 fusion
  26.4 1.6 collective-permute-start.7
  28.0 13.6 %collective-permute-done.7 = bf16[512,256]{1,0:T(8,128)(2,1)S(1)} collective-permute-done((bf16[512,256]{1,0:T(8,128)(2,1)S(1)}, bf16[512,256]{1,0:T(8,128)(2,1)S(1)}, u32[]{:S(2)}, u32[]{:S(2)}) %collective-permute-start.7) | collective-permute-done | bytes 262176 | tf_op jit(solution)/shard_map/ppermute | solution.py:32
  41.7 2.7 %collective-permute-start.11 = (bf16[2,512,256]{2,1,0:T(8,128)(2,1)S(1)}, bf16[2,512,256]{2,1,0:T(8,128)(2,1)S(1)}, u32[]{:S(2)}, u32[]{:S(2)}) collective-permute-start(bf16[2,512,256]{2,1,0:T(8,128)(2,1)S(1)} %pad_maximum_fusion.refs_8_), channel_id=1, source_target_pairs={{0,56},{1,9},{8,16},{9,1},{16,8},{17,25},{24,32},{25,17},{32,24},{... | collective-permute-start | bytes 1572872 | tf_op jit(solution)/shard_map/ppermute | solution.py:32
  44.4 0.5 collective-permute-start.9
  45.0 1.2 collective-permute-start.8
  46.1 1.6 collective-permute-start
  47.7 4.5 %collective-permute-done.11.refs_12_ = bf16[2,512,256]{2,1,0:T(8,128)(2,1)S(1)} collective-permute-done((bf16[2,512,256]{2,1,0:T(8,128)(2,1)S(1)}, bf16[2,512,256]{2,1,0:T(8,128)(2,1)S(1)}, u32[]{:S(2)}, u32[]{:S(2)}) %collective-permute-start.11) | collective-permute-done | bytes 524320 | tf_op jit(solution)/shard_map/ppermute | solution.py:32
  52.2 0.6 collective-permute-start.13
  52.7 6.5 %collective-permute-done.9.refs_10_ = bf16[2,512,256]{2,1,0:T(8,128)(2,1)} collective-permute-done((bf16[2,512,256]{2,1,0:T(8,128)(2,1)S(1)}, bf16[2,512,256]{2,1,0:T(8,128)(2,1)}, u32[]{:S(2)}, u32[]{:S(2)}) %collective-permute-start.9) | collective-permute-done | bytes 524320 | tf_op jit(solution)/shard_map/ppermute | solution.py:32
  59.3 0.9 collective-permute-start.12
  60.2 1.3 collective-permute-start.10
  61.5 2.5 %collective-permute-start.19 = (bf16[2,512,256]{2,1,0:T(8,128)(2,1)S(1)}, bf16[2,512,256]{2,1,0:T(8,128)(2,1)S(1)}, u32[]{:S(2)}, u32[]{:S(2)}) collective-permute-start(bf16[2,512,256]{2,1,0:T(8,128)(2,1)S(1)} %collective-permute-done.15.refs_16_), channel_id=1, source_target_pairs={{0,56},{1,9},{8,16},{9,1},{16,8},{17,25},{24,32},{25,17},{32,24},{... | collective-permute-start | bytes 1572872 | tf_op jit(solution)/shard_map/ppermute | solution.py:32
  64.0 5.1 %collective-permute-done.13.refs_14_ = bf16[2,512,256]{2,1,0:T(8,128)(2,1)S(1)} collective-permute-done((bf16[2,512,256]{2,1,0:T(8,128)(2,1)S(1)}, bf16[2,512,256]{2,1,0:T(8,128)(2,1)S(1)}, u32[]{:S(2)}, u32[]{:S(2)}) %collective-permute-start.13) | collective-permute-done | bytes 524320 | tf_op jit(solution)/shard_map/ppermute | solution.py:32
  69.4 4.7 %collective-permute-done.12.refs_13_ = bf16[2,512,256]{2,1,0:T(8,128)(2,1)S(1)} collective-permute-done((bf16[2,512,256]{2,1,0:T(8,128)(2,1)S(1)}, bf16[2,512,256]{2,1,0:T(8,128)(2,1)S(1)}, u32[]{:S(2)}, u32[]{:S(2)}) %collective-permute-start.12) | collective-permute-done | bytes 524320 | tf_op jit(solution)/shard_map/ppermute | solution.py:32
  74.1 0.9 collective-permute-start.16
  75.0 3.8 %collective-permute-done.10.refs_11_ = bf16[2,512,256]{2,1,0:T(8,128)(2,1)S(1)} collective-permute-done((bf16[2,512,256]{2,1,0:T(8,128)(2,1)}, bf16[2,512,256]{2,1,0:T(8,128)(2,1)S(1)}, u32[]{:S(2)}, u32[]{:S(2)}) %collective-permute-start.10) | collective-permute-done | bytes 524320 | tf_op jit(solution)/shard_map/ppermute | solution.py:32
  78.9 3.0 %collective-permute-start.1 = (bf16[32,64,256]{2,1,0:T(8,128)(2,1)S(1)}, bf16[32,64,256]{2,1,0:T(8,128)(2,1)}, u32[]{:S(2)}, u32[]{:S(2)}) collective-permute-start(bf16[32,64,256]{2,1,0:T(8,128)(2,1)S(1)} %bitcast.24), channel_id=1, source_target_pairs={{0,6},{1,3},{2,4},{3,1},{4,2},{5,7},{6,0},{7,5},{8,14},{9,11},{10,... | collective-permute-start | bytes 3145736 | tf_op jit(solution)/shard_map/ppermute | solution.py:32
  82.4 4.4 %collective-permute-done.17.refs_18_ = bf16[2,512,256]{2,1,0:T(8,128)(2,1)S(1)} collective-permute-done((bf16[2,512,256]{2,1,0:T(8,128)(2,1)S(1)}, bf16[2,512,256]{2,1,0:T(8,128)(2,1)S(1)}, u32[]{:S(2)}, u32[]{:S(2)}) %collective-permute-start.17) | collective-permute-done | bytes 524320 | tf_op jit(solution)/shard_map/ppermute | solution.py:32
  87.1 1.9 collective-permute-done.16.refs_17_
  89.0 0.9 collective-permute-start.20
  89.9 7.3 %collective-permute-done.14.refs_15_ = bf16[2,512,256]{2,1,0:T(8,128)(2,1)S(1)} collective-permute-done((bf16[2,512,256]{2,1,0:T(8,128)(2,1)S(1)}, bf16[2,512,256]{2,1,0:T(8,128)(2,1)S(1)}, u32[]{:S(2)}, u32[]{:S(2)}) %collective-permute-start.14) | collective-permute-done | bytes 524320 | tf_op jit(solution)/shard_map/ppermute | solution.py:32
  97.5 5.3 %collective-permute-done.21.refs_22_ = bf16[2,512,256]{2,1,0:T(8,128)(2,1)S(1)} collective-permute-done((bf16[2,512,256]{2,1,0:T(8,128)(2,1)S(1)}, bf16[2,512,256]{2,1,0:T(8,128)(2,1)S(1)}, u32[]{:S(2)}, u32[]{:S(2)}) %collective-permute-start.21) | collective-permute-done | bytes 524320 | tf_op jit(solution)/shard_map/ppermute | solution.py:32
  102.8 1.2 collective-permute-done.20.refs_21_
  104.0 0.5 collective-permute-start.5
  104.5 1.7 collective-permute-done.2.refs_3_
  106.2 2.2 collective-permute-done.18.refs_19_
  108.5 0.8 copy-done.30
  109.6 0.7 stack.49.place
  110.2 8.6 %collective-permute-done.22.refs_23_ = bf16[2,512,256]{2,1,0:T(8,128)(2,1)} collective-permute-done((bf16[2,512,256]{2,1,0:T(8,128)(2,1)}, bf16[2,512,256]{2,1,0:T(8,128)(2,1)}, u32[]{:S(2)}, u32[]{:S(2)}) %collective-permute-start.22) | collective-permute-done | bytes 524320 | tf_op jit(solution)/shard_map/ppermute | solution.py:32
  118.8 18.3 %shard_map.93 = (f32[32,256,256]{2,1,0:T(8,128)}, f32[16,16,128]{2,1,0:T(8,128)}) custom-call(s32[7]{0:T(128)} %stack.49.place, bf16[32,64,256]{2,1,0:T(8,128)(2,1)} %bitcast.26, bf16[32,64,256]{2,1,0:T(8,128)(2,1)} %copy-done.19, bf16[32,64,256]{2,1,0:T(8,128)(2,1)} %collective-permute-done.1.refs_2_, bf16[32,64,256]{2,1,0:T(8,128)(2,1)} %collective-permute-done.2.refs_3_, ...), custom_call_target="tpu_custom_call" | custom-call | flops 6000000000 | bytes 25165824 | tf_op jit(solution)/shard_map/pallas_call | solution.py:141
  137.2 14.7 %all_to_all.26 = f32[16,16,128]{2,1,0:T(8,128)S(1)} all-to-all(f32[16,16,128]{2,1,0:T(8,128)} %get-tuple-element.10), channel_id=1, replica_groups=mesh['x'=4,'z'=8,'y'=4,'c'=2] {'x','y'}, dimensions={0} | all-to-all | bytes 262144 | tf_op jit(solution)/shard_map/all_to_all | solution.py:291
  151.9 13.8 %all_to_all.27.sums_ref = f32[16,16,128]{2,1,0:T(8,128)} all-to-all(f32[16,16,128]{2,1,0:T(8,128)S(1)} %broadcast_in_dim.2), channel_id=1, replica_groups=mesh['x'=4,'z'=8,'y'=4,'c'=2] {'z','c'}, dimensions={0} | all-to-all | bytes 262144 | tf_op jit(solution)/shard_map/all_to_all | solution.py:292
  165.7 6.3 %shard_map.94 = (bf16[256,256]{1,0:T(8,128)(2,1)}, f32[256,256]{1,0:T(8,128)}, f32[256,256]{1,0:T(8,128)}, f32[256,256]{1,0:T(8,128)}) custom-call(s32[7]{0:T(128)} %stack.49.place, f32[16,16,128]{2,1,0:T(8,128)} %all_to_all.27.sums_ref, f32[32,256,256]{2,1,0:T(8,128)} %get-tuple-element.11.g_hbm, f32[256,256]{1,0:T(8,128)} %master_ref.1, ...), custom_call_target="tpu_custom_call" | custom-call | flops 5000000 | bytes 10485760 | tf_op jit(solution)/shard_map/pallas_call | solution.py:237
  172.0 0.6 collective-permute-start.23
  172.6 4.6 %collective-permute-done.23 = bf16[256,256]{1,0:T(8,128)(2,1)S(1)} collective-permute-done((bf16[256,256]{1,0:T(8,128)(2,1)}, bf16[256,256]{1,0:T(8,128)(2,1)S(1)}, u32[]{:S(2)}, u32[]{:S(2)}) %collective-permute-start.23) | collective-permute-done | bytes 131104 | tf_op jit(solution)/shard_map/ppermute | solution.py:32
  177.2 0.9 pad_maximum_fusion.1.refs_0_
  178.4 7.4 %collective-permute-done.24.refs_4_ = bf16[2,256,256]{2,1,0:T(8,128)(2,1)S(1)} collective-permute-done((bf16[2,256,256]{2,1,0:T(8,128)(2,1)S(1)}, bf16[2,256,256]{2,1,0:T(8,128)(2,1)S(1)}, u32[]{:S(2)}, u32[]{:S(2)}) %collective-permute-start.24) | collective-permute-done | bytes 262176 | tf_op jit(solution)/shard_map/ppermute | solution.py:32
  185.9 1.4 collective-permute-start.30
  187.2 1.5 collective-permute-start.31
  188.7 3.5 %collective-permute-done.25.refs_8_ = bf16[2,256,256]{2,1,0:T(8,128)(2,1)S(1)} collective-permute-done((bf16[2,256,256]{2,1,0:T(8,128)(2,1)S(1)}, bf16[2,256,256]{2,1,0:T(8,128)(2,1)S(1)}, u32[]{:S(2)}, u32[]{:S(2)}) %collective-permute-start.25) | collective-permute-done | bytes 262176 | tf_op jit(solution)/shard_map/ppermute | solution.py:32
  192.4 2.4 %collective-permute-done.30.refs_1_ = bf16[2,256,256]{2,1,0:T(8,128)(2,1)S(1)} collective-permute-done((bf16[2,256,256]{2,1,0:T(8,128)(2,1)S(1)}, bf16[2,256,256]{2,1,0:T(8,128)(2,1)S(1)}, u32[]{:S(2)}, u32[]{:S(2)}) %collective-permute-start.30) | collective-permute-done | bytes 262176 | tf_op jit(solution)/shard_map/ppermute | solution.py:32
  194.9 2.3 %collective-permute-start.33 = (bf16[2,256,256]{2,1,0:T(8,128)(2,1)S(1)}, bf16[2,256,256]{2,1,0:T(8,128)(2,1)S(1)}, u32[]{:S(2)}, u32[]{:S(2)}) collective-permute-start(bf16[2,256,256]{2,1,0:T(8,128)(2,1)S(1)} %collective-permute-done.24.refs_4_), channel_id=1, source_target_pairs={{0,64},{1,193},{64,0},{65,129},{128,192},{129,65},{192,128},{193,1... | collective-permute-start | bytes 786440 | tf_op jit(solution)/shard_map/ppermute | solution.py:32
  197.3 1.8 collective-permute-start.34
  199.0 0.8 collective-permute-done.26.refs_0_
  199.8 1.8 collective-permute-start.27
  201.6 2.4 %collective-permute-done.32.refs_3_ = bf16[2,256,256]{2,1,0:T(8,128)(2,1)S(1)} collective-permute-done((bf16[2,256,256]{2,1,0:T(8,128)(2,1)S(1)}, bf16[2,256,256]{2,1,0:T(8,128)(2,1)S(1)}, u32[]{:S(2)}, u32[]{:S(2)}) %collective-permute-start.32) | collective-permute-done | bytes 262176 | tf_op jit(solution)/shard_map/ppermute | solution.py:32
  204.1 0.3 collective-permute-done.33.refs_5_
  204.5 1.7 collective-permute-start.35
  206.2 3.9 %collective-permute-done.36.refs_9_ = bf16[2,256,256]{2,1,0:T(8,128)(2,1)S(1)} collective-permute-done((bf16[2,256,256]{2,1,0:T(8,128)(2,1)S(1)}, bf16[2,256,256]{2,1,0:T(8,128)(2,1)S(1)}, u32[]{:S(2)}, u32[]{:S(2)}) %collective-permute-start.36) | collective-permute-done | bytes 262176 | tf_op jit(solution)/shard_map/ppermute | solution.py:32
  210.1 1.7 collective-permute-start.38
  211.8 0.3 collective-permute-start.28
  212.1 3.6 %collective-permute-done.27.refs_1_ = bf16[2,256,256]{2,1,0:T(8,128)(2,1)S(1)} collective-permute-done((bf16[2,256,256]{2,1,0:T(8,128)(2,1)S(1)}, bf16[2,256,256]{2,1,0:T(8,128)(2,1)S(1)}, u32[]{:S(2)}, u32[]{:S(2)}) %collective-permute-start.27) | collective-permute-done | bytes 262176 | tf_op jit(solution)/shard_map/ppermute | solution.py:32
  215.7 1.7 collective-permute-start.29
  217.5 0.6 copy-done.17
  218.2 0.7 copy-done.18
  218.9 3.9 %shard_map.95.refs_4_ = bf16[32,256,256]{2,1,0:T(8,128)(2,1)} custom-call(s32[7]{0:T(128)} %stack.49.place, bf16[2,256,256]{2,1,0:T(8,128)(2,1)} %copy-done.2, bf16[2,256,256]{2,1,0:T(8,128)(2,1)} %copy-done.10, bf16[2,256,256]{2,1,0:T(8,128)(2,1)} %copy-done.11, bf16[2,256,256]{2,1,0:T(8,128)(2,1)} %copy-done.12, bf16[2,256,256]{2,1,0:T(8,128)(2,1)} %copy-done.8, ...), custom_call_target="tpu_custom_call" | custom-call | bytes 3145728 | tf_op jit(solution)/shard_map/pallas_call | solution.py:274
  223.0 0.5 copy-done.6
  223.6 0.7 copy-done.7
  224.3 2.8 %shard_map.96 = bf16[32,256,256]{2,1,0:T(8,128)(2,1)} custom-call(s32[7]{0:T(128)} %stack.49.place, bf16[2,256,256]{2,1,0:T(8,128)(2,1)} %copy-done.4, bf16[2,256,256]{2,1,0:T(8,128)(2,1)} %copy-done.5, bf16[2,256,256]{2,1,0:T(8,128)(2,1)} %copy-done.6, bf16[2,256,256]{2,1,0:T(8,128)(2,1)} %copy-done.7, ...), custom_call_target="tpu_custom_call", output_to_operand_aliasing={{}: (5, {})} | custom-call | bytes 1048576 | tf_op jit(solution)/shard_map/pallas_call | solution.py:274
  (101 shorter events, 3.4 us)
Async XLA Ops:
  0.6 14.0 %copy-start.32 = (u32[256]{0:T(256)S(1)}, u32[256]{0:T(256)}, u32[]{:S(2)}) copy-start(u32[256]{0:T(256)} %constant.46) | copy-start | bytes 3076
  0.6 15.3 %copy-start.31 = (s32[64]{0:T(128)S(1)}, s32[64]{0:T(128)}, u32[]{:S(2)}) copy-start(s32[64]{0:T(128)} %param.7) | copy-start | bytes 772
  0.7 25.6 %copy-start.1 = (bf16[512,256]{1,0:T(8,128)(2,1)S(1)}, bf16[512,256]{1,0:T(8,128)(2,1)}, u32[]{:S(2)}) copy-start(bf16[512,256]{1,0:T(8,128)(2,1)} %param.8) | copy-start | bytes 786436
  3.0 43.1 %all-to-all-start = ((bf16[64,32,256]{2,0,1:T(8,128)(2,1)}), bf16[64,32,256]{2,0,1:T(8,128)(2,1)S(1)}, u32[]{:S(2)}, u32[]{:S(2)}) async-start(bf16[64,32,256]{2,0,1:T(8,128)(2,1)} %bitcast.20), calls=%async_computation | async-start | bytes 2097152 | tf_op jit(solution)/shard_map/all_to_all | solution.py:306
  26.4 15.3 %collective-permute-start.7 = (bf16[512,256]{1,0:T(8,128)(2,1)S(1)}, bf16[512,256]{1,0:T(8,128)(2,1)S(1)}, u32[]{:S(2)}, u32[]{:S(2)}) collective-permute-start(bf16[512,256]{1,0:T(8,128)(2,1)S(1)} %multiply_convert_fusion), channel_id=1, source_target_pairs={{0,8},{1,57},{8,0},{9,17},{16,24},{17,9},{24,16},{25,33},{32,40},{... | collective-permute-start | bytes 786440 | tf_op jit(solution)/shard_map/ppermute | solution.py:32
  41.7 77.1 %copy-start.3 = (bf16[2,512,256]{2,1,0:T(8,128)(2,1)}, bf16[2,512,256]{2,1,0:T(8,128)(2,1)S(1)}, u32[]{:S(2)}) copy-start(bf16[2,512,256]{2,1,0:T(8,128)(2,1)S(1)} %pad_maximum_fusion.refs_8_) | copy-start | bytes 1572868
  41.7 10.5 %collective-permute-start.11 = (bf16[2,512,256]{2,1,0:T(8,128)(2,1)S(1)}, bf16[2,512,256]{2,1,0:T(8,128)(2,1)S(1)}, u32[]{:S(2)}, u32[]{:S(2)}) collective-permute-start(bf16[2,512,256]{2,1,0:T(8,128)(2,1)S(1)} %pad_maximum_fusion.refs_8_), channel_id=1, source_target_pairs={{0,56},{1,9},{8,16},{9,1},{16,8},{17,25},{24,32},{25,17},{32,24},{... | collective-permute-start | bytes 1572872 | tf_op jit(solution)/shard_map/ppermute | solution.py:32
  44.4 14.8 %collective-permute-start.9 = (bf16[2,512,256]{2,1,0:T(8,128)(2,1)S(1)}, bf16[2,512,256]{2,1,0:T(8,128)(2,1)}, u32[]{:S(2)}, u32[]{:S(2)}) collective-permute-start(bf16[2,512,256]{2,1,0:T(8,128)(2,1)S(1)} %pad_maximum_fusion.refs_8_), channel_id=1, source_target_pairs={{0,192},{1,65},{64,128},{65,1},{128,64},{129,193},{192,0},{193,129... | collective-permute-start | bytes 1572872 | tf_op jit(solution)/shard_map/ppermute | solution.py:32
  45.0 15.2 %collective-permute-start.8 = (bf16[2,512,256]{2,1,0:T(8,128)(2,1)S(1)}, bf16[2,512,256]{2,1,0:T(8,128)(2,1)}, u32[]{:S(2)}, u32[]{:S(2)}) collective-permute-start(bf16[2,512,256]{2,1,0:T(8,128)(2,1)S(1)} %pad_maximum_fusion.refs_8_), channel_id=1, source_target_pairs={{0,64},{1,193},{64,0},{65,129},{128,192},{129,65},{192,128},{193,1... | collective-permute-start | bytes 1572872 | tf_op jit(solution)/shard_map/ppermute | solution.py:32
  46.1 72.7 %copy-start = (bf16[64,32,256]{2,0,1:T(8,128)(2,1)}, bf16[64,32,256]{2,0,1:T(8,128)(2,1)S(1)}, u32[]{:S(2)}) copy-start(bf16[64,32,256]{2,0,1:T(8,128)(2,1)S(1)} %all-to-all-done) | copy-start | bytes 3145732
  46.1 35.7 %collective-permute-start = (bf16[32,64,256]{2,1,0:T(8,128)(2,1)S(1)}, bf16[32,64,256]{2,1,0:T(8,128)(2,1)S(1)}, u32[]{:S(2)}, u32[]{:S(2)}) collective-permute-start(bf16[32,64,256]{2,1,0:T(8,128)(2,1)S(1)} %bitcast.23), channel_id=1, source_target_pairs={{0,2},{1,7},{2,0},{3,5},{4,6},{5,3},{6,4},{7,1},{8,10},{9,15},{10,... | collective-permute-start | bytes 3145736 | tf_op jit(solution)/shard_map/ppermute | solution.py:32
  52.2 66.6 %copy-start.20 = (bf16[2,512,256]{2,1,0:T(8,128)(2,1)}, bf16[2,512,256]{2,1,0:T(8,128)(2,1)S(1)}, u32[]{:S(2)}) copy-start(bf16[2,512,256]{2,1,0:T(8,128)(2,1)S(1)} %collective-permute-done.11.refs_12_) | copy-start | bytes 1572868
  52.2 9.3 %collective-permute-start.15 = (bf16[2,512,256]{2,1,0:T(8,128)(2,1)S(1)}, bf16[2,512,256]{2,1,0:T(8,128)(2,1)S(1)}, u32[]{:S(2)}, u32[]{:S(2)}) collective-permute-start(bf16[2,512,256]{2,1,0:T(8,128)(2,1)S(1)} %collective-permute-done.11.refs_12_), channel_id=1, source_target_pairs={{0,8},{1,57},{8,0},{9,17},{16,24},{17,9},{24,16},{25,33},{32,40},{... | collective-permute-start | bytes 1572872 | tf_op jit(solution)/shard_map/ppermute | solution.py:32
  52.2 16.9 %collective-permute-start.13 = (bf16[2,512,256]{2,1,0:T(8,128)(2,1)S(1)}, bf16[2,512,256]{2,1,0:T(8,128)(2,1)S(1)}, u32[]{:S(2)}, u32[]{:S(2)}) collective-permute-start(bf16[2,512,256]{2,1,0:T(8,128)(2,1)S(1)} %collective-permute-done.11.refs_12_), channel_id=1, source_target_pairs={{0,192},{1,65},{64,128},{65,1},{128,64},{129,193},{192,0},{193,129... | collective-permute-start | bytes 1572872 | tf_op jit(solution)/shard_map/ppermute | solution.py:32
  59.3 14.9 %collective-permute-start.12 = (bf16[2,512,256]{2,1,0:T(8,128)(2,1)S(1)}, bf16[2,512,256]{2,1,0:T(8,128)(2,1)S(1)}, u32[]{:S(2)}, u32[]{:S(2)}) collective-permute-start(bf16[2,512,256]{2,1,0:T(8,128)(2,1)S(1)} %collective-permute-done.11.refs_12_), channel_id=1, source_target_pairs={{0,64},{1,193},{64,0},{65,129},{128,192},{129,65},{192,128},{193,1... | collective-permute-start | bytes 1572872 | tf_op jit(solution)/shard_map/ppermute | solution.py:32
  60.2 18.7 %collective-permute-start.10 = (bf16[2,512,256]{2,1,0:T(8,128)(2,1)}, bf16[2,512,256]{2,1,0:T(8,128)(2,1)S(1)}, u32[]{:S(2)}, u32[]{:S(2)}) collective-permute-start(bf16[2,512,256]{2,1,0:T(8,128)(2,1)} %collective-permute-done.8.refs_9_), channel_id=1, source_target_pairs={{0,192},{1,65},{64,128},{65,1},{128,64},{129,193},{192,0},{193,129... | collective-permute-start | bytes 1572872 | tf_op jit(solution)/shard_map/ppermute | solution.py:32
  61.5 44.7 %copy-start.21 = (bf16[2,512,256]{2,1,0:T(8,128)(2,1)}, bf16[2,512,256]{2,1,0:T(8,128)(2,1)S(1)}, u32[]{:S(2)}) copy-start(bf16[2,512,256]{2,1,0:T(8,128)(2,1)S(1)} %collective-permute-done.15.refs_16_) | copy-start | bytes 1572868
  61.5 20.6 %collective-permute-start.19 = (bf16[2,512,256]{2,1,0:T(8,128)(2,1)S(1)}, bf16[2,512,256]{2,1,0:T(8,128)(2,1)S(1)}, u32[]{:S(2)}, u32[]{:S(2)}) collective-permute-start(bf16[2,512,256]{2,1,0:T(8,128)(2,1)S(1)} %collective-permute-done.15.refs_16_), channel_id=1, source_target_pairs={{0,56},{1,9},{8,16},{9,1},{16,8},{17,25},{24,32},{25,17},{32,24},{... | collective-permute-start | bytes 1572872 | tf_op jit(solution)/shard_map/ppermute | solution.py:32
  69.1 37.1 %copy-start.22 = (bf16[2,512,256]{2,1,0:T(8,128)(2,1)}, bf16[2,512,256]{2,1,0:T(8,128)(2,1)S(1)}, u32[]{:S(2)}) copy-start(bf16[2,512,256]{2,1,0:T(8,128)(2,1)S(1)} %collective-permute-done.13.refs_14_) | copy-start | bytes 1572868
  69.1 17.7 %collective-permute-start.17 = (bf16[2,512,256]{2,1,0:T(8,128)(2,1)S(1)}, bf16[2,512,256]{2,1,0:T(8,128)(2,1)S(1)}, u32[]{:S(2)}, u32[]{:S(2)}) collective-permute-start(bf16[2,512,256]{2,1,0:T(8,128)(2,1)S(1)} %collective-permute-done.15.refs_16_), channel_id=1, source_target_pairs={{0,192},{1,65},{64,128},{65,1},{128,64},{129,193},{192,0},{193,129... | collective-permute-start | bytes 1572872 | tf_op jit(solution)/shard_map/ppermute | solution.py:32
  74.1 34.3 %copy-start.23 = (bf16[2,512,256]{2,1,0:T(8,128)(2,1)}, bf16[2,512,256]{2,1,0:T(8,128)(2,1)S(1)}, u32[]{:S(2)}) copy-start(bf16[2,512,256]{2,1,0:T(8,128)(2,1)S(1)} %collective-permute-done.12.refs_13_) | copy-start | bytes 1572868
  74.1 14.9 %collective-permute-start.16 = (bf16[2,512,256]{2,1,0:T(8,128)(2,1)S(1)}, bf16[2,512,256]{2,1,0:T(8,128)(2,1)S(1)}, u32[]{:S(2)}, u32[]{:S(2)}) collective-permute-start(bf16[2,512,256]{2,1,0:T(8,128)(2,1)S(1)} %collective-permute-done.15.refs_16_), channel_id=1, source_target_pairs={{0,64},{1,193},{64,0},{65,129},{128,192},{129,65},{192,128},{193,1... | collective-permute-start | bytes 1572872 | tf_op jit(solution)/shard_map/ppermute | solution.py:32
  78.9 29.6 %copy-start.24 = (bf16[2,512,256]{2,1,0:T(8,128)(2,1)}, bf16[2,512,256]{2,1,0:T(8,128)(2,1)S(1)}, u32[]{:S(2)}) copy-start(bf16[2,512,256]{2,1,0:T(8,128)(2,1)S(1)} %collective-permute-done.10.refs_11_) | copy-start | bytes 1572868
  78.9 25.1 %collective-permute-start.1 = (bf16[32,64,256]{2,1,0:T(8,128)(2,1)S(1)}, bf16[32,64,256]{2,1,0:T(8,128)(2,1)}, u32[]{:S(2)}, u32[]{:S(2)}) collective-permute-start(bf16[32,64,256]{2,1,0:T(8,128)(2,1)S(1)} %bitcast.24), channel_id=1, source_target_pairs={{0,6},{1,3},{2,4},{3,1},{4,2},{5,7},{6,0},{7,5},{8,14},{9,11},{10,... | collective-permute-start | bytes 3145736 | tf_op jit(solution)/shard_map/ppermute | solution.py:32
  81.9 36.9 %copy-start.19 = (bf16[32,64,256]{2,1,0:T(8,128)(2,1)}, bf16[32,64,256]{2,1,0:T(8,128)(2,1)S(1)}, u32[]{:S(2)}) copy-start(bf16[32,64,256]{2,1,0:T(8,128)(2,1)S(1)} %collective-permute-done.refs_1_) | copy-start | bytes 3145732
  81.9 24.3 %collective-permute-start.2 = (bf16[32,64,256]{2,1,0:T(8,128)(2,1)S(1)}, bf16[32,64,256]{2,1,0:T(8,128)(2,1)}, u32[]{:S(2)}, u32[]{:S(2)}) collective-permute-start(bf16[32,64,256]{2,1,0:T(8,128)(2,1)S(1)} %collective-permute-done.refs_1_), channel_id=1, source_target_pairs={{0,6},{1,3},{2,4},{3,1},{4,2},{5,7},{6,0},{7,5},{8,14},{9,11},{10,... | collective-permute-start | bytes 3145736 | tf_op jit(solution)/shard_map/ppermute | solution.py:32
  82.1 26.3 %copy-start.25 = (bf16[2,512,256]{2,1,0:T(8,128)(2,1)}, bf16[2,512,256]{2,1,0:T(8,128)(2,1)S(1)}, u32[]{:S(2)}) copy-start(bf16[2,512,256]{2,1,0:T(8,128)(2,1)S(1)} %collective-permute-done.19.refs_20_) | copy-start | bytes 1572868
  82.1 15.1 %collective-permute-start.14 = (bf16[2,512,256]{2,1,0:T(8,128)(2,1)S(1)}, bf16[2,512,256]{2,1,0:T(8,128)(2,1)S(1)}, u32[]{:S(2)}, u32[]{:S(2)}) collective-permute-start(bf16[2,512,256]{2,1,0:T(8,128)(2,1)S(1)} %collective-permute-done.12.refs_13_), channel_id=1, source_target_pairs={{0,192},{1,65},{64,128},{65,1},{128,64},{129,193},{192,0},{193,129... | collective-permute-start | bytes 1572872 | tf_op jit(solution)/shard_map/ppermute | solution.py:32
  86.8 21.6 %copy-start.26 = (bf16[2,512,256]{2,1,0:T(8,128)(2,1)}, bf16[2,512,256]{2,1,0:T(8,128)(2,1)S(1)}, u32[]{:S(2)}) copy-start(bf16[2,512,256]{2,1,0:T(8,128)(2,1)S(1)} %collective-permute-done.17.refs_18_) | copy-start | bytes 1572868
  86.8 16.0 %collective-permute-start.21 = (bf16[2,512,256]{2,1,0:T(8,128)(2,1)S(1)}, bf16[2,512,256]{2,1,0:T(8,128)(2,1)S(1)}, u32[]{:S(2)}, u32[]{:S(2)}) collective-permute-start(bf16[2,512,256]{2,1,0:T(8,128)(2,1)S(1)} %collective-permute-done.19.refs_20_), channel_id=1, source_target_pairs={{0,192},{1,65},{64,128},{65,1},{128,64},{129,193},{192,0},{193,129... | collective-permute-start | bytes 1572872 | tf_op jit(solution)/shard_map/ppermute | solution.py:32
  89.0 19.4 %copy-start.27 = (bf16[2,512,256]{2,1,0:T(8,128)(2,1)}, bf16[2,512,256]{2,1,0:T(8,128)(2,1)S(1)}, u32[]{:S(2)}) copy-start(bf16[2,512,256]{2,1,0:T(8,128)(2,1)S(1)} %collective-permute-done.16.refs_17_) | copy-start | bytes 1572868
  89.0 15.0 %collective-permute-start.20 = (bf16[2,512,256]{2,1,0:T(8,128)(2,1)S(1)}, bf16[2,512,256]{2,1,0:T(8,128)(2,1)}, u32[]{:S(2)}, u32[]{:S(2)}) collective-permute-start(bf16[2,512,256]{2,1,0:T(8,128)(2,1)S(1)} %collective-permute-done.19.refs_20_), channel_id=1, source_target_pairs={{0,64},{1,193},{64,0},{65,129},{128,192},{129,65},{192,128},{193,1... | collective-permute-start | bytes 1572872 | tf_op jit(solution)/shard_map/ppermute | solution.py:32
  97.2 11.3 %copy-start.28 = (bf16[2,512,256]{2,1,0:T(8,128)(2,1)}, bf16[2,512,256]{2,1,0:T(8,128)(2,1)S(1)}, u32[]{:S(2)}) copy-start(bf16[2,512,256]{2,1,0:T(8,128)(2,1)S(1)} %collective-permute-done.14.refs_15_) | copy-start | bytes 1572868
  97.2 11.2 %collective-permute-start.18 = (bf16[2,512,256]{2,1,0:T(8,128)(2,1)S(1)}, bf16[2,512,256]{2,1,0:T(8,128)(2,1)S(1)}, u32[]{:S(2)}, u32[]{:S(2)}) collective-permute-start(bf16[2,512,256]{2,1,0:T(8,128)(2,1)S(1)} %collective-permute-done.16.refs_17_), channel_id=1, source_target_pairs={{0,192},{1,65},{64,128},{65,1},{128,64},{129,193},{192,0},{193,129... | collective-permute-start | bytes 1572872 | tf_op jit(solution)/shard_map/ppermute | solution.py:32
  102.8 16.0 %collective-permute-start.3 = (bf16[32,64,256]{2,1,0:T(8,128)(2,1)S(1)}, bf16[32,64,256]{2,1,0:T(8,128)(2,1)}, u32[]{:S(2)}, u32[]{:S(2)}) collective-permute-start(bf16[32,64,256]{2,1,0:T(8,128)(2,1)S(1)} %bitcast.25), channel_id=1, source_target_pairs={{0,1},{1,0},{2,3},{3,2},{4,5},{5,4},{6,7},{7,6},{8,9},{9,8},{10,11... | collective-permute-start | bytes 3145736 | tf_op jit(solution)/shard_map/ppermute | solution.py:23
  104.0 14.8 %collective-permute-start.4 = (bf16[32,64,256]{2,1,0:T(8,128)(2,1)S(1)}, bf16[32,64,256]{2,1,0:T(8,128)(2,1)}, u32[]{:S(2)}, u32[]{:S(2)}) collective-permute-start(bf16[32,64,256]{2,1,0:T(8,128)(2,1)S(1)} %collective-permute-done.refs_1_), channel_id=1, source_target_pairs={{0,1},{1,0},{2,3},{3,2},{4,5},{5,4},{6,7},{7,6},{8,9},{9,8},{10,11... | collective-permute-start | bytes 3145736 | tf_op jit(solution)/shard_map/ppermute | solution.py:23
  104.0 14.8 %collective-permute-start.5 = (bf16[32,64,256]{2,1,0:T(8,128)(2,1)}, bf16[32,64,256]{2,1,0:T(8,128)(2,1)}, u32[]{:S(2)}, u32[]{:S(2)}) collective-permute-start(bf16[32,64,256]{2,1,0:T(8,128)(2,1)} %collective-permute-done.1.refs_2_), channel_id=1, source_target_pairs={{0,1},{1,0},{2,3},{3,2},{4,5},{5,4},{6,7},{7,6},{8,9},{9,8},{10,11... | collective-permute-start | bytes 3145736 | tf_op jit(solution)/shard_map/ppermute | solution.py:23
  106.2 12.6 %collective-permute-start.6 = (bf16[32,64,256]{2,1,0:T(8,128)(2,1)}, bf16[32,64,256]{2,1,0:T(8,128)(2,1)}, u32[]{:S(2)}, u32[]{:S(2)}) collective-permute-start(bf16[32,64,256]{2,1,0:T(8,128)(2,1)} %collective-permute-done.2.refs_3_), channel_id=1, source_target_pairs={{0,1},{1,0},{2,3},{3,2},{4,5},{5,4},{6,7},{7,6},{8,9},{9,8},{10,11... | collective-permute-start | bytes 3145736 | tf_op jit(solution)/shard_map/ppermute | solution.py:23
  109.3 9.5 %collective-permute-start.22 = (bf16[2,512,256]{2,1,0:T(8,128)(2,1)}, bf16[2,512,256]{2,1,0:T(8,128)(2,1)}, u32[]{:S(2)}, u32[]{:S(2)}) collective-permute-start(bf16[2,512,256]{2,1,0:T(8,128)(2,1)} %collective-permute-done.20.refs_21_), channel_id=1, source_target_pairs={{0,192},{1,65},{64,128},{65,1},{128,64},{129,193},{192,0},{193,129... | collective-permute-start | bytes 1572872 | tf_op jit(solution)/shard_map/ppermute | solution.py:32
  172.0 5.3 %collective-permute-start.23 = (bf16[256,256]{1,0:T(8,128)(2,1)}, bf16[256,256]{1,0:T(8,128)(2,1)S(1)}, u32[]{:S(2)}, u32[]{:S(2)}) collective-permute-start(bf16[256,256]{1,0:T(8,128)(2,1)} %get-tuple-element.12), channel_id=1, source_target_pairs={{0,8},{1,57},{8,0},{9,17},{16,24},{17,9},{24,16},{25,33},{32,40},{... | collective-permute-start | bytes 393224 | tf_op jit(solution)/shard_map/ppermute | solution.py:32
  178.2 39.3 %copy-start.2 = (bf16[2,256,256]{2,1,0:T(8,128)(2,1)}, bf16[2,256,256]{2,1,0:T(8,128)(2,1)S(1)}, u32[]{:S(2)}) copy-start(bf16[2,256,256]{2,1,0:T(8,128)(2,1)S(1)} %pad_maximum_fusion.1.refs_0_) | copy-start | bytes 786436
  178.2 7.7 %collective-permute-start.24 = (bf16[2,256,256]{2,1,0:T(8,128)(2,1)S(1)}, bf16[2,256,256]{2,1,0:T(8,128)(2,1)S(1)}, u32[]{:S(2)}, u32[]{:S(2)}) collective-permute-start(bf16[2,256,256]{2,1,0:T(8,128)(2,1)S(1)} %pad_maximum_fusion.1.refs_0_), channel_id=1, source_target_pairs={{0,56},{1,9},{8,16},{9,1},{16,8},{17,25},{24,32},{25,17},{32,24},{... | collective-permute-start | bytes 786440 | tf_op jit(solution)/shard_map/ppermute | solution.py:32
  185.8 31.6 %copy-start.8 = (bf16[2,256,256]{2,1,0:T(8,128)(2,1)}, bf16[2,256,256]{2,1,0:T(8,128)(2,1)S(1)}, u32[]{:S(2)}) copy-start(bf16[2,256,256]{2,1,0:T(8,128)(2,1)S(1)} %collective-permute-done.24.refs_4_) | copy-start | bytes 786436
  185.9 6.4 %collective-permute-start.25 = (bf16[2,256,256]{2,1,0:T(8,128)(2,1)S(1)}, bf16[2,256,256]{2,1,0:T(8,128)(2,1)S(1)}, u32[]{:S(2)}, u32[]{:S(2)}) collective-permute-start(bf16[2,256,256]{2,1,0:T(8,128)(2,1)S(1)} %collective-permute-done.24.refs_4_), channel_id=1, source_target_pairs={{0,8},{1,57},{8,0},{9,17},{16,24},{17,9},{24,16},{25,33},{32,40},{... | collective-permute-start | bytes 786440 | tf_op jit(solution)/shard_map/ppermute | solution.py:32
  185.9 8.9 %collective-permute-start.30 = (bf16[2,256,256]{2,1,0:T(8,128)(2,1)S(1)}, bf16[2,256,256]{2,1,0:T(8,128)(2,1)S(1)}, u32[]{:S(2)}, u32[]{:S(2)}) collective-permute-start(bf16[2,256,256]{2,1,0:T(8,128)(2,1)S(1)} %pad_maximum_fusion.1.refs_0_), channel_id=1, source_target_pairs={{0,64},{1,193},{64,0},{65,129},{128,192},{129,65},{192,128},{193,1... | collective-permute-start | bytes 786440 | tf_op jit(solution)/shard_map/ppermute | solution.py:32
  187.2 10.0 %collective-permute-start.31 = (bf16[2,256,256]{2,1,0:T(8,128)(2,1)S(1)}, bf16[2,256,256]{2,1,0:T(8,128)(2,1)S(1)}, u32[]{:S(2)}, u32[]{:S(2)}) collective-permute-start(bf16[2,256,256]{2,1,0:T(8,128)(2,1)S(1)} %pad_maximum_fusion.1.refs_0_), channel_id=1, source_target_pairs={{0,192},{1,65},{64,128},{65,1},{128,64},{129,193},{192,0},{193,129... | collective-permute-start | bytes 786440 | tf_op jit(solution)/shard_map/ppermute | solution.py:32
  192.2 25.2 %copy-start.9 = (bf16[2,256,256]{2,1,0:T(8,128)(2,1)}, bf16[2,256,256]{2,1,0:T(8,128)(2,1)S(1)}, u32[]{:S(2)}) copy-start(bf16[2,256,256]{2,1,0:T(8,128)(2,1)S(1)} %collective-permute-done.25.refs_8_) | copy-start | bytes 786436
  192.2 7.6 %collective-permute-start.26 = (bf16[2,256,256]{2,1,0:T(8,128)(2,1)S(1)}, bf16[2,256,256]{2,1,0:T(8,128)(2,1)S(1)}, u32[]{:S(2)}, u32[]{:S(2)}) collective-permute-start(bf16[2,256,256]{2,1,0:T(8,128)(2,1)S(1)} %collective-permute-done.25.refs_8_), channel_id=1, source_target_pairs={{0,56},{1,9},{8,16},{9,1},{16,8},{17,25},{24,32},{25,17},{32,24},{... | collective-permute-start | bytes 786440 | tf_op jit(solution)/shard_map/ppermute | solution.py:32
  194.7 22.7 %copy-start.10 = (bf16[2,256,256]{2,1,0:T(8,128)(2,1)}, bf16[2,256,256]{2,1,0:T(8,128)(2,1)S(1)}, u32[]{:S(2)}) copy-start(bf16[2,256,256]{2,1,0:T(8,128)(2,1)S(1)} %collective-permute-done.30.refs_1_) | copy-start | bytes 786436
  194.7 9.2 %collective-permute-start.32 = (bf16[2,256,256]{2,1,0:T(8,128)(2,1)S(1)}, bf16[2,256,256]{2,1,0:T(8,128)(2,1)S(1)}, u32[]{:S(2)}, u32[]{:S(2)}) collective-permute-start(bf16[2,256,256]{2,1,0:T(8,128)(2,1)S(1)} %collective-permute-done.30.refs_1_), channel_id=1, source_target_pairs={{0,192},{1,65},{64,128},{65,1},{128,64},{129,193},{192,0},{193,129... | collective-permute-start | bytes 786440 | tf_op jit(solution)/shard_map/ppermute | solution.py:32
  194.9 9.6 %collective-permute-start.33 = (bf16[2,256,256]{2,1,0:T(8,128)(2,1)S(1)}, bf16[2,256,256]{2,1,0:T(8,128)(2,1)S(1)}, u32[]{:S(2)}, u32[]{:S(2)}) collective-permute-start(bf16[2,256,256]{2,1,0:T(8,128)(2,1)S(1)} %collective-permute-done.24.refs_4_), channel_id=1, source_target_pairs={{0,64},{1,193},{64,0},{65,129},{128,192},{129,65},{192,128},{193,1... | collective-permute-start | bytes 786440 | tf_op jit(solution)/shard_map/ppermute | solution.py:32
  197.2 12.8 %collective-permute-start.36 = (bf16[2,256,256]{2,1,0:T(8,128)(2,1)S(1)}, bf16[2,256,256]{2,1,0:T(8,128)(2,1)S(1)}, u32[]{:S(2)}, u32[]{:S(2)}) collective-permute-start(bf16[2,256,256]{2,1,0:T(8,128)(2,1)S(1)} %collective-permute-done.25.refs_8_), channel_id=1, source_target_pairs={{0,64},{1,193},{64,0},{65,129},{128,192},{129,65},{192,128},{193,1... | collective-permute-start | bytes 786440 | tf_op jit(solution)/shard_map/ppermute | solution.py:32
  197.3 20.2 %copy-start.11 = (bf16[2,256,256]{2,1,0:T(8,128)(2,1)}, bf16[2,256,256]{2,1,0:T(8,128)(2,1)S(1)}, u32[]{:S(2)}) copy-start(bf16[2,256,256]{2,1,0:T(8,128)(2,1)S(1)} %collective-permute-done.31.refs_2_) | copy-start | bytes 786436
  197.3 14.5 %collective-permute-start.34 = (bf16[2,256,256]{2,1,0:T(8,128)(2,1)S(1)}, bf16[2,256,256]{2,1,0:T(8,128)(2,1)S(1)}, u32[]{:S(2)}, u32[]{:S(2)}) collective-permute-start(bf16[2,256,256]{2,1,0:T(8,128)(2,1)S(1)} %collective-permute-done.24.refs_4_), channel_id=1, source_target_pairs={{0,192},{1,65},{64,128},{65,1},{128,64},{129,193},{192,0},{193,129... | collective-permute-start | bytes 786440 | tf_op jit(solution)/shard_map/ppermute | solution.py:32
  199.8 23.2 %copy-start.4 = (bf16[2,256,256]{2,1,0:T(8,128)(2,1)}, bf16[2,256,256]{2,1,0:T(8,128)(2,1)S(1)}, u32[]{:S(2)}) copy-start(bf16[2,256,256]{2,1,0:T(8,128)(2,1)S(1)} %collective-permute-done.26.refs_0_) | copy-start | bytes 786436
  199.8 15.9 %collective-permute-start.27 = (bf16[2,256,256]{2,1,0:T(8,128)(2,1)S(1)}, bf16[2,256,256]{2,1,0:T(8,128)(2,1)S(1)}, u32[]{:S(2)}, u32[]{:S(2)}) collective-permute-start(bf16[2,256,256]{2,1,0:T(8,128)(2,1)S(1)} %collective-permute-done.26.refs_0_), channel_id=1, source_target_pairs={{0,64},{1,193},{64,0},{65,129},{128,192},{129,65},{192,128},{193,1... | collective-permute-start | bytes 786440 | tf_op jit(solution)/shard_map/ppermute | solution.py:32
  204.0 13.5 %copy-start.12 = (bf16[2,256,256]{2,1,0:T(8,128)(2,1)}, bf16[2,256,256]{2,1,0:T(8,128)(2,1)S(1)}, u32[]{:S(2)}) copy-start(bf16[2,256,256]{2,1,0:T(8,128)(2,1)S(1)} %collective-permute-done.32.refs_3_) | copy-start | bytes 786436
  204.0 13.4 %collective-permute-start.37 = (bf16[2,256,256]{2,1,0:T(8,128)(2,1)S(1)}, bf16[2,256,256]{2,1,0:T(8,128)(2,1)S(1)}, u32[]{:S(2)}, u32[]{:S(2)}) collective-permute-start(bf16[2,256,256]{2,1,0:T(8,128)(2,1)S(1)} %collective-permute-done.25.refs_8_), channel_id=1, source_target_pairs={{0,192},{1,65},{64,128},{65,1},{128,64},{129,193},{192,0},{193,129... | collective-permute-start | bytes 786440 | tf_op jit(solution)/shard_map/ppermute | solution.py:32
  204.4 13.0 %copy-start.13 = (bf16[2,256,256]{2,1,0:T(8,128)(2,1)}, bf16[2,256,256]{2,1,0:T(8,128)(2,1)S(1)}, u32[]{:S(2)}) copy-start(bf16[2,256,256]{2,1,0:T(8,128)(2,1)S(1)} %collective-permute-done.33.refs_5_) | copy-start | bytes 786436
  204.5 13.0 %collective-permute-start.35 = (bf16[2,256,256]{2,1,0:T(8,128)(2,1)S(1)}, bf16[2,256,256]{2,1,0:T(8,128)(2,1)S(1)}, u32[]{:S(2)}, u32[]{:S(2)}) collective-permute-start(bf16[2,256,256]{2,1,0:T(8,128)(2,1)S(1)} %collective-permute-done.33.refs_5_), channel_id=1, source_target_pairs={{0,192},{1,65},{64,128},{65,1},{128,64},{129,193},{192,0},{193,129... | collective-permute-start | bytes 786440 | tf_op jit(solution)/shard_map/ppermute | solution.py:32
  210.1 7.4 %copy-start.14 = (bf16[2,256,256]{2,1,0:T(8,128)(2,1)}, bf16[2,256,256]{2,1,0:T(8,128)(2,1)S(1)}, u32[]{:S(2)}) copy-start(bf16[2,256,256]{2,1,0:T(8,128)(2,1)S(1)} %collective-permute-done.36.refs_9_) | copy-start | bytes 786436
  210.1 7.4 %collective-permute-start.38 = (bf16[2,256,256]{2,1,0:T(8,128)(2,1)S(1)}, bf16[2,256,256]{2,1,0:T(8,128)(2,1)S(1)}, u32[]{:S(2)}, u32[]{:S(2)}) collective-permute-start(bf16[2,256,256]{2,1,0:T(8,128)(2,1)S(1)} %collective-permute-done.36.refs_9_), channel_id=1, source_target_pairs={{0,192},{1,65},{64,128},{65,1},{128,64},{129,193},{192,0},{193,129... | collective-permute-start | bytes 786440 | tf_op jit(solution)/shard_map/ppermute | solution.py:32
  211.8 11.1 %collective-permute-start.28 = (bf16[2,256,256]{2,1,0:T(8,128)(2,1)S(1)}, bf16[2,256,256]{2,1,0:T(8,128)(2,1)S(1)}, u32[]{:S(2)}, u32[]{:S(2)}) collective-permute-start(bf16[2,256,256]{2,1,0:T(8,128)(2,1)S(1)} %collective-permute-done.26.refs_0_), channel_id=1, source_target_pairs={{0,192},{1,65},{64,128},{65,1},{128,64},{129,193},{192,0},{193,129... | collective-permute-start | bytes 786440 | tf_op jit(solution)/shard_map/ppermute | solution.py:32
  215.7 7.4 %collective-permute-start.29 = (bf16[2,256,256]{2,1,0:T(8,128)(2,1)S(1)}, bf16[2,256,256]{2,1,0:T(8,128)(2,1)S(1)}, u32[]{:S(2)}, u32[]{:S(2)}) collective-permute-start(bf16[2,256,256]{2,1,0:T(8,128)(2,1)S(1)} %collective-permute-done.27.refs_1_), channel_id=1, source_target_pairs={{0,192},{1,65},{64,128},{65,1},{128,64},{129,193},{192,0},{193,129... | collective-permute-start | bytes 786440 | tf_op jit(solution)/shard_map/ppermute | solution.py:32
  (9 other events, 23.1 us)

commit v2 on v1

--- a/solution.py
+++ b/solution.py
@@ -14,6 +14,8 @@
 REP = NX * NZ
 TOK = 512
 BLK = 256
+ROWS_A = 352
+CHUNKS = 2
 F32 = jnp.float32
 BF16 = jnp.bfloat16
 HIGH = lax.Precision.HIGHEST
@@ -33,8 +35,8 @@
 
 
 def swapped_ring(block, axis, size):
-    pair = jnp.stack([block, near(block, axis, size, 1)])
-    found, held, which = [pair], pair, -1
+    held, which = jnp.stack([block, near(block, axis, size, 1)]), -1
+    found = [held]
     for _ in range(size // 2 - 1):
         held = near(held, axis, size, which)
         found.append(held)
@@ -42,11 +44,19 @@
     return found
 
 
-def gather_plane(block):
-    out = []
-    for line in swapped_ring(block, "z", NZ):
+def gather_plane(block, cut, chunks):
+    out, kz = [], 0
+    lines = swapped_ring(block[:cut], "z", NZ)
+    for chunk in range(chunks):
+        line = lines[chunk * 4 // chunks:(chunk + 1) * 4 // chunks]
+        line = line[0] if len(line) == 1 else jnp.concatenate(line)
         ahead, behind = near(line, "x", NX, 1), near(line, "x", NX, -1)
-        out += [line, ahead, behind, near(ahead, "x", NX, -1)]
+        for kx, piece in enumerate((line, ahead, behind, near(ahead, "x", NX, -1))):
+            out.append((piece[:, None], 0, kz, kx))
+        kz += line.shape[0]
+    if cut < block.shape[0]:
+        for no, piece in enumerate(swapped_ring(jnp.concatenate(swapped_ring(block[cut:], "x", NX)), "z", NZ)):
+            out.append((piece, cut, 2 * no, 0))
     return out
 
 
@@ -69,9 +79,10 @@
     return x * NZ + z
 
 
-def grads_kernel(count, place, *refs):
+def grads_kernel(layout, place, *refs):
     tokens = NY * NC
     x_pieces, refs = refs[:tokens], refs[tokens:]
+    count = len(layout)
     pieces, (weights_ref, g_hbm, sums_ref) = refs[:count], refs[count:count + 3]
     xv, wv, gv, xsem, wsem, gsem = refs[count + 3:]
     y, core, turn = place[4], place[5], place[6]
@@ -80,8 +91,10 @@
         c = core if no < NY else 1 - core
         row = lax.rem(y + (turn if no < NY else -turn) * STEPS[no % NY] + NY, NY)
         parts.append(pltpu.make_async_copy(x_pieces[no], xv.at[row, c], xsem.at[no]))
-    loads = [pltpu.make_async_copy(pieces[no], wv.at[pl.ds(no // NX * 2, 2), no % NX], wsem.at[no])
-             for no in range(count)]
+    loads = []
+    for no, ((nz, nx, rows, _), offset, kz, kx) in enumerate(layout):
+        loads.append(pltpu.make_async_copy(
+            pieces[no], wv.at[pl.ds(kz, nz), pl.ds(kx, nx), pl.ds(offset, rows)], wsem.at[no]))
     for copy in parts + loads:
         copy.start()
     for copy in parts:
@@ -94,9 +107,12 @@
         return 0
 
     outs = []
-    for part in range(count // NX):
-        for copy in loads[part * NX:(part + 1) * NX]:
-            copy.wait()
+    waited = set()
+    for part in range(NZ // 2):
+        for no, (_, _, kz, _) in enumerate(layout):
+            if kz < 2 * part + 2 and no not in waited:
+                loads[no].wait()
+                waited.add(no)
         lax.fori_loop(part * 2 * NX, (part + 1) * 2 * NX, multiply, 0, unroll=2)
         at = pl.ds(part * 2 * NX, 2 * NX)
         outs.append(pltpu.make_async_copy(gv.at[at], g_hbm.at[at], gsem.at[part]))
@@ -137,9 +153,10 @@
 
 
 def grads_and_sums(place, x_pieces, pieces, weights):
+    layout = [(piece.shape, *where) for piece, *where in pieces]
     any_spec = pl.BlockSpec(memory_space=pl.ANY)
     return pl.pallas_call(
-        functools.partial(grads_kernel, len(pieces)),
+        functools.partial(grads_kernel, layout),
         out_shape=(jax.ShapeDtypeStruct((REP, BLK, BLK), F32), jax.ShapeDtypeStruct((NX * NY, 16, 128), F32)),
         in_specs=[pl.BlockSpec(memory_space=pltpu.SMEM)] + [any_spec] * (len(x_pieces) + len(pieces))
         + [pl.BlockSpec(memory_space=pltpu.VMEM)],
@@ -154,7 +171,7 @@
         ],
         compiler_params=pltpu.CompilerParams(vmem_limit_bytes=58 * 2**20),
         cost_estimate=pl.CostEstimate(flops=6 * 10**9, bytes_accessed=24 * 2**20, transcendentals=0),
-    )(place, *x_pieces, *pieces, weights)
+    )(place, *x_pieces, *[piece for piece, *_ in pieces], weights)
 
 
 def tree_weights(sums):
@@ -305,10 +322,10 @@
     weighted = (weights[:, None] * cotangent.astype(F32)).astype(BF16)
     own = lax.all_to_all(token_rows, ("x", "z"), 1, 0, tiled=True).reshape(REP, -1, BLK)
     x_pieces = gather_tokens(own)
-    grads, sums = grads_and_sums(place, x_pieces, gather_plane(weighted), weights.reshape(-1, 128))
+    grads, sums = grads_and_sums(place, x_pieces, gather_plane(weighted, ROWS_A, CHUNKS), weights.reshape(-1, 128))
     sums = totals_of_groups(sums)
     new_weights, new_master, new_one, new_two = update(place, sums, grads, master, moment_one, moment_two)
-    pieces = gather_plane(new_weights)
+    pieces = [piece[:, 0] for piece, *_ in gather_plane(new_weights, BLK, 4)]
     early = len(pieces) - NX
     out = place_rows(place, pieces[:early], 0, ())
     out = place_rows(place, pieces[early:], early, (out,))

time: 229 us -> 226 us (0.987)
  waiting for transfers between devices: 100 us -> 80.1 us
  starting transfers between devices: 46.9 us -> 61.8 us
    ppermute x35, waiting for transfers between devices: 100 us -> 80.1 us  [near(): return lax.ppermute(array, (axis, 'c'), pairs)]
    ppermute x35, starting transfers between devices: 34.8 us -> 49.7 us  [near(): return lax.ppermute(array, (axis, 'c'), pairs)]
  transfers between devices with their start and end apart: 40 -> 40, of which waited for: 24 -> 23; matrix products, arithmetic and copies ran while one was open for 1% -> 2% of each run, Pallas kernels for 2% -> 2%
where the time goes in v2:
time: 226 us; the launch traced here: 224 us
  waiting for transfers between devices  80.1 us (35%)
  starting transfers between devices  61.8 us (27%)
  blocking collectives  38.9 us (17%)
  Pallas kernels  31.4 us (14%)
  local copies, waits for them, and re-layouts  7.52 us (3%)
  other arithmetic  2.8 us (1%)
    ppermute x35, waiting for transfers between devices, near(): return lax.ppermute(array, (axis, 'c'), pairs)  80.1 us
    ppermute x35, starting transfers between devices, near(): return lax.ppermute(array, (axis, 'c'), pairs)  49.7 us
    pallas_call x1, Pallas kernels, grads_and_sums(): pl.pallas_call(functools.partial(grads_kernel, layout), out_shape=(jax.Sh...  18.4 us
    all_to_all x1, blocking collectives, totals_of_groups(): sums = jnp.sum(lax.all_to_all(sums, ('x', 'y'), 0, 0), axis=0)  15 us
    all_to_all x1, blocking collectives, totals_of_groups(): lax.all_to_all(jnp.broadcast_to(sums[None], (NZ * NC,) + sums.shape), ('z...  14.4 us
    all_to_all x1, starting transfers between devices, local(): lax.all_to_all(token_rows, ('x', 'z'), 1, 0, tiled=True)  11.6 us
    unnamed x1, blocking collectives  9.48 us
    pallas_call x2, Pallas kernels, place_rows(): pl.pallas_call(functools.partial(place_kernel, first, count), out_shape=j...  6.69 us
  transfers between devices with their start and end apart: 40, of which 23 were waited for; matrix products, arithmetic and copies ran while one was open for 2% of the time, Pallas kernels for 2%

profile of v2, /device:TPU:4, one launch (start us, length us, event | category | flops | bytes accessed | tf_op | source)
XLA Modules:
  0.0 224.4 jit_solution(16387650484024865482)
XLA Ops:
  0.7 2.4 %copy.30 = bf16[8,32,8,256]{3,2,0,1:T(8,128)(2,1)} copy(bf16[8,32,8,256]{3,2,1,0:T(8,128)(2,1)} %bitcast.53) | data formatting | bytes 2097152 | tf_op jit(solution)/shard_map/all_to_all | solution.py:323
  3.0 11.6 %all-to-all-start = ((bf16[64,32,256]{2,0,1:T(8,128)(2,1)}), bf16[64,32,256]{2,0,1:T(8,128)(2,1)S(1)}, u32[]{:S(2)}, u32[]{:S(2)}) async-start(bf16[64,32,256]{2,0,1:T(8,128)(2,1)} %bitcast.51), calls=%async_computation | async-start | bytes 2097152 | tf_op jit(solution)/shard_map/all_to_all | solution.py:323
  14.6 0.6 dynamic-slice
  16.2 9.5 %all-reduce = s32[512]{0:T(512)S(1)} all-reduce(s32[512]{0:T(512)S(1)} %dynamic-update-slice), channel_id=1, replica_groups=mesh['x'=4,'z'=8,'y'=4,'c'=2] {'y','c'}, use_global_device_ids=true, to_apply=%add | all-reduce | flops 512 | bytes 4096
  25.6 0.6 fusion
  26.4 1.3 collective-permute-start.17
  27.7 3.8 %collective-permute-done.17 = bf16[160,256]{1,0:T(8,128)(2,1)S(1)} collective-permute-done((bf16[160,256]{1,0:T(8,128)(2,1)S(1)}, bf16[160,256]{1,0:T(8,128)(2,1)S(1)}, u32[]{:S(2)}, u32[]{:S(2)}) %collective-permute-start.17) | collective-permute-done | bytes 81952 | tf_op jit(solution)/shard_map/ppermute | solution.py:34
  31.4 1.4 collective-permute-start.18
  32.9 0.8 collective-permute-start.7
  33.7 4.5 %collective-permute-done.18 = bf16[2,160,256]{2,1,0:T(8,128)(2,1)S(1)} collective-permute-done((bf16[2,160,256]{2,1,0:T(8,128)(2,1)S(1)}, bf16[2,160,256]{2,1,0:T(8,128)(2,1)S(1)}, u32[]{:S(2)}, u32[]{:S(2)}) %collective-permute-start.18) | collective-permute-done | bytes 163872 | tf_op jit(solution)/shard_map/ppermute | solution.py:34
  38.2 1.9 collective-permute-start.19
  40.1 0.7 collective-permute-done.7
  40.8 2.8 %collective-permute-start.8 = (bf16[2,352,256]{2,1,0:T(8,128)(2,1)S(1)}, bf16[2,352,256]{2,1,0:T(8,128)(2,1)S(1)}, u32[]{:S(2)}, u32[]{:S(2)}) collective-permute-start(bf16[2,352,256]{2,1,0:T(8,128)(2,1)S(1)} %pad_maximum_fusion.2), channel_id=1, source_target_pairs={{0,56},{1,9},{8,16},{9,1},{16,8},{17,25},{24,32},{25,17},{32,24},{... | collective-permute-start | bytes 1081352 | tf_op jit(solution)/shard_map/ppermute | solution.py:34
  43.6 1.5 collective-permute-start
  45.1 1.6 collective-permute-done.19
  46.8 4.8 %collective-permute-start.20 = (bf16[2,4,160,256]{3,2,1,0:T(8,128)(2,1)S(1)}, bf16[2,4,160,256]{3,2,1,0:T(8,128)(2,1)S(1)}, u32[]{:S(2)}, u32[]{:S(2)}) collective-permute-start(bf16[2,4,160,256]{3,2,1,0:T(8,128)(2,1)S(1)} %pad_maximum_fusion.1.refs_16_), channel_id=1, source_target_pairs={{0,56},{1,9},{8,16},{9,1},{16,8},{17,25},{24,32},{25,17},{32,24},{... | collective-permute-start | bytes 1966088 | tf_op jit(solution)/shard_map/ppermute | solution.py:34
  51.6 1.0 pad_maximum_fusion
  52.5 2.3 %collective-permute-start.9 = (bf16[4,352,256]{2,1,0:T(8,128)(2,1)S(1)}, bf16[4,352,256]{2,1,0:T(8,128)(2,1)S(1)}, u32[]{:S(2)}, u32[]{:S(2)}) collective-permute-start(bf16[4,352,256]{2,1,0:T(8,128)(2,1)S(1)} %get-tuple-element.16), channel_id=1, source_target_pairs={{0,64},{1,193},{64,0},{65,129},{128,192},{129,65},{192,128},{193,1... | collective-permute-start | bytes 2162696 | tf_op jit(solution)/shard_map/ppermute | solution.py:34
  54.8 5.3 %collective-permute-done.12 = bf16[2,352,256]{2,1,0:T(8,128)(2,1)S(1)} collective-permute-done((bf16[2,352,256]{2,1,0:T(8,128)(2,1)S(1)}, bf16[2,352,256]{2,1,0:T(8,128)(2,1)S(1)}, u32[]{:S(2)}, u32[]{:S(2)}) %collective-permute-start.12) | collective-permute-done | bytes 360480 | tf_op jit(solution)/shard_map/ppermute | solution.py:34
  60.1 3.1 %collective-permute-start.13 = (bf16[2,352,256]{2,1,0:T(8,128)(2,1)S(1)}, bf16[2,352,256]{2,1,0:T(8,128)(2,1)S(1)}, u32[]{:S(2)}, u32[]{:S(2)}) collective-permute-start(bf16[2,352,256]{2,1,0:T(8,128)(2,1)S(1)} %collective-permute-done.12), channel_id=1, source_target_pairs={{0,56},{1,9},{8,16},{9,1},{16,8},{17,25},{24,32},{25,17},{32,24},{... | collective-permute-start | bytes 1081352 | tf_op jit(solution)/shard_map/ppermute | solution.py:34
  64.0 6.6 %collective-permute-done.13 = bf16[2,352,256]{2,1,0:T(8,128)(2,1)S(1)} collective-permute-done((bf16[2,352,256]{2,1,0:T(8,128)(2,1)S(1)}, bf16[2,352,256]{2,1,0:T(8,128)(2,1)S(1)}, u32[]{:S(2)}, u32[]{:S(2)}) %collective-permute-start.13) | collective-permute-done | bytes 360480 | tf_op jit(solution)/shard_map/ppermute | solution.py:34
  70.6 3.1 %collective-permute-start.15 = (bf16[4,352,256]{2,1,0:T(8,128)(2,1)S(1)}, bf16[4,352,256]{2,1,0:T(8,128)(2,1)S(1)}, u32[]{:S(2)}, u32[]{:S(2)}) collective-permute-start(bf16[4,352,256]{2,1,0:T(8,128)(2,1)S(1)} %constant_dynamic-update-slice_fusion), channel_id=1, source_target_pairs={{0,192},{1,65},{64,128},{65,1},{128,64},{129,193},{192,0},{193,129... | collective-permute-start | bytes 2162696 | tf_op jit(solution)/shard_map/ppermute | solution.py:34
  73.8 1.7 collective-permute-start.1
  75.5 1.5 collective-permute-start.2
  77.0 1.9 collective-permute-start.14
  78.9 2.5 %collective-permute-start.11 = (bf16[4,352,256]{2,1,0:T(8,128)(2,1)S(1)}, bf16[4,352,256]{2,1,0:T(8,128)(2,1)S(1)}, u32[]{:S(2)}, u32[]{:S(2)}) collective-permute-start(bf16[4,352,256]{2,1,0:T(8,128)(2,1)S(1)} %collective-permute-done.9), channel_id=1, source_target_pairs={{0,192},{1,65},{64,128},{65,1},{128,64},{129,193},{192,0},{193,129... | collective-permute-start | bytes 2162696 | tf_op jit(solution)/shard_map/ppermute | solution.py:34
  81.5 9.2 %collective-permute-done.15 = bf16[4,352,256]{2,1,0:T(8,128)(2,1)S(1)} collective-permute-done((bf16[4,352,256]{2,1,0:T(8,128)(2,1)S(1)}, bf16[4,352,256]{2,1,0:T(8,128)(2,1)S(1)}, u32[]{:S(2)}, u32[]{:S(2)}) %collective-permute-start.15) | collective-permute-done | bytes 720928 | tf_op jit(solution)/shard_map/ppermute | solution.py:34
  90.7 2.5 %collective-permute-start.22 = (bf16[2,4,160,256]{3,2,1,0:T(8,128)(2,1)S(1)}, bf16[2,4,160,256]{3,2,1,0:T(8,128)(2,1)S(1)}, u32[]{:S(2)}, u32[]{:S(2)}) collective-permute-start(bf16[2,4,160,256]{3,2,1,0:T(8,128)(2,1)S(1)} %collective-permute-done.21.refs_18_), channel_id=1, source_target_pairs={{0,56},{1,9},{8,16},{9,1},{16,8},{17,25},{24,32},{25,17},{32,24},{... | collective-permute-start | bytes 1966088 | tf_op jit(solution)/shard_map/ppermute | solution.py:34
  93.1 2.6 %collective-permute-done.14 = bf16[4,352,256]{2,1,0:T(8,128)(2,1)} collective-permute-done((bf16[4,352,256]{2,1,0:T(8,128)(2,1)S(1)}, bf16[4,352,256]{2,1,0:T(8,128)(2,1)}, u32[]{:S(2)}, u32[]{:S(2)}) %collective-permute-start.14) | collective-permute-done | bytes 720928 | tf_op jit(solution)/shard_map/ppermute | solution.py:34
  95.8 2.6 %collective-permute-done.11 = bf16[4,352,256]{2,1,0:T(8,128)(2,1)S(1)} collective-permute-done((bf16[4,352,256]{2,1,0:T(8,128)(2,1)S(1)}, bf16[4,352,256]{2,1,0:T(8,128)(2,1)S(1)}, u32[]{:S(2)}, u32[]{:S(2)}) %collective-permute-start.11) | collective-permute-done | bytes 720928 | tf_op jit(solution)/shard_map/ppermute | solution.py:34
  98.9 2.2 collective-permute-done.2.refs_3_
  101.1 1.3 collective-permute-done.22.refs_19_
  102.5 0.9 copy-done.26
  103.3 0.6 collective-permute-start.16
  104.0 0.7 stack.67.place
  104.6 10.3 %collective-permute-done.16 = bf16[4,352,256]{2,1,0:T(8,128)(2,1)} collective-permute-done((bf16[4,352,256]{2,1,0:T(8,128)(2,1)}, bf16[4,352,256]{2,1,0:T(8,128)(2,1)}, u32[]{:S(2)}, u32[]{:S(2)}) %collective-permute-start.16) | collective-permute-done | bytes 720928 | tf_op jit(solution)/shard_map/ppermute | solution.py:34
  115.0 18.4 %shard_map.93 = (f32[32,256,256]{2,1,0:T(8,128)}, f32[16,16,128]{2,1,0:T(8,128)}) custom-call(s32[7]{0:T(128)} %stack.67.place, bf16[32,64,256]{2,1,0:T(8,128)(2,1)} %bitcast.57, bf16[32,64,256]{2,1,0:T(8,128)(2,1)} %collective-permute-done.refs_1_, bf16[32,64,256]{2,1,0:T(8,128)(2,1)} %collective-permute-done.1.refs_2_, ...), custom_call_target="tpu_custom_call" | custom-call | flops 6000000000 | bytes 25165824 | tf_op jit(solution)/shard_map/pallas_call | solution.py:158
  133.4 15.0 %all_to_all.26 = f32[16,16,128]{2,1,0:T(8,128)S(1)} all-to-all(f32[16,16,128]{2,1,0:T(8,128)} %get-tuple-element.10), channel_id=1, replica_groups=mesh['x'=4,'z'=8,'y'=4,'c'=2] {'x','y'}, dimensions={0} | all-to-all | bytes 262144 | tf_op jit(solution)/shard_map/all_to_all | solution.py:308
  148.5 14.4 %all_to_all.27.sums_ref = f32[16,16,128]{2,1,0:T(8,128)} all-to-all(f32[16,16,128]{2,1,0:T(8,128)S(1)} %broadcast_in_dim.39), channel_id=1, replica_groups=mesh['x'=4,'z'=8,'y'=4,'c'=2] {'z','c'}, dimensions={0} | all-to-all | bytes 262144 | tf_op jit(solution)/shard_map/all_to_all | solution.py:309
  162.9 6.3 %shard_map.94 = (bf16[256,256]{1,0:T(8,128)(2,1)}, f32[256,256]{1,0:T(8,128)}, f32[256,256]{1,0:T(8,128)}, f32[256,256]{1,0:T(8,128)}) custom-call(s32[7]{0:T(128)} %stack.67.place, f32[16,16,128]{2,1,0:T(8,128)} %all_to_all.27.sums_ref, f32[32,256,256]{2,1,0:T(8,128)} %get-tuple-element.11.g_hbm, f32[256,256]{1,0:T(8,128)} %master_ref.1, ...), custom_call_target="tpu_custom_call" | custom-call | flops 5000000 | bytes 10485760 | tf_op jit(solution)/shard_map/pallas_call | solution.py:254
  169.2 0.6 collective-permute-start.23
  169.8 4.6 %collective-permute-done.23 = bf16[256,256]{1,0:T(8,128)(2,1)S(1)} collective-permute-done((bf16[256,256]{1,0:T(8,128)(2,1)}, bf16[256,256]{1,0:T(8,128)(2,1)S(1)}, u32[]{:S(2)}, u32[]{:S(2)}) %collective-permute-start.23) | collective-permute-done | bytes 131104 | tf_op jit(solution)/shard_map/ppermute | solution.py:34
  174.4 0.9 pad_maximum_fusion.4.refs_0_
  175.6 7.4 %collective-permute-done.24.refs_4_ = bf16[2,256,256]{2,1,0:T(8,128)(2,1)S(1)} collective-permute-done((bf16[2,256,256]{2,1,0:T(8,128)(2,1)S(1)}, bf16[2,256,256]{2,1,0:T(8,128)(2,1)S(1)}, u32[]{:S(2)}, u32[]{:S(2)}) %collective-permute-start.24) | collective-permute-done | bytes 262176 | tf_op jit(solution)/shard_map/ppermute | solution.py:34
  183.1 1.4 collective-permute-start.30
  184.4 1.5 collective-permute-start.31
  185.9 3.5 %collective-permute-done.25.refs_8_ = bf16[2,256,256]{2,1,0:T(8,128)(2,1)S(1)} collective-permute-done((bf16[2,256,256]{2,1,0:T(8,128)(2,1)S(1)}, bf16[2,256,256]{2,1,0:T(8,128)(2,1)S(1)}, u32[]{:S(2)}, u32[]{:S(2)}) %collective-permute-start.25) | collective-permute-done | bytes 262176 | tf_op jit(solution)/shard_map/ppermute | solution.py:34
  189.6 2.4 %collective-permute-done.30.refs_1_ = bf16[2,256,256]{2,1,0:T(8,128)(2,1)S(1)} collective-permute-done((bf16[2,256,256]{2,1,0:T(8,128)(2,1)S(1)}, bf16[2,256,256]{2,1,0:T(8,128)(2,1)S(1)}, u32[]{:S(2)}, u32[]{:S(2)}) %collective-permute-start.30) | collective-permute-done | bytes 262176 | tf_op jit(solution)/shard_map/ppermute | solution.py:34
  192.1 2.3 %collective-permute-start.33 = (bf16[2,256,256]{2,1,0:T(8,128)(2,1)S(1)}, bf16[2,256,256]{2,1,0:T(8,128)(2,1)S(1)}, u32[]{:S(2)}, u32[]{:S(2)}) collective-permute-start(bf16[2,256,256]{2,1,0:T(8,128)(2,1)S(1)} %collective-permute-done.24.refs_4_), channel_id=1, source_target_pairs={{0,64},{1,193},{64,0},{65,129},{128,192},{129,65},{192,128},{193,1... | collective-permute-start | bytes 786440 | tf_op jit(solution)/shard_map/ppermute | solution.py:34
  194.5 1.8 collective-permute-start.34
  196.2 0.8 collective-permute-done.26.refs_0_
  197.0 1.8 collective-permute-start.27
  198.8 2.4 %collective-permute-done.32.refs_3_ = bf16[2,256,256]{2,1,0:T(8,128)(2,1)S(1)} collective-permute-done((bf16[2,256,256]{2,1,0:T(8,128)(2,1)S(1)}, bf16[2,256,256]{2,1,0:T(8,128)(2,1)S(1)}, u32[]{:S(2)}, u32[]{:S(2)}) %collective-permute-start.32) | collective-permute-done | bytes 262176 | tf_op jit(solution)/shard_map/ppermute | solution.py:34
  201.7 1.7 collective-permute-start.35
  203.4 3.9 %collective-permute-done.36.refs_9_ = bf16[2,256,256]{2,1,0:T(8,128)(2,1)S(1)} collective-permute-done((bf16[2,256,256]{2,1,0:T(8,128)(2,1)S(1)}, bf16[2,256,256]{2,1,0:T(8,128)(2,1)S(1)}, u32[]{:S(2)}, u32[]{:S(2)}) %collective-permute-start.36) | collective-permute-done | bytes 262176 | tf_op jit(solution)/shard_map/ppermute | solution.py:34
  207.3 1.7 collective-permute-start.38
  209.3 3.6 %collective-permute-done.27.refs_1_ = bf16[2,256,256]{2,1,0:T(8,128)(2,1)S(1)} collective-permute-done((bf16[2,256,256]{2,1,0:T(8,128)(2,1)S(1)}, bf16[2,256,256]{2,1,0:T(8,128)(2,1)S(1)}, u32[]{:S(2)}, u32[]{:S(2)}) %collective-permute-start.27) | collective-permute-done | bytes 262176 | tf_op jit(solution)/shard_map/ppermute | solution.py:34
  212.9 1.7 collective-permute-start.29
  214.7 0.6 copy-done.17
  215.4 0.7 copy-done.18
  216.1 3.9 %shard_map.95.refs_4_ = bf16[32,256,256]{2,1,0:T(8,128)(2,1)} custom-call(s32[7]{0:T(128)} %stack.67.place, bf16[2,256,256]{2,1,0:T(8,128)(2,1)} %copy-done.1, bf16[2,256,256]{2,1,0:T(8,128)(2,1)} %copy-done.10, bf16[2,256,256]{2,1,0:T(8,128)(2,1)} %copy-done.11, bf16[2,256,256]{2,1,0:T(8,128)(2,1)} %copy-done.12, bf16[2,256,256]{2,1,0:T(8,128)(2,1)} %copy-done.8, ...), custom_call_target="tpu_custom_call" | custom-call | bytes 3145728 | tf_op jit(solution)/shard_map/pallas_call | solution.py:291
  220.2 0.5 copy-done.5
  220.8 0.7 copy-done.6
  221.5 2.8 %shard_map.96 = bf16[32,256,256]{2,1,0:T(8,128)(2,1)} custom-call(s32[7]{0:T(128)} %stack.67.place, bf16[2,256,256]{2,1,0:T(8,128)(2,1)} %copy-done.3, bf16[2,256,256]{2,1,0:T(8,128)(2,1)} %copy-done.4, bf16[2,256,256]{2,1,0:T(8,128)(2,1)} %copy-done.5, bf16[2,256,256]{2,1,0:T(8,128)(2,1)} %copy-done.6, ...), custom_call_target="tpu_custom_call", output_to_operand_aliasing={{}: (5, {})} | custom-call | bytes 1048576 | tf_op jit(solution)/shard_map/pallas_call | solution.py:291
  (100 shorter events, 3.6 us)
Async XLA Ops:
  0.6 14.0 %copy-start.28 = (u32[256]{0:T(256)S(1)}, u32[256]{0:T(256)}, u32[]{:S(2)}) copy-start(u32[256]{0:T(256)} %constant.46) | copy-start | bytes 3076
  0.6 15.3 %copy-start.27 = (s32[64]{0:T(128)S(1)}, s32[64]{0:T(128)}, u32[]{:S(2)}) copy-start(s32[64]{0:T(128)} %param.7) | copy-start | bytes 772
  0.7 25.6 %copy-start.7 = (bf16[512,256]{1,0:T(8,128)(2,1)S(1)}, bf16[512,256]{1,0:T(8,128)(2,1)}, u32[]{:S(2)}) copy-start(bf16[512,256]{1,0:T(8,128)(2,1)} %param.8) | copy-start | bytes 786436
  3.0 40.6 %all-to-all-start = ((bf16[64,32,256]{2,0,1:T(8,128)(2,1)}), bf16[64,32,256]{2,0,1:T(8,128)(2,1)S(1)}, u32[]{:S(2)}, u32[]{:S(2)}) async-start(bf16[64,32,256]{2,0,1:T(8,128)(2,1)} %bitcast.51), calls=%async_computation | async-start | bytes 2097152 | tf_op jit(solution)/shard_map/all_to_all | solution.py:323
  26.4 5.0 %collective-permute-start.17 = (bf16[160,256]{1,0:T(8,128)(2,1)S(1)}, bf16[160,256]{1,0:T(8,128)(2,1)S(1)}, u32[]{:S(2)}, u32[]{:S(2)}) collective-permute-start(bf16[160,256]{1,0:T(8,128)(2,1)S(1)} %get-tuple-element.21), channel_id=1, source_target_pairs={{0,64},{1,193},{64,0},{65,129},{128,192},{129,65},{192,128},{193,1... | collective-permute-start | bytes 245768 | tf_op jit(solution)/shard_map/ppermute | solution.py:34
  31.4 6.7 %collective-permute-start.18 = (bf16[2,160,256]{2,1,0:T(8,128)(2,1)S(1)}, bf16[2,160,256]{2,1,0:T(8,128)(2,1)S(1)}, u32[]{:S(2)}, u32[]{:S(2)}) collective-permute-start(bf16[2,160,256]{2,1,0:T(8,128)(2,1)S(1)} %pad_maximum_fusion.5), channel_id=1, source_target_pairs={{0,192},{1,65},{64,128},{65,1},{128,64},{129,193},{192,0},{193,129... | collective-permute-start | bytes 491528 | tf_op jit(solution)/shard_map/ppermute | solution.py:34
  32.9 7.9 %collective-permute-start.7 = (bf16[352,256]{1,0:T(8,128)(2,1)S(1)}, bf16[352,256]{1,0:T(8,128)(2,1)S(1)}, u32[]{:S(2)}, u32[]{:S(2)}) collective-permute-start(bf16[352,256]{1,0:T(8,128)(2,1)S(1)} %get-tuple-element.23), channel_id=1, source_target_pairs={{0,8},{1,57},{8,0},{9,17},{16,24},{17,9},{24,16},{25,33},{32,40},{... | collective-permute-start | bytes 540680 | tf_op jit(solution)/shard_map/ppermute | solution.py:34
  38.2 8.5 %collective-permute-start.19 = (bf16[4,160,256]{2,1,0:T(8,128)(2,1)S(1)}, bf16[4,160,256]{2,1,0:T(8,128)(2,1)S(1)}, u32[]{:S(2)}, u32[]{:S(2)}) collective-permute-start(bf16[4,160,256]{2,1,0:T(8,128)(2,1)S(1)} %get-tuple-element.19), channel_id=1, source_target_pairs={{0,8},{1,57},{8,0},{9,17},{16,24},{17,9},{24,16},{25,33},{32,40},{... | collective-permute-start | bytes 983048 | tf_op jit(solution)/shard_map/ppermute | solution.py:34
  40.8 10.8 %collective-permute-start.8 = (bf16[2,352,256]{2,1,0:T(8,128)(2,1)S(1)}, bf16[2,352,256]{2,1,0:T(8,128)(2,1)S(1)}, u32[]{:S(2)}, u32[]{:S(2)}) collective-permute-start(bf16[2,352,256]{2,1,0:T(8,128)(2,1)S(1)} %pad_maximum_fusion.2), channel_id=1, source_target_pairs={{0,56},{1,9},{8,16},{9,1},{16,8},{17,25},{24,32},{25,17},{32,24},{... | collective-permute-start | bytes 1081352 | tf_op jit(solution)/shard_map/ppermute | solution.py:34
  43.6 71.4 %copy-start = (bf16[64,32,256]{2,0,1:T(8,128)(2,1)}, bf16[64,32,256]{2,0,1:T(8,128)(2,1)S(1)}, u32[]{:S(2)}) copy-start(bf16[64,32,256]{2,0,1:T(8,128)(2,1)S(1)} %all-to-all-done) | copy-start | bytes 3145732
  43.6 31.9 %collective-permute-start = (bf16[32,64,256]{2,1,0:T(8,128)(2,1)S(1)}, bf16[32,64,256]{2,1,0:T(8,128)(2,1)}, u32[]{:S(2)}, u32[]{:S(2)}) collective-permute-start(bf16[32,64,256]{2,1,0:T(8,128)(2,1)S(1)} %bitcast.54), channel_id=1, source_target_pairs={{0,2},{1,7},{2,0},{3,5},{4,6},{5,3},{6,4},{7,1},{8,10},{9,15},{10,... | collective-permute-start | bytes 3145736 | tf_op jit(solution)/shard_map/ppermute | solution.py:34
  46.8 68.2 %copy-start.2 = (bf16[2,4,160,256]{3,2,1,0:T(8,128)(2,1)}, bf16[2,4,160,256]{3,2,1,0:T(8,128)(2,1)S(1)}, u32[]{:S(2)}) copy-start(bf16[2,4,160,256]{3,2,1,0:T(8,128)(2,1)S(1)} %pad_maximum_fusion.1.refs_16_) | copy-start | bytes 1966084
  46.8 17.2 %collective-permute-start.20 = (bf16[2,4,160,256]{3,2,1,0:T(8,128)(2,1)S(1)}, bf16[2,4,160,256]{3,2,1,0:T(8,128)(2,1)S(1)}, u32[]{:S(2)}, u32[]{:S(2)}) collective-permute-start(bf16[2,4,160,256]{3,2,1,0:T(8,128)(2,1)S(1)} %pad_maximum_fusion.1.refs_16_), channel_id=1, source_target_pairs={{0,56},{1,9},{8,16},{9,1},{16,8},{17,25},{24,32},{25,17},{32,24},{... | collective-permute-start | bytes 1966088 | tf_op jit(solution)/shard_map/ppermute | solution.py:34
  51.6 8.6 %collective-permute-start.12 = (bf16[2,352,256]{2,1,0:T(8,128)(2,1)S(1)}, bf16[2,352,256]{2,1,0:T(8,128)(2,1)S(1)}, u32[]{:S(2)}, u32[]{:S(2)}) collective-permute-start(bf16[2,352,256]{2,1,0:T(8,128)(2,1)S(1)} %collective-permute-done.8), channel_id=1, source_target_pairs={{0,8},{1,57},{8,0},{9,17},{16,24},{17,9},{24,16},{25,33},{32,40},{... | collective-permute-start | bytes 1081352 | tf_op jit(solution)/shard_map/ppermute | solution.py:34
  52.5 21.2 %collective-permute-start.9 = (bf16[4,352,256]{2,1,0:T(8,128)(2,1)S(1)}, bf16[4,352,256]{2,1,0:T(8,128)(2,1)S(1)}, u32[]{:S(2)}, u32[]{:S(2)}) collective-permute-start(bf16[4,352,256]{2,1,0:T(8,128)(2,1)S(1)} %get-tuple-element.16), channel_id=1, source_target_pairs={{0,64},{1,193},{64,0},{65,129},{128,192},{129,65},{192,128},{193,1... | collective-permute-start | bytes 2162696 | tf_op jit(solution)/shard_map/ppermute | solution.py:34
  60.1 10.5 %collective-permute-start.13 = (bf16[2,352,256]{2,1,0:T(8,128)(2,1)S(1)}, bf16[2,352,256]{2,1,0:T(8,128)(2,1)S(1)}, u32[]{:S(2)}, u32[]{:S(2)}) collective-permute-start(bf16[2,352,256]{2,1,0:T(8,128)(2,1)S(1)} %collective-permute-done.12), channel_id=1, source_target_pairs={{0,56},{1,9},{8,16},{9,1},{16,8},{17,25},{24,32},{25,17},{32,24},{... | collective-permute-start | bytes 1081352 | tf_op jit(solution)/shard_map/ppermute | solution.py:34
  63.3 13.8 %collective-permute-start.10 = (bf16[4,352,256]{2,1,0:T(8,128)(2,1)S(1)}, bf16[4,352,256]{2,1,0:T(8,128)(2,1)S(1)}, u32[]{:S(2)}, u32[]{:S(2)}) collective-permute-start(bf16[4,352,256]{2,1,0:T(8,128)(2,1)S(1)} %get-tuple-element.16), channel_id=1, source_target_pairs={{0,192},{1,65},{64,128},{65,1},{128,64},{129,193},{192,0},{193,129... | collective-permute-start | bytes 2162696 | tf_op jit(solution)/shard_map/ppermute | solution.py:34
  64.0 38.5 %copy-start.24 = (bf16[2,4,160,256]{3,2,1,0:T(8,128)(2,1)}, bf16[2,4,160,256]{3,2,1,0:T(8,128)(2,1)S(1)}, u32[]{:S(2)}) copy-start(bf16[2,4,160,256]{3,2,1,0:T(8,128)(2,1)S(1)} %collective-permute-done.20.refs_17_) | copy-start | bytes 1966084
  64.0 15.0 %collective-permute-start.21 = (bf16[2,4,160,256]{3,2,1,0:T(8,128)(2,1)S(1)}, bf16[2,4,160,256]{3,2,1,0:T(8,128)(2,1)S(1)}, u32[]{:S(2)}, u32[]{:S(2)}) collective-permute-start(bf16[2,4,160,256]{3,2,1,0:T(8,128)(2,1)S(1)} %collective-permute-done.20.refs_17_), channel_id=1, source_target_pairs={{0,8},{1,57},{8,0},{9,17},{16,24},{17,9},{24,16},{25,33},{32,40},{... | collective-permute-start | bytes 1966088 | tf_op jit(solution)/shard_map/ppermute | solution.py:34
  70.6 44.4 %copy-start.19 = (bf16[4,352,256]{2,1,0:T(8,128)(2,1)}, bf16[4,352,256]{2,1,0:T(8,128)(2,1)S(1)}, u32[]{:S(2)}) copy-start(bf16[4,352,256]{2,1,0:T(8,128)(2,1)S(1)} %constant_dynamic-update-slice_fusion) | copy-start | bytes 2162692
  70.6 20.0 %collective-permute-start.15 = (bf16[4,352,256]{2,1,0:T(8,128)(2,1)S(1)}, bf16[4,352,256]{2,1,0:T(8,128)(2,1)S(1)}, u32[]{:S(2)}, u32[]{:S(2)}) collective-permute-start(bf16[4,352,256]{2,1,0:T(8,128)(2,1)S(1)} %constant_dynamic-update-slice_fusion), channel_id=1, source_target_pairs={{0,192},{1,65},{64,128},{65,1},{128,64},{129,193},{192,0},{193,129... | collective-permute-start | bytes 2162696 | tf_op jit(solution)/shard_map/ppermute | solution.py:34
  73.8 24.6 %copy-start.20 = (bf16[4,352,256]{2,1,0:T(8,128)(2,1)}, bf16[4,352,256]{2,1,0:T(8,128)(2,1)S(1)}, u32[]{:S(2)}) copy-start(bf16[4,352,256]{2,1,0:T(8,128)(2,1)S(1)} %collective-permute-done.9) | copy-start | bytes 2162692
  73.8 24.6 %collective-permute-start.1 = (bf16[32,64,256]{2,1,0:T(8,128)(2,1)S(1)}, bf16[32,64,256]{2,1,0:T(8,128)(2,1)}, u32[]{:S(2)}, u32[]{:S(2)}) collective-permute-start(bf16[32,64,256]{2,1,0:T(8,128)(2,1)S(1)} %bitcast.55), channel_id=1, source_target_pairs={{0,6},{1,3},{2,4},{3,1},{4,2},{5,7},{6,0},{7,5},{8,14},{9,11},{10,... | collective-permute-start | bytes 3145736 | tf_op jit(solution)/shard_map/ppermute | solution.py:34
  75.5 25.6 %collective-permute-start.2 = (bf16[32,64,256]{2,1,0:T(8,128)(2,1)}, bf16[32,64,256]{2,1,0:T(8,128)(2,1)}, u32[]{:S(2)}, u32[]{:S(2)}) collective-permute-start(bf16[32,64,256]{2,1,0:T(8,128)(2,1)} %collective-permute-done.refs_1_), channel_id=1, source_target_pairs={{0,6},{1,3},{2,4},{3,1},{4,2},{5,7},{6,0},{7,5},{8,14},{9,11},{10,... | collective-permute-start | bytes 3145736 | tf_op jit(solution)/shard_map/ppermute | solution.py:34
  77.0 21.9 %copy-start.21 = (bf16[4,352,256]{2,1,0:T(8,128)(2,1)}, bf16[4,352,256]{2,1,0:T(8,128)(2,1)S(1)}, u32[]{:S(2)}) copy-start(bf16[4,352,256]{2,1,0:T(8,128)(2,1)S(1)} %collective-permute-done.10) | copy-start | bytes 2162692
  77.0 18.7 %collective-permute-start.14 = (bf16[4,352,256]{2,1,0:T(8,128)(2,1)S(1)}, bf16[4,352,256]{2,1,0:T(8,128)(2,1)}, u32[]{:S(2)}, u32[]{:S(2)}) collective-permute-start(bf16[4,352,256]{2,1,0:T(8,128)(2,1)S(1)} %constant_dynamic-update-slice_fusion), channel_id=1, source_target_pairs={{0,64},{1,193},{64,0},{65,129},{128,192},{129,65},{192,128},{193,1... | collective-permute-start | bytes 2162696 | tf_op jit(solution)/shard_map/ppermute | solution.py:34
  78.9 23.5 %copy-start.25 = (bf16[2,4,160,256]{3,2,1,0:T(8,128)(2,1)}, bf16[2,4,160,256]{3,2,1,0:T(8,128)(2,1)S(1)}, u32[]{:S(2)}) copy-start(bf16[2,4,160,256]{3,2,1,0:T(8,128)(2,1)S(1)} %collective-permute-done.21.refs_18_) | copy-start | bytes 1966084
  78.9 19.4 %collective-permute-start.11 = (bf16[4,352,256]{2,1,0:T(8,128)(2,1)S(1)}, bf16[4,352,256]{2,1,0:T(8,128)(2,1)S(1)}, u32[]{:S(2)}, u32[]{:S(2)}) collective-permute-start(bf16[4,352,256]{2,1,0:T(8,128)(2,1)S(1)} %collective-permute-done.9), channel_id=1, source_target_pairs={{0,192},{1,65},{64,128},{65,1},{128,64},{129,193},{192,0},{193,129... | collective-permute-start | bytes 2162696 | tf_op jit(solution)/shard_map/ppermute | solution.py:34
  90.6 10.5 %copy-start.22 = (bf16[4,352,256]{2,1,0:T(8,128)(2,1)}, bf16[4,352,256]{2,1,0:T(8,128)(2,1)S(1)}, u32[]{:S(2)}) copy-start(bf16[4,352,256]{2,1,0:T(8,128)(2,1)S(1)} %collective-permute-done.15) | copy-start | bytes 2162692
  90.7 11.8 %collective-permute-start.22 = (bf16[2,4,160,256]{3,2,1,0:T(8,128)(2,1)S(1)}, bf16[2,4,160,256]{3,2,1,0:T(8,128)(2,1)S(1)}, u32[]{:S(2)}, u32[]{:S(2)}) collective-permute-start(bf16[2,4,160,256]{3,2,1,0:T(8,128)(2,1)S(1)} %collective-permute-done.21.refs_18_), channel_id=1, source_target_pairs={{0,56},{1,9},{8,16},{9,1},{16,8},{17,25},{24,32},{25,17},{32,24},{... | collective-permute-start | bytes 1966088 | tf_op jit(solution)/shard_map/ppermute | solution.py:34
  95.8 19.2 %collective-permute-start.3 = (bf16[32,64,256]{2,1,0:T(8,128)(2,1)S(1)}, bf16[32,64,256]{2,1,0:T(8,128)(2,1)}, u32[]{:S(2)}, u32[]{:S(2)}) collective-permute-start(bf16[32,64,256]{2,1,0:T(8,128)(2,1)S(1)} %bitcast.56), channel_id=1, source_target_pairs={{0,1},{1,0},{2,3},{3,2},{4,5},{5,4},{6,7},{7,6},{8,9},{9,8},{10,11... | collective-permute-start | bytes 3145736 | tf_op jit(solution)/shard_map/ppermute | solution.py:25
  98.4 2.8 %copy-start.23 = (bf16[4,352,256]{2,1,0:T(8,128)(2,1)}, bf16[4,352,256]{2,1,0:T(8,128)(2,1)S(1)}, u32[]{:S(2)}) copy-start(bf16[4,352,256]{2,1,0:T(8,128)(2,1)S(1)} %collective-permute-done.11) | copy-start | bytes 2162692
  98.4 16.6 %collective-permute-start.4 = (bf16[32,64,256]{2,1,0:T(8,128)(2,1)}, bf16[32,64,256]{2,1,0:T(8,128)(2,1)}, u32[]{:S(2)}, u32[]{:S(2)}) collective-permute-start(bf16[32,64,256]{2,1,0:T(8,128)(2,1)} %collective-permute-done.refs_1_), channel_id=1, source_target_pairs={{0,1},{1,0},{2,3},{3,2},{4,5},{5,4},{6,7},{7,6},{8,9},{9,8},{10,11... | collective-permute-start | bytes 3145736 | tf_op jit(solution)/shard_map/ppermute | solution.py:25
  98.4 16.6 %collective-permute-start.5 = (bf16[32,64,256]{2,1,0:T(8,128)(2,1)}, bf16[32,64,256]{2,1,0:T(8,128)(2,1)}, u32[]{:S(2)}, u32[]{:S(2)}) collective-permute-start(bf16[32,64,256]{2,1,0:T(8,128)(2,1)} %collective-permute-done.1.refs_2_), channel_id=1, source_target_pairs={{0,1},{1,0},{2,3},{3,2},{4,5},{5,4},{6,7},{7,6},{8,9},{9,8},{10,11... | collective-permute-start | bytes 3145736 | tf_op jit(solution)/shard_map/ppermute | solution.py:25
  101.1 13.8 %collective-permute-start.6 = (bf16[32,64,256]{2,1,0:T(8,128)(2,1)}, bf16[32,64,256]{2,1,0:T(8,128)(2,1)}, u32[]{:S(2)}, u32[]{:S(2)}) collective-permute-start(bf16[32,64,256]{2,1,0:T(8,128)(2,1)} %collective-permute-done.2.refs_3_), channel_id=1, source_target_pairs={{0,1},{1,0},{2,3},{3,2},{4,5},{5,4},{6,7},{7,6},{8,9},{9,8},{10,11... | collective-permute-start | bytes 3145736 | tf_op jit(solution)/shard_map/ppermute | solution.py:25
  102.5 0.9 copy-start.26
  103.3 11.6 %collective-permute-start.16 = (bf16[4,352,256]{2,1,0:T(8,128)(2,1)}, bf16[4,352,256]{2,1,0:T(8,128)(2,1)}, u32[]{:S(2)}, u32[]{:S(2)}) collective-permute-start(bf16[4,352,256]{2,1,0:T(8,128)(2,1)} %collective-permute-done.14), channel_id=1, source_target_pairs={{0,192},{1,65},{64,128},{65,1},{128,64},{129,193},{192,0},{193,129... | collective-permute-start | bytes 2162696 | tf_op jit(solution)/shard_map/ppermute | solution.py:34
  169.2 5.3 %collective-permute-start.23 = (bf16[256,256]{1,0:T(8,128)(2,1)}, bf16[256,256]{1,0:T(8,128)(2,1)S(1)}, u32[]{:S(2)}, u32[]{:S(2)}) collective-permute-start(bf16[256,256]{1,0:T(8,128)(2,1)} %get-tuple-element.12), channel_id=1, source_target_pairs={{0,8},{1,57},{8,0},{9,17},{16,24},{17,9},{24,16},{25,33},{32,40},{... | collective-permute-start | bytes 393224 | tf_op jit(solution)/shard_map/ppermute | solution.py:34
  175.4 39.3 %copy-start.1 = (bf16[2,256,256]{2,1,0:T(8,128)(2,1)}, bf16[2,256,256]{2,1,0:T(8,128)(2,1)S(1)}, u32[]{:S(2)}) copy-start(bf16[2,256,256]{2,1,0:T(8,128)(2,1)S(1)} %pad_maximum_fusion.4.refs_0_) | copy-start | bytes 786436
  175.4 7.7 %collective-permute-start.24 = (bf16[2,256,256]{2,1,0:T(8,128)(2,1)S(1)}, bf16[2,256,256]{2,1,0:T(8,128)(2,1)S(1)}, u32[]{:S(2)}, u32[]{:S(2)}) collective-permute-start(bf16[2,256,256]{2,1,0:T(8,128)(2,1)S(1)} %pad_maximum_fusion.4.refs_0_), channel_id=1, source_target_pairs={{0,56},{1,9},{8,16},{9,1},{16,8},{17,25},{24,32},{25,17},{32,24},{... | collective-permute-start | bytes 786440 | tf_op jit(solution)/shard_map/ppermute | solution.py:34
  183.1 31.6 %copy-start.8 = (bf16[2,256,256]{2,1,0:T(8,128)(2,1)}, bf16[2,256,256]{2,1,0:T(8,128)(2,1)S(1)}, u32[]{:S(2)}) copy-start(bf16[2,256,256]{2,1,0:T(8,128)(2,1)S(1)} %collective-permute-done.24.refs_4_) | copy-start | bytes 786436
  183.1 6.4 %collective-permute-start.25 = (bf16[2,256,256]{2,1,0:T(8,128)(2,1)S(1)}, bf16[2,256,256]{2,1,0:T(8,128)(2,1)S(1)}, u32[]{:S(2)}, u32[]{:S(2)}) collective-permute-start(bf16[2,256,256]{2,1,0:T(8,128)(2,1)S(1)} %collective-permute-done.24.refs_4_), channel_id=1, source_target_pairs={{0,8},{1,57},{8,0},{9,17},{16,24},{17,9},{24,16},{25,33},{32,40},{... | collective-permute-start | bytes 786440 | tf_op jit(solution)/shard_map/ppermute | solution.py:34
  183.1 8.9 %collective-permute-start.30 = (bf16[2,256,256]{2,1,0:T(8,128)(2,1)S(1)}, bf16[2,256,256]{2,1,0:T(8,128)(2,1)S(1)}, u32[]{:S(2)}, u32[]{:S(2)}) collective-permute-start(bf16[2,256,256]{2,1,0:T(8,128)(2,1)S(1)} %pad_maximum_fusion.4.refs_0_), channel_id=1, source_target_pairs={{0,64},{1,193},{64,0},{65,129},{128,192},{129,65},{192,128},{193,1... | collective-permute-start | bytes 786440 | tf_op jit(solution)/shard_map/ppermute | solution.py:34
  184.4 10.0 %collective-permute-start.31 = (bf16[2,256,256]{2,1,0:T(8,128)(2,1)S(1)}, bf16[2,256,256]{2,1,0:T(8,128)(2,1)S(1)}, u32[]{:S(2)}, u32[]{:S(2)}) collective-permute-start(bf16[2,256,256]{2,1,0:T(8,128)(2,1)S(1)} %pad_maximum_fusion.4.refs_0_), channel_id=1, source_target_pairs={{0,192},{1,65},{64,128},{65,1},{128,64},{129,193},{192,0},{193,129... | collective-permute-start | bytes 786440 | tf_op jit(solution)/shard_map/ppermute | solution.py:34
  189.4 25.2 %copy-start.9 = (bf16[2,256,256]{2,1,0:T(8,128)(2,1)}, bf16[2,256,256]{2,1,0:T(8,128)(2,1)S(1)}, u32[]{:S(2)}) copy-start(bf16[2,256,256]{2,1,0:T(8,128)(2,1)S(1)} %collective-permute-done.25.refs_8_) | copy-start | bytes 786436
  189.4 7.6 %collective-permute-start.26 = (bf16[2,256,256]{2,1,0:T(8,128)(2,1)S(1)}, bf16[2,256,256]{2,1,0:T(8,128)(2,1)S(1)}, u32[]{:S(2)}, u32[]{:S(2)}) collective-permute-start(bf16[2,256,256]{2,1,0:T(8,128)(2,1)S(1)} %collective-permute-done.25.refs_8_), channel_id=1, source_target_pairs={{0,56},{1,9},{8,16},{9,1},{16,8},{17,25},{24,32},{25,17},{32,24},{... | collective-permute-start | bytes 786440 | tf_op jit(solution)/shard_map/ppermute | solution.py:34
  191.9 22.7 %copy-start.10 = (bf16[2,256,256]{2,1,0:T(8,128)(2,1)}, bf16[2,256,256]{2,1,0:T(8,128)(2,1)S(1)}, u32[]{:S(2)}) copy-start(bf16[2,256,256]{2,1,0:T(8,128)(2,1)S(1)} %collective-permute-done.30.refs_1_) | copy-start | bytes 786436
  191.9 9.2 %collective-permute-start.32 = (bf16[2,256,256]{2,1,0:T(8,128)(2,1)S(1)}, bf16[2,256,256]{2,1,0:T(8,128)(2,1)S(1)}, u32[]{:S(2)}, u32[]{:S(2)}) collective-permute-start(bf16[2,256,256]{2,1,0:T(8,128)(2,1)S(1)} %collective-permute-done.30.refs_1_), channel_id=1, source_target_pairs={{0,192},{1,65},{64,128},{65,1},{128,64},{129,193},{192,0},{193,129... | collective-permute-start | bytes 786440 | tf_op jit(solution)/shard_map/ppermute | solution.py:34
  192.1 9.6 %collective-permute-start.33 = (bf16[2,256,256]{2,1,0:T(8,128)(2,1)S(1)}, bf16[2,256,256]{2,1,0:T(8,128)(2,1)S(1)}, u32[]{:S(2)}, u32[]{:S(2)}) collective-permute-start(bf16[2,256,256]{2,1,0:T(8,128)(2,1)S(1)} %collective-permute-done.24.refs_4_), channel_id=1, source_target_pairs={{0,64},{1,193},{64,0},{65,129},{128,192},{129,65},{192,128},{193,1... | collective-permute-start | bytes 786440 | tf_op jit(solution)/shard_map/ppermute | solution.py:34
  194.4 12.8 %collective-permute-start.36 = (bf16[2,256,256]{2,1,0:T(8,128)(2,1)S(1)}, bf16[2,256,256]{2,1,0:T(8,128)(2,1)S(1)}, u32[]{:S(2)}, u32[]{:S(2)}) collective-permute-start(bf16[2,256,256]{2,1,0:T(8,128)(2,1)S(1)} %collective-permute-done.25.refs_8_), channel_id=1, source_target_pairs={{0,64},{1,193},{64,0},{65,129},{128,192},{129,65},{192,128},{193,1... | collective-permute-start | bytes 786440 | tf_op jit(solution)/shard_map/ppermute | solution.py:34
  194.5 20.2 %copy-start.11 = (bf16[2,256,256]{2,1,0:T(8,128)(2,1)}, bf16[2,256,256]{2,1,0:T(8,128)(2,1)S(1)}, u32[]{:S(2)}) copy-start(bf16[2,256,256]{2,1,0:T(8,128)(2,1)S(1)} %collective-permute-done.31.refs_2_) | copy-start | bytes 786436
  194.5 14.5 %collective-permute-start.34 = (bf16[2,256,256]{2,1,0:T(8,128)(2,1)S(1)}, bf16[2,256,256]{2,1,0:T(8,128)(2,1)S(1)}, u32[]{:S(2)}, u32[]{:S(2)}) collective-permute-start(bf16[2,256,256]{2,1,0:T(8,128)(2,1)S(1)} %collective-permute-done.24.refs_4_), channel_id=1, source_target_pairs={{0,192},{1,65},{64,128},{65,1},{128,64},{129,193},{192,0},{193,129... | collective-permute-start | bytes 786440 | tf_op jit(solution)/shard_map/ppermute | solution.py:34
  197.0 23.2 %copy-start.3 = (bf16[2,256,256]{2,1,0:T(8,128)(2,1)}, bf16[2,256,256]{2,1,0:T(8,128)(2,1)S(1)}, u32[]{:S(2)}) copy-start(bf16[2,256,256]{2,1,0:T(8,128)(2,1)S(1)} %collective-permute-done.26.refs_0_) | copy-start | bytes 786436
  197.0 15.9 %collective-permute-start.27 = (bf16[2,256,256]{2,1,0:T(8,128)(2,1)S(1)}, bf16[2,256,256]{2,1,0:T(8,128)(2,1)S(1)}, u32[]{:S(2)}, u32[]{:S(2)}) collective-permute-start(bf16[2,256,256]{2,1,0:T(8,128)(2,1)S(1)} %collective-permute-done.26.refs_0_), channel_id=1, source_target_pairs={{0,64},{1,193},{64,0},{65,129},{128,192},{129,65},{192,128},{193,1... | collective-permute-start | bytes 786440 | tf_op jit(solution)/shard_map/ppermute | solution.py:34
  201.2 13.5 %copy-start.12 = (bf16[2,256,256]{2,1,0:T(8,128)(2,1)}, bf16[2,256,256]{2,1,0:T(8,128)(2,1)S(1)}, u32[]{:S(2)}) copy-start(bf16[2,256,256]{2,1,0:T(8,128)(2,1)S(1)} %collective-permute-done.32.refs_3_) | copy-start | bytes 786436
  201.2 13.4 %collective-permute-start.37 = (bf16[2,256,256]{2,1,0:T(8,128)(2,1)S(1)}, bf16[2,256,256]{2,1,0:T(8,128)(2,1)S(1)}, u32[]{:S(2)}, u32[]{:S(2)}) collective-permute-start(bf16[2,256,256]{2,1,0:T(8,128)(2,1)S(1)} %collective-permute-done.25.refs_8_), channel_id=1, source_target_pairs={{0,192},{1,65},{64,128},{65,1},{128,64},{129,193},{192,0},{193,129... | collective-permute-start | bytes 786440 | tf_op jit(solution)/shard_map/ppermute | solution.py:34
  201.7 13.0 %copy-start.13 = (bf16[2,256,256]{2,1,0:T(8,128)(2,1)}, bf16[2,256,256]{2,1,0:T(8,128)(2,1)S(1)}, u32[]{:S(2)}) copy-start(bf16[2,256,256]{2,1,0:T(8,128)(2,1)S(1)} %collective-permute-done.33.refs_5_) | copy-start | bytes 786436
  201.7 13.0 %collective-permute-start.35 = (bf16[2,256,256]{2,1,0:T(8,128)(2,1)S(1)}, bf16[2,256,256]{2,1,0:T(8,128)(2,1)S(1)}, u32[]{:S(2)}, u32[]{:S(2)}) collective-permute-start(bf16[2,256,256]{2,1,0:T(8,128)(2,1)S(1)} %collective-permute-done.33.refs_5_), channel_id=1, source_target_pairs={{0,192},{1,65},{64,128},{65,1},{128,64},{129,193},{192,0},{193,129... | collective-permute-start | bytes 786440 | tf_op jit(solution)/shard_map/ppermute | solution.py:34
  207.3 7.4 %copy-start.14 = (bf16[2,256,256]{2,1,0:T(8,128)(2,1)}, bf16[2,256,256]{2,1,0:T(8,128)(2,1)S(1)}, u32[]{:S(2)}) copy-start(bf16[2,256,256]{2,1,0:T(8,128)(2,1)S(1)} %collective-permute-done.36.refs_9_) | copy-start | bytes 786436
  207.3 7.4 %collective-permute-start.38 = (bf16[2,256,256]{2,1,0:T(8,128)(2,1)S(1)}, bf16[2,256,256]{2,1,0:T(8,128)(2,1)S(1)}, u32[]{:S(2)}, u32[]{:S(2)}) collective-permute-start(bf16[2,256,256]{2,1,0:T(8,128)(2,1)S(1)} %collective-permute-done.36.refs_9_), channel_id=1, source_target_pairs={{0,192},{1,65},{64,128},{65,1},{128,64},{129,193},{192,0},{193,129... | collective-permute-start | bytes 786440 | tf_op jit(solution)/shard_map/ppermute | solution.py:34
  209.0 5.7 %copy-start.15 = (bf16[2,256,256]{2,1,0:T(8,128)(2,1)}, bf16[2,256,256]{2,1,0:T(8,128)(2,1)S(1)}, u32[]{:S(2)}) copy-start(bf16[2,256,256]{2,1,0:T(8,128)(2,1)S(1)} %collective-permute-done.34.refs_6_) | copy-start | bytes 786436
  209.0 11.1 %collective-permute-start.28 = (bf16[2,256,256]{2,1,0:T(8,128)(2,1)S(1)}, bf16[2,256,256]{2,1,0:T(8,128)(2,1)S(1)}, u32[]{:S(2)}, u32[]{:S(2)}) collective-permute-start(bf16[2,256,256]{2,1,0:T(8,128)(2,1)S(1)} %collective-permute-done.26.refs_0_), channel_id=1, source_target_pairs={{0,192},{1,65},{64,128},{65,1},{128,64},{129,193},{192,0},{193,129... | collective-permute-start | bytes 786440 | tf_op jit(solution)/shard_map/ppermute | solution.py:34
  212.9 7.4 %copy-start.4 = (bf16[2,256,256]{2,1,0:T(8,128)(2,1)}, bf16[2,256,256]{2,1,0:T(8,128)(2,1)S(1)}, u32[]{:S(2)}) copy-start(bf16[2,256,256]{2,1,0:T(8,128)(2,1)S(1)} %collective-permute-done.27.refs_1_) | copy-start | bytes 786436
  212.9 7.4 %collective-permute-start.29 = (bf16[2,256,256]{2,1,0:T(8,128)(2,1)S(1)}, bf16[2,256,256]{2,1,0:T(8,128)(2,1)S(1)}, u32[]{:S(2)}, u32[]{:S(2)}) collective-permute-start(bf16[2,256,256]{2,1,0:T(8,128)(2,1)S(1)} %collective-permute-done.27.refs_1_), channel_id=1, source_target_pairs={{0,192},{1,65},{64,128},{65,1},{128,64},{129,193},{192,0},{193,129... | collective-permute-start | bytes 786440 | tf_op jit(solution)/shard_map/ppermute | solution.py:34
  (5 other events, 3.6 us)

commit v3 on v2

--- a/solution.py
+++ b/solution.py
@@ -113,7 +113,7 @@
             if kz < 2 * part + 2 and no not in waited:
                 loads[no].wait()
                 waited.add(no)
-        lax.fori_loop(part * 2 * NX, (part + 1) * 2 * NX, multiply, 0, unroll=2)
+        lax.fori_loop(part * 2 * NX, (part + 1) * 2 * NX, multiply, 0, unroll=8)
         at = pl.ds(part * 2 * NX, 2 * NX)
         outs.append(pltpu.make_async_copy(gv.at[at], g_hbm.at[at], gsem.at[part]))
         outs[-1].start()
@@ -126,7 +126,7 @@
         both = jnp.concatenate([high, low], axis=0)
         return total + lax.dot_general(high, both, (((1,), (1,)), ((), ())), preferred_element_type=F32)
 
-    total = lax.fori_loop(0, BLK // 32, add, jnp.zeros((BLK, 2 * BLK), F32))
+    total = lax.fori_loop(0, BLK // 32, add, jnp.zeros((BLK, 2 * BLK), F32), unroll=4)
     cross = total[:, BLK:]
     total = total[:, :BLK] + cross + cross.T
     i = lax.broadcasted_iota(jnp.int32, (BLK, BLK), 0)
@@ -233,7 +233,7 @@
             total[at, :] = total[at, :] + part if no else part
             return 0
 
-        lax.fori_loop(0, BLK // 32, strip, 0, unroll=2)
+        lax.fori_loop(0, BLK // 32, strip, 0, unroll=8)
 
     combined = total[...]
     new_one = 0.9 * one_ref[...] + 0.1 * combined

time: 226 us -> 222 us (0.982)
  Pallas kernels: 31.4 us -> 26.9 us
    pallas_call x1, Pallas kernels: 18.4 us -> 13.9 us  [grads_and_sums(): pl.pallas_call(functools.partial(grads_kernel, layout), out_shape=(jax.Sh...]
where the time goes in v3:
time: 222 us; the launch traced here: 220 us
  waiting for transfers between devices  80.1 us (36%)
  starting transfers between devices  61.8 us (28%)
  blocking collectives  38.9 us (18%)
  Pallas kernels  26.9 us (12%)
  local copies, waits for them, and re-layouts  7.53 us (3%)
  other arithmetic  2.8 us (1%)
    ppermute x35, waiting for transfers between devices, near(): return lax.ppermute(array, (axis, 'c'), pairs)  80.1 us
    ppermute x35, starting transfers between devices, near(): return lax.ppermute(array, (axis, 'c'), pairs)  49.7 us
    all_to_all x1, blocking collectives, totals_of_groups(): sums = jnp.sum(lax.all_to_all(sums, ('x', 'y'), 0, 0), axis=0)  15 us
    all_to_all x1, blocking collectives, totals_of_groups(): lax.all_to_all(jnp.broadcast_to(sums[None], (NZ * NC,) + sums.shape), ('z...  14.4 us
    pallas_call x1, Pallas kernels, grads_and_sums(): pl.pallas_call(functools.partial(grads_kernel, layout), out_shape=(jax.Sh...  13.9 us
    all_to_all x1, starting transfers between devices, local(): lax.all_to_all(token_rows, ('x', 'z'), 1, 0, tiled=True)  11.6 us
    unnamed x1, blocking collectives  9.48 us
    pallas_call x2, Pallas kernels, place_rows(): pl.pallas_call(functools.partial(place_kernel, first, count), out_shape=j...  6.69 us
  transfers between devices with their start and end apart: 40, of which 23 were waited for; matrix products, arithmetic and copies ran while one was open for 2% of the time, Pallas kernels for 2%

profile of v3, /device:TPU:4, one launch (start us, length us, event | category | flops | bytes accessed | tf_op | source)
XLA Modules:
  0.0 219.9 jit_solution(10311519134223411131)
XLA Ops:
  0.7 2.4 %copy.30 = bf16[8,32,8,256]{3,2,0,1:T(8,128)(2,1)} copy(bf16[8,32,8,256]{3,2,1,0:T(8,128)(2,1)} %bitcast.53) | data formatting | bytes 2097152 | tf_op jit(solution)/shard_map/all_to_all | solution.py:323
  3.0 11.6 %all-to-all-start = ((bf16[64,32,256]{2,0,1:T(8,128)(2,1)}), bf16[64,32,256]{2,0,1:T(8,128)(2,1)S(1)}, u32[]{:S(2)}, u32[]{:S(2)}) async-start(bf16[64,32,256]{2,0,1:T(8,128)(2,1)} %bitcast.51), calls=%async_computation | async-start | bytes 2097152 | tf_op jit(solution)/shard_map/all_to_all | solution.py:323
  14.6 0.6 dynamic-slice
  16.2 9.5 %all-reduce = s32[512]{0:T(512)S(1)} all-reduce(s32[512]{0:T(512)S(1)} %dynamic-update-slice), channel_id=1, replica_groups=mesh['x'=4,'z'=8,'y'=4,'c'=2] {'y','c'}, use_global_device_ids=true, to_apply=%add | all-reduce | flops 512 | bytes 4096
  25.6 0.6 fusion
  26.4 1.3 collective-permute-start.17
  27.7 3.8 %collective-permute-done.17 = bf16[160,256]{1,0:T(8,128)(2,1)S(1)} collective-permute-done((bf16[160,256]{1,0:T(8,128)(2,1)S(1)}, bf16[160,256]{1,0:T(8,128)(2,1)S(1)}, u32[]{:S(2)}, u32[]{:S(2)}) %collective-permute-start.17) | collective-permute-done | bytes 81952 | tf_op jit(solution)/shard_map/ppermute | solution.py:34
  31.4 1.4 collective-permute-start.18
  32.9 0.8 collective-permute-start.7
  33.7 4.5 %collective-permute-done.18 = bf16[2,160,256]{2,1,0:T(8,128)(2,1)S(1)} collective-permute-done((bf16[2,160,256]{2,1,0:T(8,128)(2,1)S(1)}, bf16[2,160,256]{2,1,0:T(8,128)(2,1)S(1)}, u32[]{:S(2)}, u32[]{:S(2)}) %collective-permute-start.18) | collective-permute-done | bytes 163872 | tf_op jit(solution)/shard_map/ppermute | solution.py:34
  38.2 1.9 collective-permute-start.19
  40.1 0.7 collective-permute-done.7
  40.8 2.8 %collective-permute-start.8 = (bf16[2,352,256]{2,1,0:T(8,128)(2,1)S(1)}, bf16[2,352,256]{2,1,0:T(8,128)(2,1)S(1)}, u32[]{:S(2)}, u32[]{:S(2)}) collective-permute-start(bf16[2,352,256]{2,1,0:T(8,128)(2,1)S(1)} %pad_maximum_fusion.2), channel_id=1, source_target_pairs={{0,56},{1,9},{8,16},{9,1},{16,8},{17,25},{24,32},{25,17},{32,24},{... | collective-permute-start | bytes 1081352 | tf_op jit(solution)/shard_map/ppermute | solution.py:34
  43.6 1.5 collective-permute-start
  45.1 1.6 collective-permute-done.19
  46.8 4.8 %collective-permute-start.20 = (bf16[2,4,160,256]{3,2,1,0:T(8,128)(2,1)S(1)}, bf16[2,4,160,256]{3,2,1,0:T(8,128)(2,1)S(1)}, u32[]{:S(2)}, u32[]{:S(2)}) collective-permute-start(bf16[2,4,160,256]{3,2,1,0:T(8,128)(2,1)S(1)} %pad_maximum_fusion.1.refs_16_), channel_id=1, source_target_pairs={{0,56},{1,9},{8,16},{9,1},{16,8},{17,25},{24,32},{25,17},{32,24},{... | collective-permute-start | bytes 1966088 | tf_op jit(solution)/shard_map/ppermute | solution.py:34
  51.6 1.0 pad_maximum_fusion
  52.5 2.3 %collective-permute-start.9 = (bf16[4,352,256]{2,1,0:T(8,128)(2,1)S(1)}, bf16[4,352,256]{2,1,0:T(8,128)(2,1)S(1)}, u32[]{:S(2)}, u32[]{:S(2)}) collective-permute-start(bf16[4,352,256]{2,1,0:T(8,128)(2,1)S(1)} %get-tuple-element.16), channel_id=1, source_target_pairs={{0,64},{1,193},{64,0},{65,129},{128,192},{129,65},{192,128},{193,1... | collective-permute-start | bytes 2162696 | tf_op jit(solution)/shard_map/ppermute | solution.py:34
  54.8 5.3 %collective-permute-done.12 = bf16[2,352,256]{2,1,0:T(8,128)(2,1)S(1)} collective-permute-done((bf16[2,352,256]{2,1,0:T(8,128)(2,1)S(1)}, bf16[2,352,256]{2,1,0:T(8,128)(2,1)S(1)}, u32[]{:S(2)}, u32[]{:S(2)}) %collective-permute-start.12) | collective-permute-done | bytes 360480 | tf_op jit(solution)/shard_map/ppermute | solution.py:34
  60.1 3.1 %collective-permute-start.13 = (bf16[2,352,256]{2,1,0:T(8,128)(2,1)S(1)}, bf16[2,352,256]{2,1,0:T(8,128)(2,1)S(1)}, u32[]{:S(2)}, u32[]{:S(2)}) collective-permute-start(bf16[2,352,256]{2,1,0:T(8,128)(2,1)S(1)} %collective-permute-done.12), channel_id=1, source_target_pairs={{0,56},{1,9},{8,16},{9,1},{16,8},{17,25},{24,32},{25,17},{32,24},{... | collective-permute-start | bytes 1081352 | tf_op jit(solution)/shard_map/ppermute | solution.py:34
  64.0 6.6 %collective-permute-done.13 = bf16[2,352,256]{2,1,0:T(8,128)(2,1)S(1)} collective-permute-done((bf16[2,352,256]{2,1,0:T(8,128)(2,1)S(1)}, bf16[2,352,256]{2,1,0:T(8,128)(2,1)S(1)}, u32[]{:S(2)}, u32[]{:S(2)}) %collective-permute-start.13) | collective-permute-done | bytes 360480 | tf_op jit(solution)/shard_map/ppermute | solution.py:34
  70.6 3.1 %collective-permute-start.15 = (bf16[4,352,256]{2,1,0:T(8,128)(2,1)S(1)}, bf16[4,352,256]{2,1,0:T(8,128)(2,1)S(1)}, u32[]{:S(2)}, u32[]{:S(2)}) collective-permute-start(bf16[4,352,256]{2,1,0:T(8,128)(2,1)S(1)} %constant_dynamic-update-slice_fusion), channel_id=1, source_target_pairs={{0,192},{1,65},{64,128},{65,1},{128,64},{129,193},{192,0},{193,129... | collective-permute-start | bytes 2162696 | tf_op jit(solution)/shard_map/ppermute | solution.py:34
  73.8 1.7 collective-permute-start.1
  75.5 1.5 collective-permute-start.2
  77.0 1.9 collective-permute-start.14
  78.9 2.5 %collective-permute-start.11 = (bf16[4,352,256]{2,1,0:T(8,128)(2,1)S(1)}, bf16[4,352,256]{2,1,0:T(8,128)(2,1)S(1)}, u32[]{:S(2)}, u32[]{:S(2)}) collective-permute-start(bf16[4,352,256]{2,1,0:T(8,128)(2,1)S(1)} %collective-permute-done.9), channel_id=1, source_target_pairs={{0,192},{1,65},{64,128},{65,1},{128,64},{129,193},{192,0},{193,129... | collective-permute-start | bytes 2162696 | tf_op jit(solution)/shard_map/ppermute | solution.py:34
  81.5 9.2 %collective-permute-done.15 = bf16[4,352,256]{2,1,0:T(8,128)(2,1)S(1)} collective-permute-done((bf16[4,352,256]{2,1,0:T(8,128)(2,1)S(1)}, bf16[4,352,256]{2,1,0:T(8,128)(2,1)S(1)}, u32[]{:S(2)}, u32[]{:S(2)}) %collective-permute-start.15) | collective-permute-done | bytes 720928 | tf_op jit(solution)/shard_map/ppermute | solution.py:34
  90.7 2.5 %collective-permute-start.22 = (bf16[2,4,160,256]{3,2,1,0:T(8,128)(2,1)S(1)}, bf16[2,4,160,256]{3,2,1,0:T(8,128)(2,1)S(1)}, u32[]{:S(2)}, u32[]{:S(2)}) collective-permute-start(bf16[2,4,160,256]{3,2,1,0:T(8,128)(2,1)S(1)} %collective-permute-done.21.refs_18_), channel_id=1, source_target_pairs={{0,56},{1,9},{8,16},{9,1},{16,8},{17,25},{24,32},{25,17},{32,24},{... | collective-permute-start | bytes 1966088 | tf_op jit(solution)/shard_map/ppermute | solution.py:34
  93.1 2.6 %collective-permute-done.14 = bf16[4,352,256]{2,1,0:T(8,128)(2,1)} collective-permute-done((bf16[4,352,256]{2,1,0:T(8,128)(2,1)S(1)}, bf16[4,352,256]{2,1,0:T(8,128)(2,1)}, u32[]{:S(2)}, u32[]{:S(2)}) %collective-permute-start.14) | collective-permute-done | bytes 720928 | tf_op jit(solution)/shard_map/ppermute | solution.py:34
  95.8 2.6 %collective-permute-done.11 = bf16[4,352,256]{2,1,0:T(8,128)(2,1)S(1)} collective-permute-done((bf16[4,352,256]{2,1,0:T(8,128)(2,1)S(1)}, bf16[4,352,256]{2,1,0:T(8,128)(2,1)S(1)}, u32[]{:S(2)}, u32[]{:S(2)}) %collective-permute-start.11) | collective-permute-done | bytes 720928 | tf_op jit(solution)/shard_map/ppermute | solution.py:34
  98.9 2.2 %collective-permute-done.2.refs_3_ = bf16[32,64,256]{2,1,0:T(8,128)(2,1)} collective-permute-done((bf16[32,64,256]{2,1,0:T(8,128)(2,1)}, bf16[32,64,256]{2,1,0:T(8,128)(2,1)}, u32[]{:S(2)}, u32[]{:S(2)}) %collective-permute-start.2) | collective-permute-done | bytes 1048608 | tf_op jit(solution)/shard_map/ppermute | solution.py:34
  101.1 1.3 collective-permute-done.22.refs_19_
  102.5 0.9 copy-done.26
  103.3 0.6 collective-permute-start.16
  104.0 0.7 stack.67.place
  104.6 10.3 %collective-permute-done.16 = bf16[4,352,256]{2,1,0:T(8,128)(2,1)} collective-permute-done((bf16[4,352,256]{2,1,0:T(8,128)(2,1)}, bf16[4,352,256]{2,1,0:T(8,128)(2,1)}, u32[]{:S(2)}, u32[]{:S(2)}) %collective-permute-start.16) | collective-permute-done | bytes 720928 | tf_op jit(solution)/shard_map/ppermute | solution.py:34
  115.0 13.9 %shard_map.93 = (f32[32,256,256]{2,1,0:T(8,128)}, f32[16,16,128]{2,1,0:T(8,128)}) custom-call(s32[7]{0:T(128)} %stack.67.place, bf16[32,64,256]{2,1,0:T(8,128)(2,1)} %bitcast.57, bf16[32,64,256]{2,1,0:T(8,128)(2,1)} %collective-permute-done.refs_1_, bf16[32,64,256]{2,1,0:T(8,128)(2,1)} %collective-permute-done.1.refs_2_, ...), custom_call_target="tpu_custom_call" | custom-call | flops 6000000000 | bytes 25165824 | tf_op jit(solution)/shard_map/pallas_call | solution.py:158
  128.9 15.0 %all_to_all.26 = f32[16,16,128]{2,1,0:T(8,128)S(1)} all-to-all(f32[16,16,128]{2,1,0:T(8,128)} %get-tuple-element.10), channel_id=1, replica_groups=mesh['x'=4,'z'=8,'y'=4,'c'=2] {'x','y'}, dimensions={0} | all-to-all | bytes 262144 | tf_op jit(solution)/shard_map/all_to_all | solution.py:308
  144.0 14.4 %all_to_all.27.sums_ref = f32[16,16,128]{2,1,0:T(8,128)} all-to-all(f32[16,16,128]{2,1,0:T(8,128)S(1)} %broadcast_in_dim.39), channel_id=1, replica_groups=mesh['x'=4,'z'=8,'y'=4,'c'=2] {'z','c'}, dimensions={0} | all-to-all | bytes 262144 | tf_op jit(solution)/shard_map/all_to_all | solution.py:309
  158.4 6.2 %shard_map.94 = (bf16[256,256]{1,0:T(8,128)(2,1)}, f32[256,256]{1,0:T(8,128)}, f32[256,256]{1,0:T(8,128)}, f32[256,256]{1,0:T(8,128)}) custom-call(s32[7]{0:T(128)} %stack.67.place, f32[16,16,128]{2,1,0:T(8,128)} %all_to_all.27.sums_ref, f32[32,256,256]{2,1,0:T(8,128)} %get-tuple-element.11.g_hbm, f32[256,256]{1,0:T(8,128)} %master_ref.1, ...), custom_call_target="tpu_custom_call" | custom-call | flops 5000000 | bytes 10485760 | tf_op jit(solution)/shard_map/pallas_call | solution.py:254
  164.7 0.6 collective-permute-start.23
  165.3 4.6 %collective-permute-done.23 = bf16[256,256]{1,0:T(8,128)(2,1)S(1)} collective-permute-done((bf16[256,256]{1,0:T(8,128)(2,1)}, bf16[256,256]{1,0:T(8,128)(2,1)S(1)}, u32[]{:S(2)}, u32[]{:S(2)}) %collective-permute-start.23) | collective-permute-done | bytes 131104 | tf_op jit(solution)/shard_map/ppermute | solution.py:34
  169.9 0.9 pad_maximum_fusion.4.refs_0_
  171.1 7.4 %collective-permute-done.24.refs_4_ = bf16[2,256,256]{2,1,0:T(8,128)(2,1)S(1)} collective-permute-done((bf16[2,256,256]{2,1,0:T(8,128)(2,1)S(1)}, bf16[2,256,256]{2,1,0:T(8,128)(2,1)S(1)}, u32[]{:S(2)}, u32[]{:S(2)}) %collective-permute-start.24) | collective-permute-done | bytes 262176 | tf_op jit(solution)/shard_map/ppermute | solution.py:34
  178.5 1.4 collective-permute-start.30
  179.9 1.5 collective-permute-start.31
  181.4 3.5 %collective-permute-done.25.refs_8_ = bf16[2,256,256]{2,1,0:T(8,128)(2,1)S(1)} collective-permute-done((bf16[2,256,256]{2,1,0:T(8,128)(2,1)S(1)}, bf16[2,256,256]{2,1,0:T(8,128)(2,1)S(1)}, u32[]{:S(2)}, u32[]{:S(2)}) %collective-permute-start.25) | collective-permute-done | bytes 262176 | tf_op jit(solution)/shard_map/ppermute | solution.py:34
  185.1 2.4 %collective-permute-done.30.refs_1_ = bf16[2,256,256]{2,1,0:T(8,128)(2,1)S(1)} collective-permute-done((bf16[2,256,256]{2,1,0:T(8,128)(2,1)S(1)}, bf16[2,256,256]{2,1,0:T(8,128)(2,1)S(1)}, u32[]{:S(2)}, u32[]{:S(2)}) %collective-permute-start.30) | collective-permute-done | bytes 262176 | tf_op jit(solution)/shard_map/ppermute | solution.py:34
  187.6 2.3 %collective-permute-start.33 = (bf16[2,256,256]{2,1,0:T(8,128)(2,1)S(1)}, bf16[2,256,256]{2,1,0:T(8,128)(2,1)S(1)}, u32[]{:S(2)}, u32[]{:S(2)}) collective-permute-start(bf16[2,256,256]{2,1,0:T(8,128)(2,1)S(1)} %collective-permute-done.24.refs_4_), channel_id=1, source_target_pairs={{0,64},{1,193},{64,0},{65,129},{128,192},{129,65},{192,128},{193,1... | collective-permute-start | bytes 786440 | tf_op jit(solution)/shard_map/ppermute | solution.py:34
  190.0 1.8 collective-permute-start.34
  191.7 0.8 collective-permute-done.26.refs_0_
  192.5 1.8 collective-permute-start.27
  194.3 2.4 %collective-permute-done.32.refs_3_ = bf16[2,256,256]{2,1,0:T(8,128)(2,1)S(1)} collective-permute-done((bf16[2,256,256]{2,1,0:T(8,128)(2,1)S(1)}, bf16[2,256,256]{2,1,0:T(8,128)(2,1)S(1)}, u32[]{:S(2)}, u32[]{:S(2)}) %collective-permute-start.32) | collective-permute-done | bytes 262176 | tf_op jit(solution)/shard_map/ppermute | solution.py:34
  197.1 1.7 collective-permute-start.35
  198.9 3.9 %collective-permute-done.36.refs_9_ = bf16[2,256,256]{2,1,0:T(8,128)(2,1)S(1)} collective-permute-done((bf16[2,256,256]{2,1,0:T(8,128)(2,1)S(1)}, bf16[2,256,256]{2,1,0:T(8,128)(2,1)S(1)}, u32[]{:S(2)}, u32[]{:S(2)}) %collective-permute-start.36) | collective-permute-done | bytes 262176 | tf_op jit(solution)/shard_map/ppermute | solution.py:34
  202.8 1.7 collective-permute-start.38
  204.8 3.6 %collective-permute-done.27.refs_1_ = bf16[2,256,256]{2,1,0:T(8,128)(2,1)S(1)} collective-permute-done((bf16[2,256,256]{2,1,0:T(8,128)(2,1)S(1)}, bf16[2,256,256]{2,1,0:T(8,128)(2,1)S(1)}, u32[]{:S(2)}, u32[]{:S(2)}) %collective-permute-start.27) | collective-permute-done | bytes 262176 | tf_op jit(solution)/shard_map/ppermute | solution.py:34
  208.4 1.7 collective-permute-start.29
  210.2 0.6 copy-done.17
  210.9 0.7 copy-done.18
  211.6 3.9 %shard_map.95.refs_4_ = bf16[32,256,256]{2,1,0:T(8,128)(2,1)} custom-call(s32[7]{0:T(128)} %stack.67.place, bf16[2,256,256]{2,1,0:T(8,128)(2,1)} %copy-done.1, bf16[2,256,256]{2,1,0:T(8,128)(2,1)} %copy-done.10, bf16[2,256,256]{2,1,0:T(8,128)(2,1)} %copy-done.11, bf16[2,256,256]{2,1,0:T(8,128)(2,1)} %copy-done.12, bf16[2,256,256]{2,1,0:T(8,128)(2,1)} %copy-done.8, ...), custom_call_target="tpu_custom_call" | custom-call | bytes 3145728 | tf_op jit(solution)/shard_map/pallas_call | solution.py:291
  215.7 0.5 copy-done.5
  216.3 0.7 copy-done.6
  217.0 2.8 %shard_map.96 = bf16[32,256,256]{2,1,0:T(8,128)(2,1)} custom-call(s32[7]{0:T(128)} %stack.67.place, bf16[2,256,256]{2,1,0:T(8,128)(2,1)} %copy-done.3, bf16[2,256,256]{2,1,0:T(8,128)(2,1)} %copy-done.4, bf16[2,256,256]{2,1,0:T(8,128)(2,1)} %copy-done.5, bf16[2,256,256]{2,1,0:T(8,128)(2,1)} %copy-done.6, ...), custom_call_target="tpu_custom_call", output_to_operand_aliasing={{}: (5, {})} | custom-call | bytes 1048576 | tf_op jit(solution)/shard_map/pallas_call | solution.py:291
  (100 shorter events, 3.6 us)
Async XLA Ops:
  0.6 14.0 %copy-start.28 = (u32[256]{0:T(256)S(1)}, u32[256]{0:T(256)}, u32[]{:S(2)}) copy-start(u32[256]{0:T(256)} %constant.46) | copy-start | bytes 3076
  0.6 15.3 %copy-start.27 = (s32[64]{0:T(128)S(1)}, s32[64]{0:T(128)}, u32[]{:S(2)}) copy-start(s32[64]{0:T(128)} %param.7) | copy-start | bytes 772
  0.7 25.6 %copy-start.7 = (bf16[512,256]{1,0:T(8,128)(2,1)S(1)}, bf16[512,256]{1,0:T(8,128)(2,1)}, u32[]{:S(2)}) copy-start(bf16[512,256]{1,0:T(8,128)(2,1)} %param.8) | copy-start | bytes 786436
  3.0 40.6 %all-to-all-start = ((bf16[64,32,256]{2,0,1:T(8,128)(2,1)}), bf16[64,32,256]{2,0,1:T(8,128)(2,1)S(1)}, u32[]{:S(2)}, u32[]{:S(2)}) async-start(bf16[64,32,256]{2,0,1:T(8,128)(2,1)} %bitcast.51), calls=%async_computation | async-start | bytes 2097152 | tf_op jit(solution)/shard_map/all_to_all | solution.py:323
  26.4 5.0 %collective-permute-start.17 = (bf16[160,256]{1,0:T(8,128)(2,1)S(1)}, bf16[160,256]{1,0:T(8,128)(2,1)S(1)}, u32[]{:S(2)}, u32[]{:S(2)}) collective-permute-start(bf16[160,256]{1,0:T(8,128)(2,1)S(1)} %get-tuple-element.21), channel_id=1, source_target_pairs={{0,64},{1,193},{64,0},{65,129},{128,192},{129,65},{192,128},{193,1... | collective-permute-start | bytes 245768 | tf_op jit(solution)/shard_map/ppermute | solution.py:34
  31.4 6.7 %collective-permute-start.18 = (bf16[2,160,256]{2,1,0:T(8,128)(2,1)S(1)}, bf16[2,160,256]{2,1,0:T(8,128)(2,1)S(1)}, u32[]{:S(2)}, u32[]{:S(2)}) collective-permute-start(bf16[2,160,256]{2,1,0:T(8,128)(2,1)S(1)} %pad_maximum_fusion.5), channel_id=1, source_target_pairs={{0,192},{1,65},{64,128},{65,1},{128,64},{129,193},{192,0},{193,129... | collective-permute-start | bytes 491528 | tf_op jit(solution)/shard_map/ppermute | solution.py:34
  32.9 7.9 %collective-permute-start.7 = (bf16[352,256]{1,0:T(8,128)(2,1)S(1)}, bf16[352,256]{1,0:T(8,128)(2,1)S(1)}, u32[]{:S(2)}, u32[]{:S(2)}) collective-permute-start(bf16[352,256]{1,0:T(8,128)(2,1)S(1)} %get-tuple-element.23), channel_id=1, source_target_pairs={{0,8},{1,57},{8,0},{9,17},{16,24},{17,9},{24,16},{25,33},{32,40},{... | collective-permute-start | bytes 540680 | tf_op jit(solution)/shard_map/ppermute | solution.py:34
  38.2 8.5 %collective-permute-start.19 = (bf16[4,160,256]{2,1,0:T(8,128)(2,1)S(1)}, bf16[4,160,256]{2,1,0:T(8,128)(2,1)S(1)}, u32[]{:S(2)}, u32[]{:S(2)}) collective-permute-start(bf16[4,160,256]{2,1,0:T(8,128)(2,1)S(1)} %get-tuple-element.19), channel_id=1, source_target_pairs={{0,8},{1,57},{8,0},{9,17},{16,24},{17,9},{24,16},{25,33},{32,40},{... | collective-permute-start | bytes 983048 | tf_op jit(solution)/shard_map/ppermute | solution.py:34
  40.8 10.8 %collective-permute-start.8 = (bf16[2,352,256]{2,1,0:T(8,128)(2,1)S(1)}, bf16[2,352,256]{2,1,0:T(8,128)(2,1)S(1)}, u32[]{:S(2)}, u32[]{:S(2)}) collective-permute-start(bf16[2,352,256]{2,1,0:T(8,128)(2,1)S(1)} %pad_maximum_fusion.2), channel_id=1, source_target_pairs={{0,56},{1,9},{8,16},{9,1},{16,8},{17,25},{24,32},{25,17},{32,24},{... | collective-permute-start | bytes 1081352 | tf_op jit(solution)/shard_map/ppermute | solution.py:34
  43.6 71.4 %copy-start = (bf16[64,32,256]{2,0,1:T(8,128)(2,1)}, bf16[64,32,256]{2,0,1:T(8,128)(2,1)S(1)}, u32[]{:S(2)}) copy-start(bf16[64,32,256]{2,0,1:T(8,128)(2,1)S(1)} %all-to-all-done) | copy-start | bytes 3145732
  43.6 31.9 %collective-permute-start = (bf16[32,64,256]{2,1,0:T(8,128)(2,1)S(1)}, bf16[32,64,256]{2,1,0:T(8,128)(2,1)}, u32[]{:S(2)}, u32[]{:S(2)}) collective-permute-start(bf16[32,64,256]{2,1,0:T(8,128)(2,1)S(1)} %bitcast.54), channel_id=1, source_target_pairs={{0,2},{1,7},{2,0},{3,5},{4,6},{5,3},{6,4},{7,1},{8,10},{9,15},{10,... | collective-permute-start | bytes 3145736 | tf_op jit(solution)/shard_map/ppermute | solution.py:34
  46.8 68.2 %copy-start.2 = (bf16[2,4,160,256]{3,2,1,0:T(8,128)(2,1)}, bf16[2,4,160,256]{3,2,1,0:T(8,128)(2,1)S(1)}, u32[]{:S(2)}) copy-start(bf16[2,4,160,256]{3,2,1,0:T(8,128)(2,1)S(1)} %pad_maximum_fusion.1.refs_16_) | copy-start | bytes 1966084
  46.8 17.2 %collective-permute-start.20 = (bf16[2,4,160,256]{3,2,1,0:T(8,128)(2,1)S(1)}, bf16[2,4,160,256]{3,2,1,0:T(8,128)(2,1)S(1)}, u32[]{:S(2)}, u32[]{:S(2)}) collective-permute-start(bf16[2,4,160,256]{3,2,1,0:T(8,128)(2,1)S(1)} %pad_maximum_fusion.1.refs_16_), channel_id=1, source_target_pairs={{0,56},{1,9},{8,16},{9,1},{16,8},{17,25},{24,32},{25,17},{32,24},{... | collective-permute-start | bytes 1966088 | tf_op jit(solution)/shard_map/ppermute | solution.py:34
  51.6 8.6 %collective-permute-start.12 = (bf16[2,352,256]{2,1,0:T(8,128)(2,1)S(1)}, bf16[2,352,256]{2,1,0:T(8,128)(2,1)S(1)}, u32[]{:S(2)}, u32[]{:S(2)}) collective-permute-start(bf16[2,352,256]{2,1,0:T(8,128)(2,1)S(1)} %collective-permute-done.8), channel_id=1, source_target_pairs={{0,8},{1,57},{8,0},{9,17},{16,24},{17,9},{24,16},{25,33},{32,40},{... | collective-permute-start | bytes 1081352 | tf_op jit(solution)/shard_map/ppermute | solution.py:34
  52.5 21.2 %collective-permute-start.9 = (bf16[4,352,256]{2,1,0:T(8,128)(2,1)S(1)}, bf16[4,352,256]{2,1,0:T(8,128)(2,1)S(1)}, u32[]{:S(2)}, u32[]{:S(2)}) collective-permute-start(bf16[4,352,256]{2,1,0:T(8,128)(2,1)S(1)} %get-tuple-element.16), channel_id=1, source_target_pairs={{0,64},{1,193},{64,0},{65,129},{128,192},{129,65},{192,128},{193,1... | collective-permute-start | bytes 2162696 | tf_op jit(solution)/shard_map/ppermute | solution.py:34
  60.1 10.5 %collective-permute-start.13 = (bf16[2,352,256]{2,1,0:T(8,128)(2,1)S(1)}, bf16[2,352,256]{2,1,0:T(8,128)(2,1)S(1)}, u32[]{:S(2)}, u32[]{:S(2)}) collective-permute-start(bf16[2,352,256]{2,1,0:T(8,128)(2,1)S(1)} %collective-permute-done.12), channel_id=1, source_target_pairs={{0,56},{1,9},{8,16},{9,1},{16,8},{17,25},{24,32},{25,17},{32,24},{... | collective-permute-start | bytes 1081352 | tf_op jit(solution)/shard_map/ppermute | solution.py:34
  63.3 13.8 %collective-permute-start.10 = (bf16[4,352,256]{2,1,0:T(8,128)(2,1)S(1)}, bf16[4,352,256]{2,1,0:T(8,128)(2,1)S(1)}, u32[]{:S(2)}, u32[]{:S(2)}) collective-permute-start(bf16[4,352,256]{2,1,0:T(8,128)(2,1)S(1)} %get-tuple-element.16), channel_id=1, source_target_pairs={{0,192},{1,65},{64,128},{65,1},{128,64},{129,193},{192,0},{193,129... | collective-permute-start | bytes 2162696 | tf_op jit(solution)/shard_map/ppermute | solution.py:34
  64.0 38.5 %copy-start.24 = (bf16[2,4,160,256]{3,2,1,0:T(8,128)(2,1)}, bf16[2,4,160,256]{3,2,1,0:T(8,128)(2,1)S(1)}, u32[]{:S(2)}) copy-start(bf16[2,4,160,256]{3,2,1,0:T(8,128)(2,1)S(1)} %collective-permute-done.20.refs_17_) | copy-start | bytes 1966084
  64.0 15.0 %collective-permute-start.21 = (bf16[2,4,160,256]{3,2,1,0:T(8,128)(2,1)S(1)}, bf16[2,4,160,256]{3,2,1,0:T(8,128)(2,1)S(1)}, u32[]{:S(2)}, u32[]{:S(2)}) collective-permute-start(bf16[2,4,160,256]{3,2,1,0:T(8,128)(2,1)S(1)} %collective-permute-done.20.refs_17_), channel_id=1, source_target_pairs={{0,8},{1,57},{8,0},{9,17},{16,24},{17,9},{24,16},{25,33},{32,40},{... | collective-permute-start | bytes 1966088 | tf_op jit(solution)/shard_map/ppermute | solution.py:34
  70.6 44.4 %copy-start.19 = (bf16[4,352,256]{2,1,0:T(8,128)(2,1)}, bf16[4,352,256]{2,1,0:T(8,128)(2,1)S(1)}, u32[]{:S(2)}) copy-start(bf16[4,352,256]{2,1,0:T(8,128)(2,1)S(1)} %constant_dynamic-update-slice_fusion) | copy-start | bytes 2162692
  70.6 20.0 %collective-permute-start.15 = (bf16[4,352,256]{2,1,0:T(8,128)(2,1)S(1)}, bf16[4,352,256]{2,1,0:T(8,128)(2,1)S(1)}, u32[]{:S(2)}, u32[]{:S(2)}) collective-permute-start(bf16[4,352,256]{2,1,0:T(8,128)(2,1)S(1)} %constant_dynamic-update-slice_fusion), channel_id=1, source_target_pairs={{0,192},{1,65},{64,128},{65,1},{128,64},{129,193},{192,0},{193,129... | collective-permute-start | bytes 2162696 | tf_op jit(solution)/shard_map/ppermute | solution.py:34
  73.8 24.6 %copy-start.20 = (bf16[4,352,256]{2,1,0:T(8,128)(2,1)}, bf16[4,352,256]{2,1,0:T(8,128)(2,1)S(1)}, u32[]{:S(2)}) copy-start(bf16[4,352,256]{2,1,0:T(8,128)(2,1)S(1)} %collective-permute-done.9) | copy-start | bytes 2162692
  73.8 24.6 %collective-permute-start.1 = (bf16[32,64,256]{2,1,0:T(8,128)(2,1)S(1)}, bf16[32,64,256]{2,1,0:T(8,128)(2,1)}, u32[]{:S(2)}, u32[]{:S(2)}) collective-permute-start(bf16[32,64,256]{2,1,0:T(8,128)(2,1)S(1)} %bitcast.55), channel_id=1, source_target_pairs={{0,6},{1,3},{2,4},{3,1},{4,2},{5,7},{6,0},{7,5},{8,14},{9,11},{10,... | collective-permute-start | bytes 3145736 | tf_op jit(solution)/shard_map/ppermute | solution.py:34
  75.5 25.6 %collective-permute-start.2 = (bf16[32,64,256]{2,1,0:T(8,128)(2,1)}, bf16[32,64,256]{2,1,0:T(8,128)(2,1)}, u32[]{:S(2)}, u32[]{:S(2)}) collective-permute-start(bf16[32,64,256]{2,1,0:T(8,128)(2,1)} %collective-permute-done.refs_1_), channel_id=1, source_target_pairs={{0,6},{1,3},{2,4},{3,1},{4,2},{5,7},{6,0},{7,5},{8,14},{9,11},{10,... | collective-permute-start | bytes 3145736 | tf_op jit(solution)/shard_map/ppermute | solution.py:34
  77.0 21.9 %copy-start.21 = (bf16[4,352,256]{2,1,0:T(8,128)(2,1)}, bf16[4,352,256]{2,1,0:T(8,128)(2,1)S(1)}, u32[]{:S(2)}) copy-start(bf16[4,352,256]{2,1,0:T(8,128)(2,1)S(1)} %collective-permute-done.10) | copy-start | bytes 2162692
  77.0 18.7 %collective-permute-start.14 = (bf16[4,352,256]{2,1,0:T(8,128)(2,1)S(1)}, bf16[4,352,256]{2,1,0:T(8,128)(2,1)}, u32[]{:S(2)}, u32[]{:S(2)}) collective-permute-start(bf16[4,352,256]{2,1,0:T(8,128)(2,1)S(1)} %constant_dynamic-update-slice_fusion), channel_id=1, source_target_pairs={{0,64},{1,193},{64,0},{65,129},{128,192},{129,65},{192,128},{193,1... | collective-permute-start | bytes 2162696 | tf_op jit(solution)/shard_map/ppermute | solution.py:34
  78.9 23.5 %copy-start.25 = (bf16[2,4,160,256]{3,2,1,0:T(8,128)(2,1)}, bf16[2,4,160,256]{3,2,1,0:T(8,128)(2,1)S(1)}, u32[]{:S(2)}) copy-start(bf16[2,4,160,256]{3,2,1,0:T(8,128)(2,1)S(1)} %collective-permute-done.21.refs_18_) | copy-start | bytes 1966084
  78.9 19.4 %collective-permute-start.11 = (bf16[4,352,256]{2,1,0:T(8,128)(2,1)S(1)}, bf16[4,352,256]{2,1,0:T(8,128)(2,1)S(1)}, u32[]{:S(2)}, u32[]{:S(2)}) collective-permute-start(bf16[4,352,256]{2,1,0:T(8,128)(2,1)S(1)} %collective-permute-done.9), channel_id=1, source_target_pairs={{0,192},{1,65},{64,128},{65,1},{128,64},{129,193},{192,0},{193,129... | collective-permute-start | bytes 2162696 | tf_op jit(solution)/shard_map/ppermute | solution.py:34
  90.6 10.5 %copy-start.22 = (bf16[4,352,256]{2,1,0:T(8,128)(2,1)}, bf16[4,352,256]{2,1,0:T(8,128)(2,1)S(1)}, u32[]{:S(2)}) copy-start(bf16[4,352,256]{2,1,0:T(8,128)(2,1)S(1)} %collective-permute-done.15) | copy-start | bytes 2162692
  90.7 11.8 %collective-permute-start.22 = (bf16[2,4,160,256]{3,2,1,0:T(8,128)(2,1)S(1)}, bf16[2,4,160,256]{3,2,1,0:T(8,128)(2,1)S(1)}, u32[]{:S(2)}, u32[]{:S(2)}) collective-permute-start(bf16[2,4,160,256]{3,2,1,0:T(8,128)(2,1)S(1)} %collective-permute-done.21.refs_18_), channel_id=1, source_target_pairs={{0,56},{1,9},{8,16},{9,1},{16,8},{17,25},{24,32},{25,17},{32,24},{... | collective-permute-start | bytes 1966088 | tf_op jit(solution)/shard_map/ppermute | solution.py:34
  95.8 19.2 %collective-permute-start.3 = (bf16[32,64,256]{2,1,0:T(8,128)(2,1)S(1)}, bf16[32,64,256]{2,1,0:T(8,128)(2,1)}, u32[]{:S(2)}, u32[]{:S(2)}) collective-permute-start(bf16[32,64,256]{2,1,0:T(8,128)(2,1)S(1)} %bitcast.56), channel_id=1, source_target_pairs={{0,1},{1,0},{2,3},{3,2},{4,5},{5,4},{6,7},{7,6},{8,9},{9,8},{10,11... | collective-permute-start | bytes 3145736 | tf_op jit(solution)/shard_map/ppermute | solution.py:25
  98.4 2.8 %copy-start.23 = (bf16[4,352,256]{2,1,0:T(8,128)(2,1)}, bf16[4,352,256]{2,1,0:T(8,128)(2,1)S(1)}, u32[]{:S(2)}) copy-start(bf16[4,352,256]{2,1,0:T(8,128)(2,1)S(1)} %collective-permute-done.11) | copy-start | bytes 2162692
  98.4 16.6 %collective-permute-start.4 = (bf16[32,64,256]{2,1,0:T(8,128)(2,1)}, bf16[32,64,256]{2,1,0:T(8,128)(2,1)}, u32[]{:S(2)}, u32[]{:S(2)}) collective-permute-start(bf16[32,64,256]{2,1,0:T(8,128)(2,1)} %collective-permute-done.refs_1_), channel_id=1, source_target_pairs={{0,1},{1,0},{2,3},{3,2},{4,5},{5,4},{6,7},{7,6},{8,9},{9,8},{10,11... | collective-permute-start | bytes 3145736 | tf_op jit(solution)/shard_map/ppermute | solution.py:25
  98.4 16.6 %collective-permute-start.5 = (bf16[32,64,256]{2,1,0:T(8,128)(2,1)}, bf16[32,64,256]{2,1,0:T(8,128)(2,1)}, u32[]{:S(2)}, u32[]{:S(2)}) collective-permute-start(bf16[32,64,256]{2,1,0:T(8,128)(2,1)} %collective-permute-done.1.refs_2_), channel_id=1, source_target_pairs={{0,1},{1,0},{2,3},{3,2},{4,5},{5,4},{6,7},{7,6},{8,9},{9,8},{10,11... | collective-permute-start | bytes 3145736 | tf_op jit(solution)/shard_map/ppermute | solution.py:25
  101.1 13.8 %collective-permute-start.6 = (bf16[32,64,256]{2,1,0:T(8,128)(2,1)}, bf16[32,64,256]{2,1,0:T(8,128)(2,1)}, u32[]{:S(2)}, u32[]{:S(2)}) collective-permute-start(bf16[32,64,256]{2,1,0:T(8,128)(2,1)} %collective-permute-done.2.refs_3_), channel_id=1, source_target_pairs={{0,1},{1,0},{2,3},{3,2},{4,5},{5,4},{6,7},{7,6},{8,9},{9,8},{10,11... | collective-permute-start | bytes 3145736 | tf_op jit(solution)/shard_map/ppermute | solution.py:25
  102.5 0.9 copy-start.26
  103.3 11.6 %collective-permute-start.16 = (bf16[4,352,256]{2,1,0:T(8,128)(2,1)}, bf16[4,352,256]{2,1,0:T(8,128)(2,1)}, u32[]{:S(2)}, u32[]{:S(2)}) collective-permute-start(bf16[4,352,256]{2,1,0:T(8,128)(2,1)} %collective-permute-done.14), channel_id=1, source_target_pairs={{0,192},{1,65},{64,128},{65,1},{128,64},{129,193},{192,0},{193,129... | collective-permute-start | bytes 2162696 | tf_op jit(solution)/shard_map/ppermute | solution.py:34
  164.7 5.3 %collective-permute-start.23 = (bf16[256,256]{1,0:T(8,128)(2,1)}, bf16[256,256]{1,0:T(8,128)(2,1)S(1)}, u32[]{:S(2)}, u32[]{:S(2)}) collective-permute-start(bf16[256,256]{1,0:T(8,128)(2,1)} %get-tuple-element.12), channel_id=1, source_target_pairs={{0,8},{1,57},{8,0},{9,17},{16,24},{17,9},{24,16},{25,33},{32,40},{... | collective-permute-start | bytes 393224 | tf_op jit(solution)/shard_map/ppermute | solution.py:34
  170.9 39.3 %copy-start.1 = (bf16[2,256,256]{2,1,0:T(8,128)(2,1)}, bf16[2,256,256]{2,1,0:T(8,128)(2,1)S(1)}, u32[]{:S(2)}) copy-start(bf16[2,256,256]{2,1,0:T(8,128)(2,1)S(1)} %pad_maximum_fusion.4.refs_0_) | copy-start | bytes 786436
  170.9 7.7 %collective-permute-start.24 = (bf16[2,256,256]{2,1,0:T(8,128)(2,1)S(1)}, bf16[2,256,256]{2,1,0:T(8,128)(2,1)S(1)}, u32[]{:S(2)}, u32[]{:S(2)}) collective-permute-start(bf16[2,256,256]{2,1,0:T(8,128)(2,1)S(1)} %pad_maximum_fusion.4.refs_0_), channel_id=1, source_target_pairs={{0,56},{1,9},{8,16},{9,1},{16,8},{17,25},{24,32},{25,17},{32,24},{... | collective-permute-start | bytes 786440 | tf_op jit(solution)/shard_map/ppermute | solution.py:34
  178.5 31.6 %copy-start.8 = (bf16[2,256,256]{2,1,0:T(8,128)(2,1)}, bf16[2,256,256]{2,1,0:T(8,128)(2,1)S(1)}, u32[]{:S(2)}) copy-start(bf16[2,256,256]{2,1,0:T(8,128)(2,1)S(1)} %collective-permute-done.24.refs_4_) | copy-start | bytes 786436
  178.5 6.4 %collective-permute-start.25 = (bf16[2,256,256]{2,1,0:T(8,128)(2,1)S(1)}, bf16[2,256,256]{2,1,0:T(8,128)(2,1)S(1)}, u32[]{:S(2)}, u32[]{:S(2)}) collective-permute-start(bf16[2,256,256]{2,1,0:T(8,128)(2,1)S(1)} %collective-permute-done.24.refs_4_), channel_id=1, source_target_pairs={{0,8},{1,57},{8,0},{9,17},{16,24},{17,9},{24,16},{25,33},{32,40},{... | collective-permute-start | bytes 786440 | tf_op jit(solution)/shard_map/ppermute | solution.py:34
  178.5 8.9 %collective-permute-start.30 = (bf16[2,256,256]{2,1,0:T(8,128)(2,1)S(1)}, bf16[2,256,256]{2,1,0:T(8,128)(2,1)S(1)}, u32[]{:S(2)}, u32[]{:S(2)}) collective-permute-start(bf16[2,256,256]{2,1,0:T(8,128)(2,1)S(1)} %pad_maximum_fusion.4.refs_0_), channel_id=1, source_target_pairs={{0,64},{1,193},{64,0},{65,129},{128,192},{129,65},{192,128},{193,1... | collective-permute-start | bytes 786440 | tf_op jit(solution)/shard_map/ppermute | solution.py:34
  179.9 10.0 %collective-permute-start.31 = (bf16[2,256,256]{2,1,0:T(8,128)(2,1)S(1)}, bf16[2,256,256]{2,1,0:T(8,128)(2,1)S(1)}, u32[]{:S(2)}, u32[]{:S(2)}) collective-permute-start(bf16[2,256,256]{2,1,0:T(8,128)(2,1)S(1)} %pad_maximum_fusion.4.refs_0_), channel_id=1, source_target_pairs={{0,192},{1,65},{64,128},{65,1},{128,64},{129,193},{192,0},{193,129... | collective-permute-start | bytes 786440 | tf_op jit(solution)/shard_map/ppermute | solution.py:34
  184.9 25.2 %copy-start.9 = (bf16[2,256,256]{2,1,0:T(8,128)(2,1)}, bf16[2,256,256]{2,1,0:T(8,128)(2,1)S(1)}, u32[]{:S(2)}) copy-start(bf16[2,256,256]{2,1,0:T(8,128)(2,1)S(1)} %collective-permute-done.25.refs_8_) | copy-start | bytes 786436
  184.9 7.6 %collective-permute-start.26 = (bf16[2,256,256]{2,1,0:T(8,128)(2,1)S(1)}, bf16[2,256,256]{2,1,0:T(8,128)(2,1)S(1)}, u32[]{:S(2)}, u32[]{:S(2)}) collective-permute-start(bf16[2,256,256]{2,1,0:T(8,128)(2,1)S(1)} %collective-permute-done.25.refs_8_), channel_id=1, source_target_pairs={{0,56},{1,9},{8,16},{9,1},{16,8},{17,25},{24,32},{25,17},{32,24},{... | collective-permute-start | bytes 786440 | tf_op jit(solution)/shard_map/ppermute | solution.py:34
  187.4 22.7 %copy-start.10 = (bf16[2,256,256]{2,1,0:T(8,128)(2,1)}, bf16[2,256,256]{2,1,0:T(8,128)(2,1)S(1)}, u32[]{:S(2)}) copy-start(bf16[2,256,256]{2,1,0:T(8,128)(2,1)S(1)} %collective-permute-done.30.refs_1_) | copy-start | bytes 786436
  187.4 9.2 %collective-permute-start.32 = (bf16[2,256,256]{2,1,0:T(8,128)(2,1)S(1)}, bf16[2,256,256]{2,1,0:T(8,128)(2,1)S(1)}, u32[]{:S(2)}, u32[]{:S(2)}) collective-permute-start(bf16[2,256,256]{2,1,0:T(8,128)(2,1)S(1)} %collective-permute-done.30.refs_1_), channel_id=1, source_target_pairs={{0,192},{1,65},{64,128},{65,1},{128,64},{129,193},{192,0},{193,129... | collective-permute-start | bytes 786440 | tf_op jit(solution)/shard_map/ppermute | solution.py:34
  187.6 9.6 %collective-permute-start.33 = (bf16[2,256,256]{2,1,0:T(8,128)(2,1)S(1)}, bf16[2,256,256]{2,1,0:T(8,128)(2,1)S(1)}, u32[]{:S(2)}, u32[]{:S(2)}) collective-permute-start(bf16[2,256,256]{2,1,0:T(8,128)(2,1)S(1)} %collective-permute-done.24.refs_4_), channel_id=1, source_target_pairs={{0,64},{1,193},{64,0},{65,129},{128,192},{129,65},{192,128},{193,1... | collective-permute-start | bytes 786440 | tf_op jit(solution)/shard_map/ppermute | solution.py:34
  189.9 12.8 %collective-permute-start.36 = (bf16[2,256,256]{2,1,0:T(8,128)(2,1)S(1)}, bf16[2,256,256]{2,1,0:T(8,128)(2,1)S(1)}, u32[]{:S(2)}, u32[]{:S(2)}) collective-permute-start(bf16[2,256,256]{2,1,0:T(8,128)(2,1)S(1)} %collective-permute-done.25.refs_8_), channel_id=1, source_target_pairs={{0,64},{1,193},{64,0},{65,129},{128,192},{129,65},{192,128},{193,1... | collective-permute-start | bytes 786440 | tf_op jit(solution)/shard_map/ppermute | solution.py:34
  190.0 20.2 %copy-start.11 = (bf16[2,256,256]{2,1,0:T(8,128)(2,1)}, bf16[2,256,256]{2,1,0:T(8,128)(2,1)S(1)}, u32[]{:S(2)}) copy-start(bf16[2,256,256]{2,1,0:T(8,128)(2,1)S(1)} %collective-permute-done.31.refs_2_) | copy-start | bytes 786436
  190.0 14.5 %collective-permute-start.34 = (bf16[2,256,256]{2,1,0:T(8,128)(2,1)S(1)}, bf16[2,256,256]{2,1,0:T(8,128)(2,1)S(1)}, u32[]{:S(2)}, u32[]{:S(2)}) collective-permute-start(bf16[2,256,256]{2,1,0:T(8,128)(2,1)S(1)} %collective-permute-done.24.refs_4_), channel_id=1, source_target_pairs={{0,192},{1,65},{64,128},{65,1},{128,64},{129,193},{192,0},{193,129... | collective-permute-start | bytes 786440 | tf_op jit(solution)/shard_map/ppermute | solution.py:34
  192.5 23.2 %copy-start.3 = (bf16[2,256,256]{2,1,0:T(8,128)(2,1)}, bf16[2,256,256]{2,1,0:T(8,128)(2,1)S(1)}, u32[]{:S(2)}) copy-start(bf16[2,256,256]{2,1,0:T(8,128)(2,1)S(1)} %collective-permute-done.26.refs_0_) | copy-start | bytes 786436
  192.5 15.9 %collective-permute-start.27 = (bf16[2,256,256]{2,1,0:T(8,128)(2,1)S(1)}, bf16[2,256,256]{2,1,0:T(8,128)(2,1)S(1)}, u32[]{:S(2)}, u32[]{:S(2)}) collective-permute-start(bf16[2,256,256]{2,1,0:T(8,128)(2,1)S(1)} %collective-permute-done.26.refs_0_), channel_id=1, source_target_pairs={{0,64},{1,193},{64,0},{65,129},{128,192},{129,65},{192,128},{193,1... | collective-permute-start | bytes 786440 | tf_op jit(solution)/shard_map/ppermute | solution.py:34
  196.7 13.5 %copy-start.12 = (bf16[2,256,256]{2,1,0:T(8,128)(2,1)}, bf16[2,256,256]{2,1,0:T(8,128)(2,1)S(1)}, u32[]{:S(2)}) copy-start(bf16[2,256,256]{2,1,0:T(8,128)(2,1)S(1)} %collective-permute-done.32.refs_3_) | copy-start | bytes 786436
  196.7 13.4 %collective-permute-start.37 = (bf16[2,256,256]{2,1,0:T(8,128)(2,1)S(1)}, bf16[2,256,256]{2,1,0:T(8,128)(2,1)S(1)}, u32[]{:S(2)}, u32[]{:S(2)}) collective-permute-start(bf16[2,256,256]{2,1,0:T(8,128)(2,1)S(1)} %collective-permute-done.25.refs_8_), channel_id=1, source_target_pairs={{0,192},{1,65},{64,128},{65,1},{128,64},{129,193},{192,0},{193,129... | collective-permute-start | bytes 786440 | tf_op jit(solution)/shard_map/ppermute | solution.py:34
  197.1 13.1 %copy-start.13 = (bf16[2,256,256]{2,1,0:T(8,128)(2,1)}, bf16[2,256,256]{2,1,0:T(8,128)(2,1)S(1)}, u32[]{:S(2)}) copy-start(bf16[2,256,256]{2,1,0:T(8,128)(2,1)S(1)} %collective-permute-done.33.refs_5_) | copy-start | bytes 786436
  197.1 13.0 %collective-permute-start.35 = (bf16[2,256,256]{2,1,0:T(8,128)(2,1)S(1)}, bf16[2,256,256]{2,1,0:T(8,128)(2,1)S(1)}, u32[]{:S(2)}, u32[]{:S(2)}) collective-permute-start(bf16[2,256,256]{2,1,0:T(8,128)(2,1)S(1)} %collective-permute-done.33.refs_5_), channel_id=1, source_target_pairs={{0,192},{1,65},{64,128},{65,1},{128,64},{129,193},{192,0},{193,129... | collective-permute-start | bytes 786440 | tf_op jit(solution)/shard_map/ppermute | solution.py:34
  202.8 7.4 %copy-start.14 = (bf16[2,256,256]{2,1,0:T(8,128)(2,1)}, bf16[2,256,256]{2,1,0:T(8,128)(2,1)S(1)}, u32[]{:S(2)}) copy-start(bf16[2,256,256]{2,1,0:T(8,128)(2,1)S(1)} %collective-permute-done.36.refs_9_) | copy-start | bytes 786436
  202.8 7.4 %collective-permute-start.38 = (bf16[2,256,256]{2,1,0:T(8,128)(2,1)S(1)}, bf16[2,256,256]{2,1,0:T(8,128)(2,1)S(1)}, u32[]{:S(2)}, u32[]{:S(2)}) collective-permute-start(bf16[2,256,256]{2,1,0:T(8,128)(2,1)S(1)} %collective-permute-done.36.refs_9_), channel_id=1, source_target_pairs={{0,192},{1,65},{64,128},{65,1},{128,64},{129,193},{192,0},{193,129... | collective-permute-start | bytes 786440 | tf_op jit(solution)/shard_map/ppermute | solution.py:34
  204.5 5.7 %copy-start.15 = (bf16[2,256,256]{2,1,0:T(8,128)(2,1)}, bf16[2,256,256]{2,1,0:T(8,128)(2,1)S(1)}, u32[]{:S(2)}) copy-start(bf16[2,256,256]{2,1,0:T(8,128)(2,1)S(1)} %collective-permute-done.34.refs_6_) | copy-start | bytes 786436
  204.5 11.1 %collective-permute-start.28 = (bf16[2,256,256]{2,1,0:T(8,128)(2,1)S(1)}, bf16[2,256,256]{2,1,0:T(8,128)(2,1)S(1)}, u32[]{:S(2)}, u32[]{:S(2)}) collective-permute-start(bf16[2,256,256]{2,1,0:T(8,128)(2,1)S(1)} %collective-permute-done.26.refs_0_), channel_id=1, source_target_pairs={{0,192},{1,65},{64,128},{65,1},{128,64},{129,193},{192,0},{193,129... | collective-permute-start | bytes 786440 | tf_op jit(solution)/shard_map/ppermute | solution.py:34
  208.4 7.4 %copy-start.4 = (bf16[2,256,256]{2,1,0:T(8,128)(2,1)}, bf16[2,256,256]{2,1,0:T(8,128)(2,1)S(1)}, u32[]{:S(2)}) copy-start(bf16[2,256,256]{2,1,0:T(8,128)(2,1)S(1)} %collective-permute-done.27.refs_1_) | copy-start | bytes 786436
  208.4 7.4 %collective-permute-start.29 = (bf16[2,256,256]{2,1,0:T(8,128)(2,1)S(1)}, bf16[2,256,256]{2,1,0:T(8,128)(2,1)S(1)}, u32[]{:S(2)}, u32[]{:S(2)}) collective-permute-start(bf16[2,256,256]{2,1,0:T(8,128)(2,1)S(1)} %collective-permute-done.27.refs_1_), channel_id=1, source_target_pairs={{0,192},{1,65},{64,128},{65,1},{128,64},{129,193},{192,0},{193,129... | collective-permute-start | bytes 786440 | tf_op jit(solution)/shard_map/ppermute | solution.py:34
  (5 other events, 3.6 us)

commit v4 on v3

--- a/solution.py
+++ b/solution.py
@@ -95,7 +95,7 @@
     for no, ((nz, nx, rows, _), offset, kz, kx) in enumerate(layout):
         loads.append(pltpu.make_async_copy(
             pieces[no], wv.at[pl.ds(kz, nz), pl.ds(kx, nx), pl.ds(offset, rows)], wsem.at[no]))
-    for copy in parts + loads:
+    for copy in parts + [loads[no] for no in sorted(range(count), key=lambda no: layout[no][2])]:
         copy.start()
     for copy in parts:
         copy.wait()

time: 222 us -> 222 us (level)
  no operation moved by 1% of the time
where the time goes in v4:
time: 222 us; the launch traced here: 220 us
  waiting for transfers between devices  80.1 us (36%)
  starting transfers between devices  61.8 us (28%)
  blocking collectives  38.9 us (18%)
  Pallas kernels  26.9 us (12%)
  local copies, waits for them, and re-layouts  7.53 us (3%)
  other arithmetic  2.8 us (1%)
    ppermute x35, waiting for transfers between devices, near(): return lax.ppermute(array, (axis, 'c'), pairs)  80.1 us
    ppermute x35, starting transfers between devices, near(): return lax.ppermute(array, (axis, 'c'), pairs)  49.7 us
    all_to_all x1, blocking collectives, totals_of_groups(): sums = jnp.sum(lax.all_to_all(sums, ('x', 'y'), 0, 0), axis=0)  15 us
    all_to_all x1, blocking collectives, totals_of_groups(): lax.all_to_all(jnp.broadcast_to(sums[None], (NZ * NC,) + sums.shape), ('z...  14.4 us
    pallas_call x1, Pallas kernels, grads_and_sums(): pl.pallas_call(functools.partial(grads_kernel, layout), out_shape=(jax.Sh...  13.9 us
    all_to_all x1, starting transfers between devices, local(): lax.all_to_all(token_rows, ('x', 'z'), 1, 0, tiled=True)  11.6 us
    unnamed x1, blocking collectives  9.48 us
    pallas_call x2, Pallas kernels, place_rows(): pl.pallas_call(functools.partial(place_kernel, first, count), out_shape=j...  6.69 us
  transfers between devices with their start and end apart: 40, of which 23 were waited for; matrix products, arithmetic and copies ran while one was open for 2% of the time, Pallas kernels for 2%

profile of v4, /device:TPU:4, one launch (start us, length us, event | category | flops | bytes accessed | tf_op | source)
XLA Modules:
  0.0 219.9 jit_solution(5685438370974708980)
XLA Ops:
  0.7 2.4 %copy.30 = bf16[8,32,8,256]{3,2,0,1:T(8,128)(2,1)} copy(bf16[8,32,8,256]{3,2,1,0:T(8,128)(2,1)} %bitcast.53) | data formatting | bytes 2097152 | tf_op jit(solution)/shard_map/all_to_all | solution.py:323
  3.0 11.6 %all-to-all-start = ((bf16[64,32,256]{2,0,1:T(8,128)(2,1)}), bf16[64,32,256]{2,0,1:T(8,128)(2,1)S(1)}, u32[]{:S(2)}, u32[]{:S(2)}) async-start(bf16[64,32,256]{2,0,1:T(8,128)(2,1)} %bitcast.51), calls=%async_computation | async-start | bytes 2097152 | tf_op jit(solution)/shard_map/all_to_all | solution.py:323
  14.6 0.6 dynamic-slice
  16.2 9.5 %all-reduce = s32[512]{0:T(512)S(1)} all-reduce(s32[512]{0:T(512)S(1)} %dynamic-update-slice), channel_id=1, replica_groups=mesh['x'=4,'z'=8,'y'=4,'c'=2] {'y','c'}, use_global_device_ids=true, to_apply=%add | all-reduce | flops 512 | bytes 4096
  25.6 0.6 fusion
  26.4 1.3 collective-permute-start.17
  27.7 3.8 %collective-permute-done.17 = bf16[160,256]{1,0:T(8,128)(2,1)S(1)} collective-permute-done((bf16[160,256]{1,0:T(8,128)(2,1)S(1)}, bf16[160,256]{1,0:T(8,128)(2,1)S(1)}, u32[]{:S(2)}, u32[]{:S(2)}) %collective-permute-start.17) | collective-permute-done | bytes 81952 | tf_op jit(solution)/shard_map/ppermute | solution.py:34
  31.4 1.4 collective-permute-start.18
  32.9 0.8 collective-permute-start.7
  33.7 4.5 %collective-permute-done.18 = bf16[2,160,256]{2,1,0:T(8,128)(2,1)S(1)} collective-permute-done((bf16[2,160,256]{2,1,0:T(8,128)(2,1)S(1)}, bf16[2,160,256]{2,1,0:T(8,128)(2,1)S(1)}, u32[]{:S(2)}, u32[]{:S(2)}) %collective-permute-start.18) | collective-permute-done | bytes 163872 | tf_op jit(solution)/shard_map/ppermute | solution.py:34
  38.2 1.9 collective-permute-start.19
  40.1 0.7 collective-permute-done.7
  40.8 2.8 %collective-permute-start.8 = (bf16[2,352,256]{2,1,0:T(8,128)(2,1)S(1)}, bf16[2,352,256]{2,1,0:T(8,128)(2,1)S(1)}, u32[]{:S(2)}, u32[]{:S(2)}) collective-permute-start(bf16[2,352,256]{2,1,0:T(8,128)(2,1)S(1)} %pad_maximum_fusion.2), channel_id=1, source_target_pairs={{0,56},{1,9},{8,16},{9,1},{16,8},{17,25},{24,32},{25,17},{32,24},{... | collective-permute-start | bytes 1081352 | tf_op jit(solution)/shard_map/ppermute | solution.py:34
  43.6 1.5 collective-permute-start
  45.1 1.6 collective-permute-done.19
  46.8 4.8 %collective-permute-start.20 = (bf16[2,4,160,256]{3,2,1,0:T(8,128)(2,1)S(1)}, bf16[2,4,160,256]{3,2,1,0:T(8,128)(2,1)S(1)}, u32[]{:S(2)}, u32[]{:S(2)}) collective-permute-start(bf16[2,4,160,256]{3,2,1,0:T(8,128)(2,1)S(1)} %pad_maximum_fusion.1.refs_16_), channel_id=1, source_target_pairs={{0,56},{1,9},{8,16},{9,1},{16,8},{17,25},{24,32},{25,17},{32,24},{... | collective-permute-start | bytes 1966088 | tf_op jit(solution)/shard_map/ppermute | solution.py:34
  51.6 1.0 pad_maximum_fusion
  52.5 2.3 %collective-permute-start.9 = (bf16[4,352,256]{2,1,0:T(8,128)(2,1)S(1)}, bf16[4,352,256]{2,1,0:T(8,128)(2,1)S(1)}, u32[]{:S(2)}, u32[]{:S(2)}) collective-permute-start(bf16[4,352,256]{2,1,0:T(8,128)(2,1)S(1)} %get-tuple-element.16), channel_id=1, source_target_pairs={{0,64},{1,193},{64,0},{65,129},{128,192},{129,65},{192,128},{193,1... | collective-permute-start | bytes 2162696 | tf_op jit(solution)/shard_map/ppermute | solution.py:34
  54.8 5.3 %collective-permute-done.12 = bf16[2,352,256]{2,1,0:T(8,128)(2,1)S(1)} collective-permute-done((bf16[2,352,256]{2,1,0:T(8,128)(2,1)S(1)}, bf16[2,352,256]{2,1,0:T(8,128)(2,1)S(1)}, u32[]{:S(2)}, u32[]{:S(2)}) %collective-permute-start.12) | collective-permute-done | bytes 360480 | tf_op jit(solution)/shard_map/ppermute | solution.py:34
  60.1 3.1 %collective-permute-start.13 = (bf16[2,352,256]{2,1,0:T(8,128)(2,1)S(1)}, bf16[2,352,256]{2,1,0:T(8,128)(2,1)S(1)}, u32[]{:S(2)}, u32[]{:S(2)}) collective-permute-start(bf16[2,352,256]{2,1,0:T(8,128)(2,1)S(1)} %collective-permute-done.12), channel_id=1, source_target_pairs={{0,56},{1,9},{8,16},{9,1},{16,8},{17,25},{24,32},{25,17},{32,24},{... | collective-permute-start | bytes 1081352 | tf_op jit(solution)/shard_map/ppermute | solution.py:34
  64.0 6.6 %collective-permute-done.13 = bf16[2,352,256]{2,1,0:T(8,128)(2,1)S(1)} collective-permute-done((bf16[2,352,256]{2,1,0:T(8,128)(2,1)S(1)}, bf16[2,352,256]{2,1,0:T(8,128)(2,1)S(1)}, u32[]{:S(2)}, u32[]{:S(2)}) %collective-permute-start.13) | collective-permute-done | bytes 360480 | tf_op jit(solution)/shard_map/ppermute | solution.py:34
  70.6 3.1 %collective-permute-start.15 = (bf16[4,352,256]{2,1,0:T(8,128)(2,1)S(1)}, bf16[4,352,256]{2,1,0:T(8,128)(2,1)S(1)}, u32[]{:S(2)}, u32[]{:S(2)}) collective-permute-start(bf16[4,352,256]{2,1,0:T(8,128)(2,1)S(1)} %constant_dynamic-update-slice_fusion), channel_id=1, source_target_pairs={{0,192},{1,65},{64,128},{65,1},{128,64},{129,193},{192,0},{193,129... | collective-permute-start | bytes 2162696 | tf_op jit(solution)/shard_map/ppermute | solution.py:34
  73.8 1.7 collective-permute-start.1
  75.5 1.5 collective-permute-start.2
  77.0 1.9 collective-permute-start.14
  78.9 2.5 %collective-permute-start.11 = (bf16[4,352,256]{2,1,0:T(8,128)(2,1)S(1)}, bf16[4,352,256]{2,1,0:T(8,128)(2,1)S(1)}, u32[]{:S(2)}, u32[]{:S(2)}) collective-permute-start(bf16[4,352,256]{2,1,0:T(8,128)(2,1)S(1)} %collective-permute-done.9), channel_id=1, source_target_pairs={{0,192},{1,65},{64,128},{65,1},{128,64},{129,193},{192,0},{193,129... | collective-permute-start | bytes 2162696 | tf_op jit(solution)/shard_map/ppermute | solution.py:34
  81.5 9.2 %collective-permute-done.15 = bf16[4,352,256]{2,1,0:T(8,128)(2,1)S(1)} collective-permute-done((bf16[4,352,256]{2,1,0:T(8,128)(2,1)S(1)}, bf16[4,352,256]{2,1,0:T(8,128)(2,1)S(1)}, u32[]{:S(2)}, u32[]{:S(2)}) %collective-permute-start.15) | collective-permute-done | bytes 720928 | tf_op jit(solution)/shard_map/ppermute | solution.py:34
  90.7 2.5 %collective-permute-start.22 = (bf16[2,4,160,256]{3,2,1,0:T(8,128)(2,1)S(1)}, bf16[2,4,160,256]{3,2,1,0:T(8,128)(2,1)S(1)}, u32[]{:S(2)}, u32[]{:S(2)}) collective-permute-start(bf16[2,4,160,256]{3,2,1,0:T(8,128)(2,1)S(1)} %collective-permute-done.21.refs_18_), channel_id=1, source_target_pairs={{0,56},{1,9},{8,16},{9,1},{16,8},{17,25},{24,32},{25,17},{32,24},{... | collective-permute-start | bytes 1966088 | tf_op jit(solution)/shard_map/ppermute | solution.py:34
  93.1 2.6 %collective-permute-done.14 = bf16[4,352,256]{2,1,0:T(8,128)(2,1)} collective-permute-done((bf16[4,352,256]{2,1,0:T(8,128)(2,1)S(1)}, bf16[4,352,256]{2,1,0:T(8,128)(2,1)}, u32[]{:S(2)}, u32[]{:S(2)}) %collective-permute-start.14) | collective-permute-done | bytes 720928 | tf_op jit(solution)/shard_map/ppermute | solution.py:34
  95.8 2.6 %collective-permute-done.11 = bf16[4,352,256]{2,1,0:T(8,128)(2,1)S(1)} collective-permute-done((bf16[4,352,256]{2,1,0:T(8,128)(2,1)S(1)}, bf16[4,352,256]{2,1,0:T(8,128)(2,1)S(1)}, u32[]{:S(2)}, u32[]{:S(2)}) %collective-permute-start.11) | collective-permute-done | bytes 720928 | tf_op jit(solution)/shard_map/ppermute | solution.py:34
  98.9 2.2 %collective-permute-done.2.refs_3_ = bf16[32,64,256]{2,1,0:T(8,128)(2,1)} collective-permute-done((bf16[32,64,256]{2,1,0:T(8,128)(2,1)}, bf16[32,64,256]{2,1,0:T(8,128)(2,1)}, u32[]{:S(2)}, u32[]{:S(2)}) %collective-permute-start.2) | collective-permute-done | bytes 1048608 | tf_op jit(solution)/shard_map/ppermute | solution.py:34
  101.1 1.3 collective-permute-done.22.refs_19_
  102.5 0.9 copy-done.26
  103.3 0.6 collective-permute-start.16
  104.0 0.7 stack.67.place
  104.6 10.3 %collective-permute-done.16 = bf16[4,352,256]{2,1,0:T(8,128)(2,1)} collective-permute-done((bf16[4,352,256]{2,1,0:T(8,128)(2,1)}, bf16[4,352,256]{2,1,0:T(8,128)(2,1)}, u32[]{:S(2)}, u32[]{:S(2)}) %collective-permute-start.16) | collective-permute-done | bytes 720928 | tf_op jit(solution)/shard_map/ppermute | solution.py:34
  115.0 13.9 %shard_map.93 = (f32[32,256,256]{2,1,0:T(8,128)}, f32[16,16,128]{2,1,0:T(8,128)}) custom-call(s32[7]{0:T(128)} %stack.67.place, bf16[32,64,256]{2,1,0:T(8,128)(2,1)} %bitcast.57, bf16[32,64,256]{2,1,0:T(8,128)(2,1)} %collective-permute-done.refs_1_, bf16[32,64,256]{2,1,0:T(8,128)(2,1)} %collective-permute-done.1.refs_2_, ...), custom_call_target="tpu_custom_call" | custom-call | flops 6000000000 | bytes 25165824 | tf_op jit(solution)/shard_map/pallas_call | solution.py:158
  128.9 15.0 %all_to_all.26 = f32[16,16,128]{2,1,0:T(8,128)S(1)} all-to-all(f32[16,16,128]{2,1,0:T(8,128)} %get-tuple-element.10), channel_id=1, replica_groups=mesh['x'=4,'z'=8,'y'=4,'c'=2] {'x','y'}, dimensions={0} | all-to-all | bytes 262144 | tf_op jit(solution)/shard_map/all_to_all | solution.py:308
  144.0 14.4 %all_to_all.27.sums_ref = f32[16,16,128]{2,1,0:T(8,128)} all-to-all(f32[16,16,128]{2,1,0:T(8,128)S(1)} %broadcast_in_dim.39), channel_id=1, replica_groups=mesh['x'=4,'z'=8,'y'=4,'c'=2] {'z','c'}, dimensions={0} | all-to-all | bytes 262144 | tf_op jit(solution)/shard_map/all_to_all | solution.py:309
  158.4 6.2 %shard_map.94 = (bf16[256,256]{1,0:T(8,128)(2,1)}, f32[256,256]{1,0:T(8,128)}, f32[256,256]{1,0:T(8,128)}, f32[256,256]{1,0:T(8,128)}) custom-call(s32[7]{0:T(128)} %stack.67.place, f32[16,16,128]{2,1,0:T(8,128)} %all_to_all.27.sums_ref, f32[32,256,256]{2,1,0:T(8,128)} %get-tuple-element.11.g_hbm, f32[256,256]{1,0:T(8,128)} %master_ref.1, ...), custom_call_target="tpu_custom_call" | custom-call | flops 5000000 | bytes 10485760 | tf_op jit(solution)/shard_map/pallas_call | solution.py:254
  164.7 0.6 collective-permute-start.23
  165.3 4.6 %collective-permute-done.23 = bf16[256,256]{1,0:T(8,128)(2,1)S(1)} collective-permute-done((bf16[256,256]{1,0:T(8,128)(2,1)}, bf16[256,256]{1,0:T(8,128)(2,1)S(1)}, u32[]{:S(2)}, u32[]{:S(2)}) %collective-permute-start.23) | collective-permute-done | bytes 131104 | tf_op jit(solution)/shard_map/ppermute | solution.py:34
  169.9 0.9 pad_maximum_fusion.4.refs_0_
  171.1 7.4 %collective-permute-done.24.refs_4_ = bf16[2,256,256]{2,1,0:T(8,128)(2,1)S(1)} collective-permute-done((bf16[2,256,256]{2,1,0:T(8,128)(2,1)S(1)}, bf16[2,256,256]{2,1,0:T(8,128)(2,1)S(1)}, u32[]{:S(2)}, u32[]{:S(2)}) %collective-permute-start.24) | collective-permute-done | bytes 262176 | tf_op jit(solution)/shard_map/ppermute | solution.py:34
  178.5 1.4 collective-permute-start.30
  179.9 1.5 collective-permute-start.31
  181.4 3.5 %collective-permute-done.25.refs_8_ = bf16[2,256,256]{2,1,0:T(8,128)(2,1)S(1)} collective-permute-done((bf16[2,256,256]{2,1,0:T(8,128)(2,1)S(1)}, bf16[2,256,256]{2,1,0:T(8,128)(2,1)S(1)}, u32[]{:S(2)}, u32[]{:S(2)}) %collective-permute-start.25) | collective-permute-done | bytes 262176 | tf_op jit(solution)/shard_map/ppermute | solution.py:34
  185.1 2.4 %collective-permute-done.30.refs_1_ = bf16[2,256,256]{2,1,0:T(8,128)(2,1)S(1)} collective-permute-done((bf16[2,256,256]{2,1,0:T(8,128)(2,1)S(1)}, bf16[2,256,256]{2,1,0:T(8,128)(2,1)S(1)}, u32[]{:S(2)}, u32[]{:S(2)}) %collective-permute-start.30) | collective-permute-done | bytes 262176 | tf_op jit(solution)/shard_map/ppermute | solution.py:34
  187.6 2.3 %collective-permute-start.33 = (bf16[2,256,256]{2,1,0:T(8,128)(2,1)S(1)}, bf16[2,256,256]{2,1,0:T(8,128)(2,1)S(1)}, u32[]{:S(2)}, u32[]{:S(2)}) collective-permute-start(bf16[2,256,256]{2,1,0:T(8,128)(2,1)S(1)} %collective-permute-done.24.refs_4_), channel_id=1, source_target_pairs={{0,64},{1,193},{64,0},{65,129},{128,192},{129,65},{192,128},{193,1... | collective-permute-start | bytes 786440 | tf_op jit(solution)/shard_map/ppermute | solution.py:34
  190.0 1.8 collective-permute-start.34
  191.7 0.8 collective-permute-done.26.refs_0_
  192.5 1.8 collective-permute-start.27
  194.3 2.4 %collective-permute-done.32.refs_3_ = bf16[2,256,256]{2,1,0:T(8,128)(2,1)S(1)} collective-permute-done((bf16[2,256,256]{2,1,0:T(8,128)(2,1)S(1)}, bf16[2,256,256]{2,1,0:T(8,128)(2,1)S(1)}, u32[]{:S(2)}, u32[]{:S(2)}) %collective-permute-start.32) | collective-permute-done | bytes 262176 | tf_op jit(solution)/shard_map/ppermute | solution.py:34
  197.1 1.7 collective-permute-start.35
  198.9 3.9 %collective-permute-done.36.refs_9_ = bf16[2,256,256]{2,1,0:T(8,128)(2,1)S(1)} collective-permute-done((bf16[2,256,256]{2,1,0:T(8,128)(2,1)S(1)}, bf16[2,256,256]{2,1,0:T(8,128)(2,1)S(1)}, u32[]{:S(2)}, u32[]{:S(2)}) %collective-permute-start.36) | collective-permute-done | bytes 262176 | tf_op jit(solution)/shard_map/ppermute | solution.py:34
  202.8 1.7 collective-permute-start.38
  204.8 3.6 %collective-permute-done.27.refs_1_ = bf16[2,256,256]{2,1,0:T(8,128)(2,1)S(1)} collective-permute-done((bf16[2,256,256]{2,1,0:T(8,128)(2,1)S(1)}, bf16[2,256,256]{2,1,0:T(8,128)(2,1)S(1)}, u32[]{:S(2)}, u32[]{:S(2)}) %collective-permute-start.27) | collective-permute-done | bytes 262176 | tf_op jit(solution)/shard_map/ppermute | solution.py:34
  208.4 1.7 collective-permute-start.29
  210.2 0.6 copy-done.17
  210.9 0.7 copy-done.18
  211.6 3.9 %shard_map.95.refs_4_ = bf16[32,256,256]{2,1,0:T(8,128)(2,1)} custom-call(s32[7]{0:T(128)} %stack.67.place, bf16[2,256,256]{2,1,0:T(8,128)(2,1)} %copy-done.1, bf16[2,256,256]{2,1,0:T(8,128)(2,1)} %copy-done.10, bf16[2,256,256]{2,1,0:T(8,128)(2,1)} %copy-done.11, bf16[2,256,256]{2,1,0:T(8,128)(2,1)} %copy-done.12, bf16[2,256,256]{2,1,0:T(8,128)(2,1)} %copy-done.8, ...), custom_call_target="tpu_custom_call" | custom-call | bytes 3145728 | tf_op jit(solution)/shard_map/pallas_call | solution.py:291
  215.7 0.5 copy-done.5
  216.2 0.7 copy-done.6
  216.9 2.8 %shard_map.96 = bf16[32,256,256]{2,1,0:T(8,128)(2,1)} custom-call(s32[7]{0:T(128)} %stack.67.place, bf16[2,256,256]{2,1,0:T(8,128)(2,1)} %copy-done.3, bf16[2,256,256]{2,1,0:T(8,128)(2,1)} %copy-done.4, bf16[2,256,256]{2,1,0:T(8,128)(2,1)} %copy-done.5, bf16[2,256,256]{2,1,0:T(8,128)(2,1)} %copy-done.6, ...), custom_call_target="tpu_custom_call", output_to_operand_aliasing={{}: (5, {})} | custom-call | bytes 1048576 | tf_op jit(solution)/shard_map/pallas_call | solution.py:291
  (100 shorter events, 3.6 us)
Async XLA Ops:
  0.6 14.0 %copy-start.28 = (u32[256]{0:T(256)S(1)}, u32[256]{0:T(256)}, u32[]{:S(2)}) copy-start(u32[256]{0:T(256)} %constant.46) | copy-start | bytes 3076
  0.6 15.3 %copy-start.27 = (s32[64]{0:T(128)S(1)}, s32[64]{0:T(128)}, u32[]{:S(2)}) copy-start(s32[64]{0:T(128)} %param.7) | copy-start | bytes 772
  0.7 25.6 %copy-start.7 = (bf16[512,256]{1,0:T(8,128)(2,1)S(1)}, bf16[512,256]{1,0:T(8,128)(2,1)}, u32[]{:S(2)}) copy-start(bf16[512,256]{1,0:T(8,128)(2,1)} %param.8) | copy-start | bytes 786436
  3.0 40.6 %all-to-all-start = ((bf16[64,32,256]{2,0,1:T(8,128)(2,1)}), bf16[64,32,256]{2,0,1:T(8,128)(2,1)S(1)}, u32[]{:S(2)}, u32[]{:S(2)}) async-start(bf16[64,32,256]{2,0,1:T(8,128)(2,1)} %bitcast.51), calls=%async_computation | async-start | bytes 2097152 | tf_op jit(solution)/shard_map/all_to_all | solution.py:323
  26.4 5.0 %collective-permute-start.17 = (bf16[160,256]{1,0:T(8,128)(2,1)S(1)}, bf16[160,256]{1,0:T(8,128)(2,1)S(1)}, u32[]{:S(2)}, u32[]{:S(2)}) collective-permute-start(bf16[160,256]{1,0:T(8,128)(2,1)S(1)} %get-tuple-element.21), channel_id=1, source_target_pairs={{0,64},{1,193},{64,0},{65,129},{128,192},{129,65},{192,128},{193,1... | collective-permute-start | bytes 245768 | tf_op jit(solution)/shard_map/ppermute | solution.py:34
  31.4 6.7 %collective-permute-start.18 = (bf16[2,160,256]{2,1,0:T(8,128)(2,1)S(1)}, bf16[2,160,256]{2,1,0:T(8,128)(2,1)S(1)}, u32[]{:S(2)}, u32[]{:S(2)}) collective-permute-start(bf16[2,160,256]{2,1,0:T(8,128)(2,1)S(1)} %pad_maximum_fusion.5), channel_id=1, source_target_pairs={{0,192},{1,65},{64,128},{65,1},{128,64},{129,193},{192,0},{193,129... | collective-permute-start | bytes 491528 | tf_op jit(solution)/shard_map/ppermute | solution.py:34
  32.9 7.9 %collective-permute-start.7 = (bf16[352,256]{1,0:T(8,128)(2,1)S(1)}, bf16[352,256]{1,0:T(8,128)(2,1)S(1)}, u32[]{:S(2)}, u32[]{:S(2)}) collective-permute-start(bf16[352,256]{1,0:T(8,128)(2,1)S(1)} %get-tuple-element.23), channel_id=1, source_target_pairs={{0,8},{1,57},{8,0},{9,17},{16,24},{17,9},{24,16},{25,33},{32,40},{... | collective-permute-start | bytes 540680 | tf_op jit(solution)/shard_map/ppermute | solution.py:34
  38.2 8.5 %collective-permute-start.19 = (bf16[4,160,256]{2,1,0:T(8,128)(2,1)S(1)}, bf16[4,160,256]{2,1,0:T(8,128)(2,1)S(1)}, u32[]{:S(2)}, u32[]{:S(2)}) collective-permute-start(bf16[4,160,256]{2,1,0:T(8,128)(2,1)S(1)} %get-tuple-element.19), channel_id=1, source_target_pairs={{0,8},{1,57},{8,0},{9,17},{16,24},{17,9},{24,16},{25,33},{32,40},{... | collective-permute-start | bytes 983048 | tf_op jit(solution)/shard_map/ppermute | solution.py:34
  40.8 10.8 %collective-permute-start.8 = (bf16[2,352,256]{2,1,0:T(8,128)(2,1)S(1)}, bf16[2,352,256]{2,1,0:T(8,128)(2,1)S(1)}, u32[]{:S(2)}, u32[]{:S(2)}) collective-permute-start(bf16[2,352,256]{2,1,0:T(8,128)(2,1)S(1)} %pad_maximum_fusion.2), channel_id=1, source_target_pairs={{0,56},{1,9},{8,16},{9,1},{16,8},{17,25},{24,32},{25,17},{32,24},{... | collective-permute-start | bytes 1081352 | tf_op jit(solution)/shard_map/ppermute | solution.py:34
  43.6 71.4 %copy-start = (bf16[64,32,256]{2,0,1:T(8,128)(2,1)}, bf16[64,32,256]{2,0,1:T(8,128)(2,1)S(1)}, u32[]{:S(2)}) copy-start(bf16[64,32,256]{2,0,1:T(8,128)(2,1)S(1)} %all-to-all-done) | copy-start | bytes 3145732
  43.6 31.9 %collective-permute-start = (bf16[32,64,256]{2,1,0:T(8,128)(2,1)S(1)}, bf16[32,64,256]{2,1,0:T(8,128)(2,1)}, u32[]{:S(2)}, u32[]{:S(2)}) collective-permute-start(bf16[32,64,256]{2,1,0:T(8,128)(2,1)S(1)} %bitcast.54), channel_id=1, source_target_pairs={{0,2},{1,7},{2,0},{3,5},{4,6},{5,3},{6,4},{7,1},{8,10},{9,15},{10,... | collective-permute-start | bytes 3145736 | tf_op jit(solution)/shard_map/ppermute | solution.py:34
  46.8 68.2 %copy-start.2 = (bf16[2,4,160,256]{3,2,1,0:T(8,128)(2,1)}, bf16[2,4,160,256]{3,2,1,0:T(8,128)(2,1)S(1)}, u32[]{:S(2)}) copy-start(bf16[2,4,160,256]{3,2,1,0:T(8,128)(2,1)S(1)} %pad_maximum_fusion.1.refs_16_) | copy-start | bytes 1966084
  46.8 17.2 %collective-permute-start.20 = (bf16[2,4,160,256]{3,2,1,0:T(8,128)(2,1)S(1)}, bf16[2,4,160,256]{3,2,1,0:T(8,128)(2,1)S(1)}, u32[]{:S(2)}, u32[]{:S(2)}) collective-permute-start(bf16[2,4,160,256]{3,2,1,0:T(8,128)(2,1)S(1)} %pad_maximum_fusion.1.refs_16_), channel_id=1, source_target_pairs={{0,56},{1,9},{8,16},{9,1},{16,8},{17,25},{24,32},{25,17},{32,24},{... | collective-permute-start | bytes 1966088 | tf_op jit(solution)/shard_map/ppermute | solution.py:34
  51.6 8.6 %collective-permute-start.12 = (bf16[2,352,256]{2,1,0:T(8,128)(2,1)S(1)}, bf16[2,352,256]{2,1,0:T(8,128)(2,1)S(1)}, u32[]{:S(2)}, u32[]{:S(2)}) collective-permute-start(bf16[2,352,256]{2,1,0:T(8,128)(2,1)S(1)} %collective-permute-done.8), channel_id=1, source_target_pairs={{0,8},{1,57},{8,0},{9,17},{16,24},{17,9},{24,16},{25,33},{32,40},{... | collective-permute-start | bytes 1081352 | tf_op jit(solution)/shard_map/ppermute | solution.py:34
  52.5 21.2 %collective-permute-start.9 = (bf16[4,352,256]{2,1,0:T(8,128)(2,1)S(1)}, bf16[4,352,256]{2,1,0:T(8,128)(2,1)S(1)}, u32[]{:S(2)}, u32[]{:S(2)}) collective-permute-start(bf16[4,352,256]{2,1,0:T(8,128)(2,1)S(1)} %get-tuple-element.16), channel_id=1, source_target_pairs={{0,64},{1,193},{64,0},{65,129},{128,192},{129,65},{192,128},{193,1... | collective-permute-start | bytes 2162696 | tf_op jit(solution)/shard_map/ppermute | solution.py:34
  60.1 10.5 %collective-permute-start.13 = (bf16[2,352,256]{2,1,0:T(8,128)(2,1)S(1)}, bf16[2,352,256]{2,1,0:T(8,128)(2,1)S(1)}, u32[]{:S(2)}, u32[]{:S(2)}) collective-permute-start(bf16[2,352,256]{2,1,0:T(8,128)(2,1)S(1)} %collective-permute-done.12), channel_id=1, source_target_pairs={{0,56},{1,9},{8,16},{9,1},{16,8},{17,25},{24,32},{25,17},{32,24},{... | collective-permute-start | bytes 1081352 | tf_op jit(solution)/shard_map/ppermute | solution.py:34
  63.3 13.8 %collective-permute-start.10 = (bf16[4,352,256]{2,1,0:T(8,128)(2,1)S(1)}, bf16[4,352,256]{2,1,0:T(8,128)(2,1)S(1)}, u32[]{:S(2)}, u32[]{:S(2)}) collective-permute-start(bf16[4,352,256]{2,1,0:T(8,128)(2,1)S(1)} %get-tuple-element.16), channel_id=1, source_target_pairs={{0,192},{1,65},{64,128},{65,1},{128,64},{129,193},{192,0},{193,129... | collective-permute-start | bytes 2162696 | tf_op jit(solution)/shard_map/ppermute | solution.py:34
  64.0 38.5 %copy-start.24 = (bf16[2,4,160,256]{3,2,1,0:T(8,128)(2,1)}, bf16[2,4,160,256]{3,2,1,0:T(8,128)(2,1)S(1)}, u32[]{:S(2)}) copy-start(bf16[2,4,160,256]{3,2,1,0:T(8,128)(2,1)S(1)} %collective-permute-done.20.refs_17_) | copy-start | bytes 1966084
  64.0 15.0 %collective-permute-start.21 = (bf16[2,4,160,256]{3,2,1,0:T(8,128)(2,1)S(1)}, bf16[2,4,160,256]{3,2,1,0:T(8,128)(2,1)S(1)}, u32[]{:S(2)}, u32[]{:S(2)}) collective-permute-start(bf16[2,4,160,256]{3,2,1,0:T(8,128)(2,1)S(1)} %collective-permute-done.20.refs_17_), channel_id=1, source_target_pairs={{0,8},{1,57},{8,0},{9,17},{16,24},{17,9},{24,16},{25,33},{32,40},{... | collective-permute-start | bytes 1966088 | tf_op jit(solution)/shard_map/ppermute | solution.py:34
  70.6 44.4 %copy-start.19 = (bf16[4,352,256]{2,1,0:T(8,128)(2,1)}, bf16[4,352,256]{2,1,0:T(8,128)(2,1)S(1)}, u32[]{:S(2)}) copy-start(bf16[4,352,256]{2,1,0:T(8,128)(2,1)S(1)} %constant_dynamic-update-slice_fusion) | copy-start | bytes 2162692
  70.6 20.0 %collective-permute-start.15 = (bf16[4,352,256]{2,1,0:T(8,128)(2,1)S(1)}, bf16[4,352,256]{2,1,0:T(8,128)(2,1)S(1)}, u32[]{:S(2)}, u32[]{:S(2)}) collective-permute-start(bf16[4,352,256]{2,1,0:T(8,128)(2,1)S(1)} %constant_dynamic-update-slice_fusion), channel_id=1, source_target_pairs={{0,192},{1,65},{64,128},{65,1},{128,64},{129,193},{192,0},{193,129... | collective-permute-start | bytes 2162696 | tf_op jit(solution)/shard_map/ppermute | solution.py:34
  73.8 24.6 %copy-start.20 = (bf16[4,352,256]{2,1,0:T(8,128)(2,1)}, bf16[4,352,256]{2,1,0:T(8,128)(2,1)S(1)}, u32[]{:S(2)}) copy-start(bf16[4,352,256]{2,1,0:T(8,128)(2,1)S(1)} %collective-permute-done.9) | copy-start | bytes 2162692
  73.8 24.6 %collective-permute-start.1 = (bf16[32,64,256]{2,1,0:T(8,128)(2,1)S(1)}, bf16[32,64,256]{2,1,0:T(8,128)(2,1)}, u32[]{:S(2)}, u32[]{:S(2)}) collective-permute-start(bf16[32,64,256]{2,1,0:T(8,128)(2,1)S(1)} %bitcast.55), channel_id=1, source_target_pairs={{0,6},{1,3},{2,4},{3,1},{4,2},{5,7},{6,0},{7,5},{8,14},{9,11},{10,... | collective-permute-start | bytes 3145736 | tf_op jit(solution)/shard_map/ppermute | solution.py:34
  75.5 25.6 %collective-permute-start.2 = (bf16[32,64,256]{2,1,0:T(8,128)(2,1)}, bf16[32,64,256]{2,1,0:T(8,128)(2,1)}, u32[]{:S(2)}, u32[]{:S(2)}) collective-permute-start(bf16[32,64,256]{2,1,0:T(8,128)(2,1)} %collective-permute-done.refs_1_), channel_id=1, source_target_pairs={{0,6},{1,3},{2,4},{3,1},{4,2},{5,7},{6,0},{7,5},{8,14},{9,11},{10,... | collective-permute-start | bytes 3145736 | tf_op jit(solution)/shard_map/ppermute | solution.py:34
  77.0 21.9 %copy-start.21 = (bf16[4,352,256]{2,1,0:T(8,128)(2,1)}, bf16[4,352,256]{2,1,0:T(8,128)(2,1)S(1)}, u32[]{:S(2)}) copy-start(bf16[4,352,256]{2,1,0:T(8,128)(2,1)S(1)} %collective-permute-done.10) | copy-start | bytes 2162692
  77.0 18.7 %collective-permute-start.14 = (bf16[4,352,256]{2,1,0:T(8,128)(2,1)S(1)}, bf16[4,352,256]{2,1,0:T(8,128)(2,1)}, u32[]{:S(2)}, u32[]{:S(2)}) collective-permute-start(bf16[4,352,256]{2,1,0:T(8,128)(2,1)S(1)} %constant_dynamic-update-slice_fusion), channel_id=1, source_target_pairs={{0,64},{1,193},{64,0},{65,129},{128,192},{129,65},{192,128},{193,1... | collective-permute-start | bytes 2162696 | tf_op jit(solution)/shard_map/ppermute | solution.py:34
  78.9 23.5 %copy-start.25 = (bf16[2,4,160,256]{3,2,1,0:T(8,128)(2,1)}, bf16[2,4,160,256]{3,2,1,0:T(8,128)(2,1)S(1)}, u32[]{:S(2)}) copy-start(bf16[2,4,160,256]{3,2,1,0:T(8,128)(2,1)S(1)} %collective-permute-done.21.refs_18_) | copy-start | bytes 1966084
  78.9 19.4 %collective-permute-start.11 = (bf16[4,352,256]{2,1,0:T(8,128)(2,1)S(1)}, bf16[4,352,256]{2,1,0:T(8,128)(2,1)S(1)}, u32[]{:S(2)}, u32[]{:S(2)}) collective-permute-start(bf16[4,352,256]{2,1,0:T(8,128)(2,1)S(1)} %collective-permute-done.9), channel_id=1, source_target_pairs={{0,192},{1,65},{64,128},{65,1},{128,64},{129,193},{192,0},{193,129... | collective-permute-start | bytes 2162696 | tf_op jit(solution)/shard_map/ppermute | solution.py:34
  90.6 10.5 %copy-start.22 = (bf16[4,352,256]{2,1,0:T(8,128)(2,1)}, bf16[4,352,256]{2,1,0:T(8,128)(2,1)S(1)}, u32[]{:S(2)}) copy-start(bf16[4,352,256]{2,1,0:T(8,128)(2,1)S(1)} %collective-permute-done.15) | copy-start | bytes 2162692
  90.7 11.8 %collective-permute-start.22 = (bf16[2,4,160,256]{3,2,1,0:T(8,128)(2,1)S(1)}, bf16[2,4,160,256]{3,2,1,0:T(8,128)(2,1)S(1)}, u32[]{:S(2)}, u32[]{:S(2)}) collective-permute-start(bf16[2,4,160,256]{3,2,1,0:T(8,128)(2,1)S(1)} %collective-permute-done.21.refs_18_), channel_id=1, source_target_pairs={{0,56},{1,9},{8,16},{9,1},{16,8},{17,25},{24,32},{25,17},{32,24},{... | collective-permute-start | bytes 1966088 | tf_op jit(solution)/shard_map/ppermute | solution.py:34
  95.8 19.2 %collective-permute-start.3 = (bf16[32,64,256]{2,1,0:T(8,128)(2,1)S(1)}, bf16[32,64,256]{2,1,0:T(8,128)(2,1)}, u32[]{:S(2)}, u32[]{:S(2)}) collective-permute-start(bf16[32,64,256]{2,1,0:T(8,128)(2,1)S(1)} %bitcast.56), channel_id=1, source_target_pairs={{0,1},{1,0},{2,3},{3,2},{4,5},{5,4},{6,7},{7,6},{8,9},{9,8},{10,11... | collective-permute-start | bytes 3145736 | tf_op jit(solution)/shard_map/ppermute | solution.py:25
  98.4 2.8 %copy-start.23 = (bf16[4,352,256]{2,1,0:T(8,128)(2,1)}, bf16[4,352,256]{2,1,0:T(8,128)(2,1)S(1)}, u32[]{:S(2)}) copy-start(bf16[4,352,256]{2,1,0:T(8,128)(2,1)S(1)} %collective-permute-done.11) | copy-start | bytes 2162692
  98.4 16.6 %collective-permute-start.4 = (bf16[32,64,256]{2,1,0:T(8,128)(2,1)}, bf16[32,64,256]{2,1,0:T(8,128)(2,1)}, u32[]{:S(2)}, u32[]{:S(2)}) collective-permute-start(bf16[32,64,256]{2,1,0:T(8,128)(2,1)} %collective-permute-done.refs_1_), channel_id=1, source_target_pairs={{0,1},{1,0},{2,3},{3,2},{4,5},{5,4},{6,7},{7,6},{8,9},{9,8},{10,11... | collective-permute-start | bytes 3145736 | tf_op jit(solution)/shard_map/ppermute | solution.py:25
  98.4 16.6 %collective-permute-start.5 = (bf16[32,64,256]{2,1,0:T(8,128)(2,1)}, bf16[32,64,256]{2,1,0:T(8,128)(2,1)}, u32[]{:S(2)}, u32[]{:S(2)}) collective-permute-start(bf16[32,64,256]{2,1,0:T(8,128)(2,1)} %collective-permute-done.1.refs_2_), channel_id=1, source_target_pairs={{0,1},{1,0},{2,3},{3,2},{4,5},{5,4},{6,7},{7,6},{8,9},{9,8},{10,11... | collective-permute-start | bytes 3145736 | tf_op jit(solution)/shard_map/ppermute | solution.py:25
  101.1 13.8 %collective-permute-start.6 = (bf16[32,64,256]{2,1,0:T(8,128)(2,1)}, bf16[32,64,256]{2,1,0:T(8,128)(2,1)}, u32[]{:S(2)}, u32[]{:S(2)}) collective-permute-start(bf16[32,64,256]{2,1,0:T(8,128)(2,1)} %collective-permute-done.2.refs_3_), channel_id=1, source_target_pairs={{0,1},{1,0},{2,3},{3,2},{4,5},{5,4},{6,7},{7,6},{8,9},{9,8},{10,11... | collective-permute-start | bytes 3145736 | tf_op jit(solution)/shard_map/ppermute | solution.py:25
  102.5 0.9 copy-start.26
  103.3 11.6 %collective-permute-start.16 = (bf16[4,352,256]{2,1,0:T(8,128)(2,1)}, bf16[4,352,256]{2,1,0:T(8,128)(2,1)}, u32[]{:S(2)}, u32[]{:S(2)}) collective-permute-start(bf16[4,352,256]{2,1,0:T(8,128)(2,1)} %collective-permute-done.14), channel_id=1, source_target_pairs={{0,192},{1,65},{64,128},{65,1},{128,64},{129,193},{192,0},{193,129... | collective-permute-start | bytes 2162696 | tf_op jit(solution)/shard_map/ppermute | solution.py:34
  164.7 5.3 %collective-permute-start.23 = (bf16[256,256]{1,0:T(8,128)(2,1)}, bf16[256,256]{1,0:T(8,128)(2,1)S(1)}, u32[]{:S(2)}, u32[]{:S(2)}) collective-permute-start(bf16[256,256]{1,0:T(8,128)(2,1)} %get-tuple-element.12), channel_id=1, source_target_pairs={{0,8},{1,57},{8,0},{9,17},{16,24},{17,9},{24,16},{25,33},{32,40},{... | collective-permute-start | bytes 393224 | tf_op jit(solution)/shard_map/ppermute | solution.py:34
  170.9 39.3 %copy-start.1 = (bf16[2,256,256]{2,1,0:T(8,128)(2,1)}, bf16[2,256,256]{2,1,0:T(8,128)(2,1)S(1)}, u32[]{:S(2)}) copy-start(bf16[2,256,256]{2,1,0:T(8,128)(2,1)S(1)} %pad_maximum_fusion.4.refs_0_) | copy-start | bytes 786436
  170.9 7.7 %collective-permute-start.24 = (bf16[2,256,256]{2,1,0:T(8,128)(2,1)S(1)}, bf16[2,256,256]{2,1,0:T(8,128)(2,1)S(1)}, u32[]{:S(2)}, u32[]{:S(2)}) collective-permute-start(bf16[2,256,256]{2,1,0:T(8,128)(2,1)S(1)} %pad_maximum_fusion.4.refs_0_), channel_id=1, source_target_pairs={{0,56},{1,9},{8,16},{9,1},{16,8},{17,25},{24,32},{25,17},{32,24},{... | collective-permute-start | bytes 786440 | tf_op jit(solution)/shard_map/ppermute | solution.py:34
  178.5 31.6 %copy-start.8 = (bf16[2,256,256]{2,1,0:T(8,128)(2,1)}, bf16[2,256,256]{2,1,0:T(8,128)(2,1)S(1)}, u32[]{:S(2)}) copy-start(bf16[2,256,256]{2,1,0:T(8,128)(2,1)S(1)} %collective-permute-done.24.refs_4_) | copy-start | bytes 786436
  178.5 6.4 %collective-permute-start.25 = (bf16[2,256,256]{2,1,0:T(8,128)(2,1)S(1)}, bf16[2,256,256]{2,1,0:T(8,128)(2,1)S(1)}, u32[]{:S(2)}, u32[]{:S(2)}) collective-permute-start(bf16[2,256,256]{2,1,0:T(8,128)(2,1)S(1)} %collective-permute-done.24.refs_4_), channel_id=1, source_target_pairs={{0,8},{1,57},{8,0},{9,17},{16,24},{17,9},{24,16},{25,33},{32,40},{... | collective-permute-start | bytes 786440 | tf_op jit(solution)/shard_map/ppermute | solution.py:34
  178.5 8.9 %collective-permute-start.30 = (bf16[2,256,256]{2,1,0:T(8,128)(2,1)S(1)}, bf16[2,256,256]{2,1,0:T(8,128)(2,1)S(1)}, u32[]{:S(2)}, u32[]{:S(2)}) collective-permute-start(bf16[2,256,256]{2,1,0:T(8,128)(2,1)S(1)} %pad_maximum_fusion.4.refs_0_), channel_id=1, source_target_pairs={{0,64},{1,193},{64,0},{65,129},{128,192},{129,65},{192,128},{193,1... | collective-permute-start | bytes 786440 | tf_op jit(solution)/shard_map/ppermute | solution.py:34
  179.9 10.0 %collective-permute-start.31 = (bf16[2,256,256]{2,1,0:T(8,128)(2,1)S(1)}, bf16[2,256,256]{2,1,0:T(8,128)(2,1)S(1)}, u32[]{:S(2)}, u32[]{:S(2)}) collective-permute-start(bf16[2,256,256]{2,1,0:T(8,128)(2,1)S(1)} %pad_maximum_fusion.4.refs_0_), channel_id=1, source_target_pairs={{0,192},{1,65},{64,128},{65,1},{128,64},{129,193},{192,0},{193,129... | collective-permute-start | bytes 786440 | tf_op jit(solution)/shard_map/ppermute | solution.py:34
  184.9 25.2 %copy-start.9 = (bf16[2,256,256]{2,1,0:T(8,128)(2,1)}, bf16[2,256,256]{2,1,0:T(8,128)(2,1)S(1)}, u32[]{:S(2)}) copy-start(bf16[2,256,256]{2,1,0:T(8,128)(2,1)S(1)} %collective-permute-done.25.refs_8_) | copy-start | bytes 786436
  184.9 7.6 %collective-permute-start.26 = (bf16[2,256,256]{2,1,0:T(8,128)(2,1)S(1)}, bf16[2,256,256]{2,1,0:T(8,128)(2,1)S(1)}, u32[]{:S(2)}, u32[]{:S(2)}) collective-permute-start(bf16[2,256,256]{2,1,0:T(8,128)(2,1)S(1)} %collective-permute-done.25.refs_8_), channel_id=1, source_target_pairs={{0,56},{1,9},{8,16},{9,1},{16,8},{17,25},{24,32},{25,17},{32,24},{... | collective-permute-start | bytes 786440 | tf_op jit(solution)/shard_map/ppermute | solution.py:34
  187.4 22.7 %copy-start.10 = (bf16[2,256,256]{2,1,0:T(8,128)(2,1)}, bf16[2,256,256]{2,1,0:T(8,128)(2,1)S(1)}, u32[]{:S(2)}) copy-start(bf16[2,256,256]{2,1,0:T(8,128)(2,1)S(1)} %collective-permute-done.30.refs_1_) | copy-start | bytes 786436
  187.4 9.2 %collective-permute-start.32 = (bf16[2,256,256]{2,1,0:T(8,128)(2,1)S(1)}, bf16[2,256,256]{2,1,0:T(8,128)(2,1)S(1)}, u32[]{:S(2)}, u32[]{:S(2)}) collective-permute-start(bf16[2,256,256]{2,1,0:T(8,128)(2,1)S(1)} %collective-permute-done.30.refs_1_), channel_id=1, source_target_pairs={{0,192},{1,65},{64,128},{65,1},{128,64},{129,193},{192,0},{193,129... | collective-permute-start | bytes 786440 | tf_op jit(solution)/shard_map/ppermute | solution.py:34
  187.6 9.6 %collective-permute-start.33 = (bf16[2,256,256]{2,1,0:T(8,128)(2,1)S(1)}, bf16[2,256,256]{2,1,0:T(8,128)(2,1)S(1)}, u32[]{:S(2)}, u32[]{:S(2)}) collective-permute-start(bf16[2,256,256]{2,1,0:T(8,128)(2,1)S(1)} %collective-permute-done.24.refs_4_), channel_id=1, source_target_pairs={{0,64},{1,193},{64,0},{65,129},{128,192},{129,65},{192,128},{193,1... | collective-permute-start | bytes 786440 | tf_op jit(solution)/shard_map/ppermute | solution.py:34
  189.9 12.8 %collective-permute-start.36 = (bf16[2,256,256]{2,1,0:T(8,128)(2,1)S(1)}, bf16[2,256,256]{2,1,0:T(8,128)(2,1)S(1)}, u32[]{:S(2)}, u32[]{:S(2)}) collective-permute-start(bf16[2,256,256]{2,1,0:T(8,128)(2,1)S(1)} %collective-permute-done.25.refs_8_), channel_id=1, source_target_pairs={{0,64},{1,193},{64,0},{65,129},{128,192},{129,65},{192,128},{193,1... | collective-permute-start | bytes 786440 | tf_op jit(solution)/shard_map/ppermute | solution.py:34
  190.0 20.2 %copy-start.11 = (bf16[2,256,256]{2,1,0:T(8,128)(2,1)}, bf16[2,256,256]{2,1,0:T(8,128)(2,1)S(1)}, u32[]{:S(2)}) copy-start(bf16[2,256,256]{2,1,0:T(8,128)(2,1)S(1)} %collective-permute-done.31.refs_2_) | copy-start | bytes 786436
  190.0 14.5 %collective-permute-start.34 = (bf16[2,256,256]{2,1,0:T(8,128)(2,1)S(1)}, bf16[2,256,256]{2,1,0:T(8,128)(2,1)S(1)}, u32[]{:S(2)}, u32[]{:S(2)}) collective-permute-start(bf16[2,256,256]{2,1,0:T(8,128)(2,1)S(1)} %collective-permute-done.24.refs_4_), channel_id=1, source_target_pairs={{0,192},{1,65},{64,128},{65,1},{128,64},{129,193},{192,0},{193,129... | collective-permute-start | bytes 786440 | tf_op jit(solution)/shard_map/ppermute | solution.py:34
  192.5 23.2 %copy-start.3 = (bf16[2,256,256]{2,1,0:T(8,128)(2,1)}, bf16[2,256,256]{2,1,0:T(8,128)(2,1)S(1)}, u32[]{:S(2)}) copy-start(bf16[2,256,256]{2,1,0:T(8,128)(2,1)S(1)} %collective-permute-done.26.refs_0_) | copy-start | bytes 786436
  192.5 15.9 %collective-permute-start.27 = (bf16[2,256,256]{2,1,0:T(8,128)(2,1)S(1)}, bf16[2,256,256]{2,1,0:T(8,128)(2,1)S(1)}, u32[]{:S(2)}, u32[]{:S(2)}) collective-permute-start(bf16[2,256,256]{2,1,0:T(8,128)(2,1)S(1)} %collective-permute-done.26.refs_0_), channel_id=1, source_target_pairs={{0,64},{1,193},{64,0},{65,129},{128,192},{129,65},{192,128},{193,1... | collective-permute-start | bytes 786440 | tf_op jit(solution)/shard_map/ppermute | solution.py:34
  196.7 13.5 %copy-start.12 = (bf16[2,256,256]{2,1,0:T(8,128)(2,1)}, bf16[2,256,256]{2,1,0:T(8,128)(2,1)S(1)}, u32[]{:S(2)}) copy-start(bf16[2,256,256]{2,1,0:T(8,128)(2,1)S(1)} %collective-permute-done.32.refs_3_) | copy-start | bytes 786436
  196.7 13.4 %collective-permute-start.37 = (bf16[2,256,256]{2,1,0:T(8,128)(2,1)S(1)}, bf16[2,256,256]{2,1,0:T(8,128)(2,1)S(1)}, u32[]{:S(2)}, u32[]{:S(2)}) collective-permute-start(bf16[2,256,256]{2,1,0:T(8,128)(2,1)S(1)} %collective-permute-done.25.refs_8_), channel_id=1, source_target_pairs={{0,192},{1,65},{64,128},{65,1},{128,64},{129,193},{192,0},{193,129... | collective-permute-start | bytes 786440 | tf_op jit(solution)/shard_map/ppermute | solution.py:34
  197.1 13.1 %copy-start.13 = (bf16[2,256,256]{2,1,0:T(8,128)(2,1)}, bf16[2,256,256]{2,1,0:T(8,128)(2,1)S(1)}, u32[]{:S(2)}) copy-start(bf16[2,256,256]{2,1,0:T(8,128)(2,1)S(1)} %collective-permute-done.33.refs_5_) | copy-start | bytes 786436
  197.1 13.0 %collective-permute-start.35 = (bf16[2,256,256]{2,1,0:T(8,128)(2,1)S(1)}, bf16[2,256,256]{2,1,0:T(8,128)(2,1)S(1)}, u32[]{:S(2)}, u32[]{:S(2)}) collective-permute-start(bf16[2,256,256]{2,1,0:T(8,128)(2,1)S(1)} %collective-permute-done.33.refs_5_), channel_id=1, source_target_pairs={{0,192},{1,65},{64,128},{65,1},{128,64},{129,193},{192,0},{193,129... | collective-permute-start | bytes 786440 | tf_op jit(solution)/shard_map/ppermute | solution.py:34
  202.8 7.4 %copy-start.14 = (bf16[2,256,256]{2,1,0:T(8,128)(2,1)}, bf16[2,256,256]{2,1,0:T(8,128)(2,1)S(1)}, u32[]{:S(2)}) copy-start(bf16[2,256,256]{2,1,0:T(8,128)(2,1)S(1)} %collective-permute-done.36.refs_9_) | copy-start | bytes 786436
  202.8 7.4 %collective-permute-start.38 = (bf16[2,256,256]{2,1,0:T(8,128)(2,1)S(1)}, bf16[2,256,256]{2,1,0:T(8,128)(2,1)S(1)}, u32[]{:S(2)}, u32[]{:S(2)}) collective-permute-start(bf16[2,256,256]{2,1,0:T(8,128)(2,1)S(1)} %collective-permute-done.36.refs_9_), channel_id=1, source_target_pairs={{0,192},{1,65},{64,128},{65,1},{128,64},{129,193},{192,0},{193,129... | collective-permute-start | bytes 786440 | tf_op jit(solution)/shard_map/ppermute | solution.py:34
  204.5 5.7 %copy-start.15 = (bf16[2,256,256]{2,1,0:T(8,128)(2,1)}, bf16[2,256,256]{2,1,0:T(8,128)(2,1)S(1)}, u32[]{:S(2)}) copy-start(bf16[2,256,256]{2,1,0:T(8,128)(2,1)S(1)} %collective-permute-done.34.refs_6_) | copy-start | bytes 786436
  204.5 11.1 %collective-permute-start.28 = (bf16[2,256,256]{2,1,0:T(8,128)(2,1)S(1)}, bf16[2,256,256]{2,1,0:T(8,128)(2,1)S(1)}, u32[]{:S(2)}, u32[]{:S(2)}) collective-permute-start(bf16[2,256,256]{2,1,0:T(8,128)(2,1)S(1)} %collective-permute-done.26.refs_0_), channel_id=1, source_target_pairs={{0,192},{1,65},{64,128},{65,1},{128,64},{129,193},{192,0},{193,129... | collective-permute-start | bytes 786440 | tf_op jit(solution)/shard_map/ppermute | solution.py:34
  208.4 7.4 %copy-start.4 = (bf16[2,256,256]{2,1,0:T(8,128)(2,1)}, bf16[2,256,256]{2,1,0:T(8,128)(2,1)S(1)}, u32[]{:S(2)}) copy-start(bf16[2,256,256]{2,1,0:T(8,128)(2,1)S(1)} %collective-permute-done.27.refs_1_) | copy-start | bytes 786436
  208.4 7.4 %collective-permute-start.29 = (bf16[2,256,256]{2,1,0:T(8,128)(2,1)S(1)}, bf16[2,256,256]{2,1,0:T(8,128)(2,1)S(1)}, u32[]{:S(2)}, u32[]{:S(2)}) collective-permute-start(bf16[2,256,256]{2,1,0:T(8,128)(2,1)S(1)} %collective-permute-done.27.refs_1_), channel_id=1, source_target_pairs={{0,192},{1,65},{64,128},{65,1},{128,64},{129,193},{192,0},{193,129... | collective-permute-start | bytes 786440 | tf_op jit(solution)/shard_map/ppermute | solution.py:34
  (5 other events, 3.6 us)
